TPU v7x, 32 devices: a whole 2x2x4 slice. The times are simulated.
32 devices in a mesh: blk: 8 (over z, y), tp: 4 (over x, core).
Axes of the slice: x: 2, y: 2, z: 4, core: 2. Of those that a mesh axis runs over, the one named last changes fastest.
Arguments:
- tokens: bfloat16 [2048, 1536], P('blk'), may hold values from -6 to 6
- lengths: int32 [5], replicated, may hold values from 1 to 1792, as said below
- attention_gain_one: float32 [1536], replicated, may hold values from 0.25 to 1.75
- query_one: bfloat16 [1536, 1536], P(None, 'tp'), may hold values from -0.15625 to 0.15625
- first_key_matrix: bfloat16 [1536, 768], P(None, 'tp'), may hold values from -0.15625 to 0.15625
- first_value_matrix: bfloat16 [1536, 768], P(None, 'tp'), may hold values from -0.15625 to 0.15625
- projection_one: bfloat16 [1536, 1536], P('tp'), may hold values from -1.75 to 1.75
- feedforward_gain_one: float32 [1536], replicated, may hold values from 0.25 to 1.75
- gate_one: bfloat16 [1536, 4096], P(None, 'tp'), may hold values from -0.15625 to 0.15625
- up_one: bfloat16 [1536, 4096], P(None, 'tp'), may hold values from -0.15625 to 0.15625
- down_one: bfloat16 [4096, 1536], P('tp'), may hold values from -0.09375 to 0.09375
- attention_gain_two: float32 [1536], replicated, may hold values from 0.25 to 1.75
- query_two: bfloat16 [1536, 1536], P(None, 'tp'), may hold values from -0.15625 to 0.15625
- second_key_matrix: bfloat16 [1536, 768], P(None, 'tp'), may hold values from -0.15625 to 0.15625
- second_value_matrix: bfloat16 [1536, 768], P(None, 'tp'), may hold values from -0.15625 to 0.15625
- projection_two: bfloat16 [1536, 1536], P('tp'), may hold values from -1.75 to 1.75
- feedforward_gain_two: float32 [1536], replicated, may hold values from 0.25 to 1.75
- gate_two: bfloat16 [1536, 4096], P(None, 'tp'), may hold values from -0.15625 to 0.15625
- up_two: bfloat16 [1536, 4096], P(None, 'tp'), may hold values from -0.15625 to 0.15625
- down_two: bfloat16 [4096, 1536], P('tp'), may hold values from -0.09375 to 0.09375
- cotangent: bfloat16 [2048, 1536], P('blk'), may hold values from -6 to 6
Outputs:
- output: bfloat16 [2048, 1536], P('blk')
- tokens_gradient: float32 [2048, 1536], P('blk')
- gradient_attention_gain_one: float32 [1536], P('blk')
- gradient_query_one: float32 [1536, 1536], P('blk', 'tp')
- gradient_key_one: float32 [1536, 768], P('blk', 'tp')
- gradient_value_one: float32 [1536, 768], P('blk', 'tp')
- gradient_projection_one: float32 [1536, 1536], P('tp', 'blk')
- gradient_feedforward_gain_one: float32 [1536], P('blk')
- gradient_gate_one: float32 [1536, 4096], P('blk', 'tp')
- gradient_up_one: float32 [1536, 4096], P('blk', 'tp')
- gradient_down_one: float32 [4096, 1536], P('tp', 'blk')
- gradient_attention_gain_two: float32 [1536], P('blk')
- gradient_query_two: float32 [1536, 1536], P('blk', 'tp')
- gradient_key_two: float32 [1536, 768], P('blk', 'tp')
- gradient_value_two: float32 [1536, 768], P('blk', 'tp')
- gradient_projection_two: float32 [1536, 1536], P('tp', 'blk')
- gradient_feedforward_gain_two: float32 [1536], P('blk')
- gradient_gate_two: float32 [1536, 4096], P('blk', 'tp')
- gradient_up_two: float32 [1536, 4096], P('blk', 'tp')
- gradient_down_two: float32 [4096, 1536], P('tp', 'blk')
Inputs may be any that keep to these rules, and one draw needn't show every extreme that they name: `lengths`: five documents in pack order; the third has exactly 1792 tokens and begins within the first 256 tokens, so it reaches from the first block of the pack to the last; the other four are shorter than 256.
All inputs are finite; a program needn't handle non-finite values.
Results may differ from a plain program's by a relative error of at most 0.034.
Values may be sent and summed in bfloat16 or wider, within the bound.
No kernel may reach another device: no remote copies, remote signals or barrier semaphores. Data moves between devices by JAX's collectives and lax.ppermute only.
A program may use at most 256 MiB of HBM per device.

v0:
```python
import math

import jax
import jax.numpy as jnp
from jax import lax
from jax.sharding import PartitionSpec as P

HEAD_SIZE = 96


EPSILON = 1e-05
ROTARY_BASE = 100000.0
NEGATIVE = -1e30
KEY_SPAN = 2048


def rms_norm(value_rows, gain):
    return (
        value_rows
        * lax.rsqrt(jnp.mean(value_rows * value_rows, axis=-1, keepdims=True) + EPSILON)
        * gain
    )


def rotate(value_rows, cosine, sine):
    half = value_rows.shape[-1] // 2
    turned = jnp.concatenate([-value_rows[..., half:], value_rows[..., :half]], axis=-1)
    return value_rows * cosine + turned * sine


def unrotate(value_rows, cosine, sine):
    half = value_rows.shape[-1] // 2
    scaled = value_rows * sine
    return value_rows * cosine + jnp.concatenate([scaled[..., half:], -scaled[..., :half]], axis=-1)


def rotary_tables(positions):
    half = HEAD_SIZE // 2
    rates = ROTARY_BASE ** (-(jnp.arange(half).astype(jnp.float32) * 2.0 / HEAD_SIZE))
    angle = positions.astype(jnp.float32)[:, None] * rates[None, :]
    angle = jnp.concatenate([angle, angle], axis=-1)
    return (jnp.cos(angle)[:, None, :], jnp.sin(angle)[:, None, :])


def documents(lengths, index):
    bounds = jnp.cumsum(lengths)
    starts = bounds - lengths
    owner = jnp.sum((index[:, None] >= bounds[None, :]).astype(jnp.int32), axis=1)
    picks = owner[:, None] == jnp.arange(lengths.shape[0], dtype=jnp.int32)[None, :]
    first = jnp.sum(jnp.where(picks, starts[None, :], 0), axis=1)
    return (owner, first)


def product(left, right):
    return jnp.dot(left, right, preferred_element_type=jnp.float32)


def product_left(left, right):
    return lax.dot_general(
        left, right, (((0,), (0,)), ((), ())), preferred_element_type=jnp.float32
    )


def product_right(left, right):
    return lax.dot_general(
        left, right, (((1,), (1,)), ((), ())), preferred_element_type=jnp.float32
    )


def swiglu(gate, up):
    return jax.nn.silu(gate) * up


def block_scores(query_rows, key_rows, key_start, context):
    places, owners, lowest, highest, lengths = context
    span = key_rows.shape[0]
    key_places = key_start + jnp.arange(span, dtype=jnp.int32)
    key_owners, unused = documents(lengths, key_places)
    raw = jnp.einsum("qhgd,khd->hgqk", query_rows, key_rows, preferred_element_type=jnp.float32)
    seen = (owners[:, None] == key_owners[None, :]) & (key_places[None, :] <= places[:, None])
    return (jnp.where(seen, raw * HEAD_SIZE ** (-0.5), NEGATIVE), seen)


def key_layout(gathered):
    total = gathered.shape[0]
    span = math.gcd(total, KEY_SPAN)
    return (span, total // span)


def slice_keys(gathered, number, span, heads):
    width = heads * HEAD_SIZE
    block = lax.dynamic_slice_in_dim(gathered, number * span, span, 0)
    return (
        block[:, :width].reshape(span, heads, HEAD_SIZE),
        block[:, width:].reshape(span, heads, HEAD_SIZE),
    )


def visible(number, span, context):
    key_start = number * span
    return (key_start <= context[3]) & (key_start + span > context[2])


def keep_state(state, number):
    return state


def log_norms(query_rows, gathered, context):
    token_rows, heads, head_group = query_rows.shape[:3]
    span, count = key_layout(gathered)
    start_state = (
        jnp.full((heads, head_group, token_rows), NEGATIVE, jnp.float32),
        jnp.zeros((heads, head_group, token_rows), jnp.float32),
    )

    def visit(state, number):
        top, mass = state
        key_rows, unused = slice_keys(gathered, number, span, heads)
        scores, seen = block_scores(query_rows, key_rows, number * span, context)
        new_top = jnp.maximum(top, jnp.max(scores, axis=-1))
        weights = jnp.where(seen, jnp.exp(scores - new_top[..., None]), 0.0)
        return (new_top, mass * jnp.exp(top - new_top) + jnp.sum(weights, axis=-1))

    def step(state, number):
        return (lax.cond(visible(number, span, context), visit, keep_state, state, number), None)

    final, unused = lax.scan(step, start_state, jnp.arange(count, dtype=jnp.int32))
    return final[0] + jnp.log(final[1])


def attend(query_rows, gathered, log_norm, context):
    token_rows, heads, head_group = query_rows.shape[:3]
    span, count = key_layout(gathered)

    def visit(total, number):
        key_rows, value_rows = slice_keys(gathered, number, span, heads)
        scores, seen = block_scores(query_rows, key_rows, number * span, context)
        weights = jnp.where(seen, jnp.exp(scores - log_norm[..., None]), 0.0).astype(jnp.bfloat16)
        return total + jnp.einsum(
            "hgqk,khd->qhgd", weights, value_rows, preferred_element_type=jnp.float32
        )

    def step(total, number):
        return (lax.cond(visible(number, span, context), visit, keep_state, total, number), None)

    start_total = jnp.zeros((token_rows, heads, head_group, HEAD_SIZE), jnp.float32)
    final, unused = lax.scan(step, start_total, jnp.arange(count, dtype=jnp.int32))
    return final


def attend_back(query_rows, gathered, log_norm, back_mixed, delta, context):
    token_rows, heads, head_group = query_rows.shape[:3]
    span, count = key_layout(gathered)
    width = heads * HEAD_SIZE

    def visit(back_query, number):
        key_rows, value_rows = slice_keys(gathered, number, span, heads)
        scores, seen = block_scores(query_rows, key_rows, number * span, context)
        probs = jnp.where(seen, jnp.exp(scores - log_norm[..., None]), 0.0)
        back_probs = jnp.einsum(
            "qhgd,khd->hgqk", back_mixed, value_rows, preferred_element_type=jnp.float32
        )
        back_scores = (probs * (back_probs - delta[..., None]) * HEAD_SIZE ** (-0.5)).astype(
            jnp.bfloat16
        )
        back_query = back_query + jnp.einsum(
            "hgqk,khd->qhgd", back_scores, key_rows, preferred_element_type=jnp.float32
        )
        back_keys = jnp.einsum(
            "hgqk,qhgd->khd", back_scores, query_rows, preferred_element_type=jnp.float32
        )
        back_values = jnp.einsum(
            "hgqk,qhgd->khd",
            probs.astype(jnp.bfloat16),
            back_mixed,
            preferred_element_type=jnp.float32,
        )
        return (
            back_query,
            jnp.concatenate(
                [back_keys.reshape(span, width), back_values.reshape(span, width)], axis=1
            ),
        )

    def skip(back_query, number):
        return (back_query, jnp.zeros((span, 2 * width), jnp.float32))

    def step(back_query, number):
        return lax.cond(visible(number, span, context), visit, skip, back_query, number)

    start_query = jnp.zeros((token_rows, heads, head_group, HEAD_SIZE), jnp.float32)
    back_query, terms = lax.scan(step, start_query, jnp.arange(count, dtype=jnp.int32))
    return (back_query, terms.reshape(span * count, 2 * width))


def layer_front(inputs, weights, context, tables, fresh):
    attention_gain, query_weight, key_weight, value_weight, projection = weights[:5]
    token_rows = inputs.shape[0]
    query_heads = query_weight.shape[1] // HEAD_SIZE
    key_heads = key_weight.shape[1] // HEAD_SIZE
    head_group = query_heads // key_heads
    cosine, sine = tables
    normalized_input = rms_norm(inputs, attention_gain).astype(jnp.bfloat16)
    query_rows = rotate(
        product(normalized_input, query_weight).reshape(token_rows, query_heads, HEAD_SIZE),
        cosine,
        sine,
    ).astype(jnp.bfloat16)
    key_rows = rotate(
        product(normalized_input, key_weight).reshape(token_rows, key_heads, HEAD_SIZE),
        cosine,
        sine,
    ).astype(jnp.bfloat16)
    value_rows = product(normalized_input, value_weight).astype(jnp.bfloat16)
    local_pairs = jnp.concatenate(
        [key_rows.reshape(token_rows, key_heads * HEAD_SIZE), value_rows], axis=1
    )
    if fresh:
        gathered = lax.all_gather(local_pairs, "blk", axis=0, tiled=True)
    else:
        gathered = lax.all_gather(local_pairs, "blk", axis=0, tiled=True)
    grouped_heads = query_rows.reshape(token_rows, key_heads, head_group, HEAD_SIZE)
    log_norm = log_norms(grouped_heads, gathered, context)
    mixed = (
        attend(grouped_heads, gathered, log_norm, context)
        .reshape(token_rows, query_heads * HEAD_SIZE)
        .astype(jnp.bfloat16)
    )
    partial_value = product(mixed, projection)
    if fresh:
        summed = lax.psum(partial_value.astype(jnp.bfloat16), "tp").astype(jnp.float32)
    else:
        summed = lax.psum(partial_value.astype(jnp.bfloat16), "tp").astype(jnp.float32)
    return (inputs + summed, (normalized_input, grouped_heads, gathered, log_norm, mixed))


def ffn_parts(hidden, weights):
    inner_in = rms_norm(hidden, weights[5]).astype(jnp.bfloat16)
    gate = product(inner_in, weights[6])
    up = product(inner_in, weights[7])
    inner = swiglu(gate, up).astype(jnp.bfloat16)
    return (inner_in, gate, up, inner)


def ffn_output(hidden, weights):
    inner_in, gate, up, inner = ffn_parts(hidden, weights)
    return hidden + lax.psum(product(inner, weights[8]).astype(jnp.bfloat16), "tp").astype(
        jnp.float32
    )


def layer_back(inputs, weights, context, tables, saved, incoming):
    attention_gain, query_weight, key_weight, value_weight, projection = weights[:5]
    feedforward_gain, gate_weight, up_weight, down_weight = weights[5:]
    hidden, normalized_input, grouped_heads, gathered, log_norm, mixed = saved
    token_rows = inputs.shape[0]
    query_heads = query_weight.shape[1] // HEAD_SIZE
    key_heads = key_weight.shape[1] // HEAD_SIZE
    cosine, sine = tables
    inner_in, gate, up, inner = ffn_parts(hidden, weights)
    incoming_low = incoming.astype(jnp.bfloat16)
    gradient_down = product_left(inner, incoming_low)
    back_inner = product_right(incoming_low, down_weight)
    unused, pull = jax.vjp(swiglu, gate, up)
    back_gate, back_up = pull(back_inner)
    back_gate = back_gate.astype(jnp.bfloat16)
    back_up = back_up.astype(jnp.bfloat16)
    gradient_gate = product_left(inner_in, back_gate)
    gradient_up = product_left(inner_in, back_up)
    partial_value = product_right(back_gate, gate_weight) + product_right(back_up, up_weight)
    back_in = lax.psum(partial_value.astype(jnp.bfloat16), "tp").astype(jnp.float32)
    unused, pull = jax.vjp(rms_norm, hidden, feedforward_gain)
    back_hidden, gradient_feedforward_gain = pull(back_in)
    back_hidden = back_hidden + incoming
    hidden_low = back_hidden.astype(jnp.bfloat16)
    gradient_projection = product_left(mixed, hidden_low)
    back_mixed = (
        product_right(hidden_low, projection).astype(jnp.bfloat16).reshape(grouped_heads.shape)
    )
    delta = jnp.einsum(
        "qhgd,qhgd->hgq",
        back_mixed.astype(jnp.float32),
        mixed.reshape(grouped_heads.shape).astype(jnp.float32),
    )
    width = key_heads * HEAD_SIZE
    back_query, terms = attend_back(grouped_heads, gathered, log_norm, back_mixed, delta, context)
    back_pairs = lax.psum_scatter(
        terms.astype(jnp.bfloat16), "blk", scatter_dimension=0, tiled=True
    ).astype(jnp.float32)
    back_q = (
        unrotate(back_query.reshape(token_rows, query_heads, HEAD_SIZE), cosine, sine)
        .reshape(token_rows, query_heads * HEAD_SIZE)
        .astype(jnp.bfloat16)
    )
    back_k = (
        unrotate(back_pairs[:, :width].reshape(token_rows, key_heads, HEAD_SIZE), cosine, sine)
        .reshape(token_rows, width)
        .astype(jnp.bfloat16)
    )
    back_v = back_pairs[:, width:].astype(jnp.bfloat16)
    gradient_query = product_left(normalized_input, back_q)
    gradient_key = product_left(normalized_input, back_k)
    gradient_value = product_left(normalized_input, back_v)
    partial_value = (
        product_right(back_q, query_weight)
        + product_right(back_k, key_weight)
        + product_right(back_v, value_weight)
    )
    back_normed = lax.psum(partial_value.astype(jnp.bfloat16), "tp").astype(jnp.float32)
    unused, pull = jax.vjp(rms_norm, inputs, attention_gain)
    back_inputs, gradient_attention_gain = pull(back_normed)
    return (
        back_inputs + back_hidden,
        (
            gradient_attention_gain,
            gradient_query,
            gradient_key,
            gradient_value,
            gradient_projection,
            gradient_feedforward_gain,
            gradient_gate,
            gradient_up,
            gradient_down,
        ),
    )


def body(
    tokens,
    lengths,
    attention_gain_one,
    query_one,
    first_key_matrix,
    first_value_matrix,
    projection_one,
    feedforward_gain_one,
    gate_one,
    up_one,
    down_one,
    attention_gain_two,
    query_two,
    second_key_matrix,
    second_value_matrix,
    projection_two,
    feedforward_gain_two,
    gate_two,
    up_two,
    down_two,
    cotangent,
):
    token_rows = tokens.shape[0]
    places = lax.axis_index("blk") * token_rows + jnp.arange(token_rows, dtype=jnp.int32)
    owners, firsts = documents(lengths, places)
    context = (places, owners, firsts[0], places[token_rows - 1], lengths)
    tables = rotary_tables(places - firsts)
    first = (
        attention_gain_one,
        query_one,
        first_key_matrix,
        first_value_matrix,
        projection_one,
        feedforward_gain_one,
        gate_one,
        up_one,
        down_one,
    )
    second = (
        attention_gain_two,
        query_two,
        second_key_matrix,
        second_value_matrix,
        projection_two,
        feedforward_gain_two,
        gate_two,
        up_two,
        down_two,
    )
    inputs_one = tokens.astype(jnp.float32)
    hidden_one, kept_one = layer_front(inputs_one, first, context, tables, True)
    inputs_two = ffn_output(hidden_one, first)
    hidden_two, kept_two = layer_front(inputs_two, second, context, tables, True)
    result = ffn_output(hidden_two, second).astype(jnp.bfloat16)
    hidden_again, kept_again = layer_front(inputs_two, second, context, tables, False)
    saved_two = (hidden_again,) + kept_again
    back_two, grads_two = layer_back(
        inputs_two, second, context, tables, saved_two, cotangent.astype(jnp.float32)
    )
    hidden_again, kept_again = layer_front(inputs_one, first, context, tables, False)
    saved_one = (hidden_again,) + kept_again
    back_one, grads_one = layer_back(inputs_one, first, context, tables, saved_one, back_two)
    shares = (
        lax.psum_scatter(
            grads_one[0].astype(jnp.bfloat16), "blk", scatter_dimension=0, tiled=True
        ).astype(jnp.float32),
        lax.psum_scatter(
            grads_one[1].astype(jnp.bfloat16), "blk", scatter_dimension=0, tiled=True
        ).astype(jnp.float32),
        lax.psum_scatter(
            grads_one[2].astype(jnp.bfloat16), "blk", scatter_dimension=0, tiled=True
        ).astype(jnp.float32),
        lax.psum_scatter(
            grads_one[3].astype(jnp.bfloat16), "blk", scatter_dimension=0, tiled=True
        ).astype(jnp.float32),
        lax.psum_scatter(
            grads_one[4].astype(jnp.bfloat16), "blk", scatter_dimension=1, tiled=True
        ).astype(jnp.float32),
        lax.psum_scatter(
            grads_one[5].astype(jnp.bfloat16), "blk", scatter_dimension=0, tiled=True
        ).astype(jnp.float32),
        lax.psum_scatter(
            grads_one[6].astype(jnp.bfloat16), "blk", scatter_dimension=0, tiled=True
        ).astype(jnp.float32),
        lax.psum_scatter(
            grads_one[7].astype(jnp.bfloat16), "blk", scatter_dimension=0, tiled=True
        ).astype(jnp.float32),
        lax.psum_scatter(
            grads_one[8].astype(jnp.bfloat16), "blk", scatter_dimension=1, tiled=True
        ).astype(jnp.float32),
        lax.psum_scatter(
            grads_two[0].astype(jnp.bfloat16), "blk", scatter_dimension=0, tiled=True
        ).astype(jnp.float32),
        lax.psum_scatter(
            grads_two[1].astype(jnp.bfloat16), "blk", scatter_dimension=0, tiled=True
        ).astype(jnp.float32),
        lax.psum_scatter(
            grads_two[2].astype(jnp.bfloat16), "blk", scatter_dimension=0, tiled=True
        ).astype(jnp.float32),
        lax.psum_scatter(
            grads_two[3].astype(jnp.bfloat16), "blk", scatter_dimension=0, tiled=True
        ).astype(jnp.float32),
        lax.psum_scatter(
            grads_two[4].astype(jnp.bfloat16), "blk", scatter_dimension=1, tiled=True
        ).astype(jnp.float32),
        lax.psum_scatter(
            grads_two[5].astype(jnp.bfloat16), "blk", scatter_dimension=0, tiled=True
        ).astype(jnp.float32),
        lax.psum_scatter(
            grads_two[6].astype(jnp.bfloat16), "blk", scatter_dimension=0, tiled=True
        ).astype(jnp.float32),
        lax.psum_scatter(
            grads_two[7].astype(jnp.bfloat16), "blk", scatter_dimension=0, tiled=True
        ).astype(jnp.float32),
        lax.psum_scatter(
            grads_two[8].astype(jnp.bfloat16), "blk", scatter_dimension=1, tiled=True
        ).astype(jnp.float32),
    )
    shares = tuple(shares)
    return (result, back_one) + shares


def solution(mesh):
    in_specs = (
        P("blk", None),
        P(),
        P(),
        P(None, "tp"),
        P(None, "tp"),
        P(None, "tp"),
        P("tp", None),
        P(),
        P(None, "tp"),
        P(None, "tp"),
        P("tp", None),
        P(),
        P(None, "tp"),
        P(None, "tp"),
        P(None, "tp"),
        P("tp", None),
        P(),
        P(None, "tp"),
        P(None, "tp"),
        P("tp", None),
        P("blk", None),
    )
    out_specs = (
        P("blk", None),
        P("blk", None),
        P("blk"),
        P("blk", "tp"),
        P("blk", "tp"),
        P("blk", "tp"),
        P("tp", "blk"),
        P("blk"),
        P("blk", "tp"),
        P("blk", "tp"),
        P("tp", "blk"),
        P("blk"),
        P("blk", "tp"),
        P("blk", "tp"),
        P("blk", "tp"),
        P("tp", "blk"),
        P("blk"),
        P("blk", "tp"),
        P("blk", "tp"),
        P("tp", "blk"),
    )
    return jax.shard_map(body, mesh=mesh, in_specs=in_specs, out_specs=out_specs, check_vma=False)
```

profile of v0, /device:TPU:0, one launch (start us, length us, event | category | flops | bytes accessed | tf_op | source)
XLA Modules:
  0.0 1656.9 jit_solution(3239092082185918942)
XLA Ops:
  19.7 42.7 %all-gather.3.cloned.1.call-done = bf16[2048,384]{0,1:T(8,128)(2,1)} async-done(((bf16[256,384]{0,1:T(8,128)(2,1)}), bf16[2048,384]{0,1:T(8,128)(2,1)}) %all-gather.3.cloned.1.call-update) | async-done | bytes 1572880 | tf_op jit(solution)/shard_map/all_gather | solution.py:219
  62.4 8.6 conditional.6
  72.4 11.6 conditional.7
  78.4 5.5 fusion.9
  89.7 32.5 %all-reduce.14.cloned.1.call-done = bf16[256,1536]{1,0:T(8,128)(2,1)} async-done(((bf16[256,1536]{1,0:T(8,128)(2,1)}), bf16[256,1536]{1,0:T(8,128)(2,1)}) %all-reduce.14.cloned.1.call-update) | async-done | bytes 786448 | tf_op jit(solution)/shard_map/psum | solution.py:231
  125.5 3.2 fusion.143
  133.6 34.8 %all-reduce.16.cloned.1.call-done = bf16[256,1536]{1,0:T(8,128)(2,1)} async-done(((bf16[256,1536]{1,0:T(8,128)(2,1)}), bf16[256,1536]{1,0:T(8,128)(2,1)}) %all-reduce.16.cloned.1.call-update) | async-done | bytes 786448 | tf_op jit(solution)/shard_map/psum | solution.py:247
  177.1 42.5 %all-gather.5.cloned.1.call-done = bf16[2048,384]{0,1:T(8,128)(2,1)} async-done(((bf16[256,384]{0,1:T(8,128)(2,1)}), bf16[2048,384]{0,1:T(8,128)(2,1)}) %all-gather.5.cloned.1.call-update) | async-done | bytes 1572880 | tf_op jit(solution)/shard_map/all_gather | solution.py:219
  219.6 8.3 conditional.8
  228.5 11.6 conditional.9
  234.6 5.5 fusion.22
  245.6 32.7 %all-reduce.18.cloned.1.call-done = bf16[256,1536]{1,0:T(8,128)(2,1)} async-done(((bf16[256,1536]{1,0:T(8,128)(2,1)}), bf16[256,1536]{1,0:T(8,128)(2,1)}) %all-reduce.18.cloned.1.call-update) | async-done | bytes 786448 | tf_op jit(solution)/shard_map/psum | solution.py:231
  289.5 34.8 %all-reduce.20.cloned.1.call-done = bf16[256,1536]{1,0:T(8,128)(2,1)} async-done(((bf16[256,1536]{1,0:T(8,128)(2,1)}), bf16[256,1536]{1,0:T(8,128)(2,1)}) %all-reduce.20.cloned.1.call-update) | async-done | bytes 786448 | tf_op jit(solution)/shard_map/psum | solution.py:271
  334.0 25.0 %conditional.10 = (f32[256,2,2,96]{0,3,2,1:T(8,128)}, bf16[2048,384]{0,1:T(8,128)(2,1)}) conditional(s32[]{:T(128)} %bitcast.76, f32[256,2,2,96]{0,3,2,1:T(8,128)S(1)} %broadcast.301, (s32[256]{0:T(256)S(1)}, s32[5]{0:T(128)}, s32[256]{0:T(256)S(1)}, bf16[2048,384]{0,1:T(8,128)(2,1)}, bf16[256,2,2,96]{0,3,2,1:T(8,128)(2,1)}, ...), branch_computations={%region_33.34_spmd, %region_34.37_spmd} | conditional | flops 2045570048 | bytes 87345480 | solution.py:189
  336.7 4.6 fusion.139
  344.6 7.2 fusion.28
  363.9 61.0 %reduce-scatter.17.cloned.1.call-done = bf16[256,384]{0,1:T(8,128)(2,1)} async-done(((bf16[2048,384]{0,1:T(8,128)(2,1)}), bf16[256,384]{0,1:T(8,128)(2,1)}) %reduce-scatter.17.cloned.1.call-update) | async-done | bytes 196624 | tf_op jit(solution)/shard_map/reduce_scatter | solution.py:287
  431.1 33.4 %all-reduce.22.cloned.1.call-done = bf16[256,1536]{1,0:T(8,128)(2,1)} async-done(((bf16[256,1536]{1,0:T(8,128)(2,1)}), bf16[256,1536]{1,0:T(8,128)(2,1)}) %all-reduce.22.cloned.1.call-update) | async-done | bytes 786448 | tf_op jit(solution)/shard_map/psum | solution.py:309
  476.1 34.8 %all-reduce.24.cloned.1.call-done = bf16[256,1536]{1,0:T(8,128)(2,1)} async-done(((bf16[256,1536]{1,0:T(8,128)(2,1)}), bf16[256,1536]{1,0:T(8,128)(2,1)}) %all-reduce.24.cloned.1.call-update) | async-done | bytes 786448 | tf_op jit(solution)/shard_map/psum | solution.py:271
  521.2 26.1 %conditional.11 = (f32[256,2,2,96]{0,3,2,1:T(8,128)S(1)}, bf16[2048,384]{0,1:T(8,128)(2,1)}) conditional(s32[]{:T(128)} %bitcast.76, f32[256,2,2,96]{0,3,2,1:T(8,128)S(1)} %broadcast.301, (s32[256]{0:T(256)S(1)}, s32[5]{0:T(128)}, s32[256]{0:T(256)S(1)}, bf16[2048,384]{0,1:T(8,128)(2,1)}, bf16[256,2,2,96]{0,3,2,1:T(8,128)(2,1)}, ...), branch_computations={%region_42.43_spmd, %region_43.46_spmd} | conditional | flops 2045570048 | bytes 85772552 | solution.py:189
  524.1 5.8 fusion.141
  532.7 7.2 fusion.43
  550.3 3.2 convolution_convert_fusion.6
  558.6 4.0 convolution_convert_fusion.2
  562.7 4.1 convolution_convert_fusion.1
  567.0 4.0 convolution_convert_fusion
  574.9 3.1 convolution_convert_fusion.8
  582.9 30.4 %reduce-scatter.19.cloned.1.call-done = bf16[256,384]{0,1:T(8,128)(2,1)} async-done(((bf16[2048,384]{0,1:T(8,128)(2,1)}), bf16[256,384]{0,1:T(8,128)(2,1)}) %reduce-scatter.19.cloned.1.call-update) | async-done | bytes 196624 | tf_op jit(solution)/shard_map/reduce_scatter | solution.py:287
  623.5 3.9 convolution_convert_fusion.5
  627.5 4.0 convolution_convert_fusion.4
  631.6 4.2 convolution_convert_fusion.3
  637.7 41.9 %reduce-scatter.35.cloned.1.call-done = bf16[192,384]{1,0:T(8,128)(2,1)} async-done(((bf16[1536,384]{1,0:T(8,128)(2,1)}), bf16[192,384]{1,0:T(8,128)(2,1)}) %reduce-scatter.35.cloned.1.call-update) | async-done | bytes 147472 | tf_op jit(solution)/shard_map/reduce_scatter | solution.py:422
  681.3 64.6 %reduce-scatter.41.cloned.1.call-done = bf16[384,192]{0,1:T(8,128)(2,1)} async-done(((bf16[384,1536]{0,1:T(8,128)(2,1)}), bf16[384,192]{0,1:T(8,128)(2,1)}) %reduce-scatter.41.cloned.1.call-update) | async-done | bytes 147472 | tf_op jit(solution)/shard_map/reduce_scatter | solution.py:431
  747.5 63.7 %reduce-scatter.37.cloned.1.call-done = bf16[192,192]{1,0:T(8,128)(2,1)} async-done(((bf16[1536,192]{1,0:T(8,128)(2,1)}), bf16[192,192]{1,0:T(8,128)(2,1)}) %reduce-scatter.37.cloned.1.call-update) | async-done | bytes 73744 | tf_op jit(solution)/shard_map/reduce_scatter | solution.py:425
  812.8 64.0 %reduce-scatter.39.cloned.1.call-done = bf16[192,192]{1,0:T(8,128)(2,1)} async-done(((bf16[1536,192]{1,0:T(8,128)(2,1)}), bf16[192,192]{1,0:T(8,128)(2,1)}) %reduce-scatter.39.cloned.1.call-update) | async-done | bytes 73744 | tf_op jit(solution)/shard_map/reduce_scatter | solution.py:428
  878.4 75.3 %reduce-scatter.43.cloned.1.call-done = bf16[192,1024]{1,0:T(8,128)(2,1)} async-done(((bf16[1536,1024]{1,0:T(8,128)(2,1)}), bf16[192,1024]{1,0:T(8,128)(2,1)}) %reduce-scatter.43.cloned.1.call-update) | async-done | bytes 393232 | tf_op jit(solution)/shard_map/reduce_scatter | solution.py:437
  955.6 74.9 %reduce-scatter.45.cloned.1.call-done = bf16[192,1024]{1,0:T(8,128)(2,1)} async-done(((bf16[1536,1024]{1,0:T(8,128)(2,1)}), bf16[192,1024]{1,0:T(8,128)(2,1)}) %reduce-scatter.45.cloned.1.call-update) | async-done | bytes 393232 | tf_op jit(solution)/shard_map/reduce_scatter | solution.py:440
  1032.5 75.0 %reduce-scatter.47.cloned.1.call-done = bf16[1024,192]{0,1:T(8,128)(2,1)} async-done(((bf16[1024,1536]{0,1:T(8,128)(2,1)}), bf16[1024,192]{0,1:T(8,128)(2,1)}) %reduce-scatter.47.cloned.1.call-update) | async-done | bytes 393232 | tf_op jit(solution)/shard_map/reduce_scatter | solution.py:443
  1109.5 64.5 %reduce-scatter.21.cloned.1.call-done = bf16[192,384]{1,0:T(8,128)(2,1)} async-done(((bf16[1536,384]{1,0:T(8,128)(2,1)}), bf16[192,384]{1,0:T(8,128)(2,1)}) %reduce-scatter.21.cloned.1.call-update) | async-done | bytes 147472 | tf_op jit(solution)/shard_map/reduce_scatter | solution.py:395
  1175.6 64.8 %reduce-scatter.27.cloned.1.call-done = bf16[384,192]{0,1:T(8,128)(2,1)} async-done(((bf16[384,1536]{0,1:T(8,128)(2,1)}), bf16[384,192]{0,1:T(8,128)(2,1)}) %reduce-scatter.27.cloned.1.call-update) | async-done | bytes 147472 | tf_op jit(solution)/shard_map/reduce_scatter | solution.py:404
  1242.0 43.2 %all-reduce.26.cloned.1.call-done = (bf16[256,1536]{1,0:T(8,128)(2,1)}, bf16[256,1536]{1,0:T(8,128)(2,1)}) async-done(((bf16[256,1536]{1,0:T(8,128)(2,1)}, bf16[256,1536]{1,0:T(8,128)(2,1)}), (bf16[256,1536]{1,0:T(8,128)(2,1)}, bf16[256,1536]{1,0:T(8,128)(2,1)})) %all-reduce.26.cloned.1.call-update) | async-done | bytes 1572880 | tf_op jit(solution)/shard_map/psum | solution.py:247
  1287.3 37.3 %all-reduce.4 = (bf16[1536]{0:T(1024)(128)(2,1)S(1)}, bf16[1536]{0:T(1024)(128)(2,1)S(1)}, bf16[1536]{0:T(1024)(128)(2,1)S(1)}, bf16[1536]{0:T(1024)(128)(2,1)S(1)}) all-reduce(bf16[1536]{0:T(1024)(128)(2,1)S(1)} %get-tuple-element.680, bf16[1536]{0:T(1024)(128)(2,1)S(1)} %get-tuple-element.678, ...), channel_id=4, replica_groups=mesh['blk'=8,'tp'=4] {'blk'}, use_global_device_ids=true, to_apply=%region_50.51.clone | all-reduce | flops 6144 | bytes 24576
  1326.0 4.6 fusion.79
  1330.6 21.2 %reduce-scatter.23.cloned.1.call-done = bf16[192,192]{1,0:T(8,128)(2,1)} async-done(((bf16[1536,192]{1,0:T(8,128)(2,1)}), bf16[192,192]{1,0:T(8,128)(2,1)}) %reduce-scatter.23.cloned.1.call-update) | async-done | bytes 73744 | tf_op jit(solution)/shard_map/reduce_scatter | solution.py:398
  1353.4 63.6 %reduce-scatter.25.cloned.1.call-done = bf16[192,192]{1,0:T(8,128)(2,1)} async-done(((bf16[1536,192]{1,0:T(8,128)(2,1)}), bf16[192,192]{1,0:T(8,128)(2,1)}) %reduce-scatter.25.cloned.1.call-update) | async-done | bytes 73744 | tf_op jit(solution)/shard_map/reduce_scatter | solution.py:401
  1418.6 75.6 %reduce-scatter.29.cloned.1.call-done = bf16[192,1024]{1,0:T(8,128)(2,1)} async-done(((bf16[1536,1024]{1,0:T(8,128)(2,1)}), bf16[192,1024]{1,0:T(8,128)(2,1)}) %reduce-scatter.29.cloned.1.call-update) | async-done | bytes 393232 | tf_op jit(solution)/shard_map/reduce_scatter | solution.py:410
  1496.1 75.1 %reduce-scatter.31.cloned.1.call-done = bf16[192,1024]{1,0:T(8,128)(2,1)} async-done(((bf16[1536,1024]{1,0:T(8,128)(2,1)}), bf16[192,1024]{1,0:T(8,128)(2,1)}) %reduce-scatter.31.cloned.1.call-update) | async-done | bytes 393232 | tf_op jit(solution)/shard_map/reduce_scatter | solution.py:413
  1573.2 75.1 %reduce-scatter.33.cloned.1.call-done = bf16[1024,192]{0,1:T(8,128)(2,1)} async-done(((bf16[1024,1536]{0,1:T(8,128)(2,1)}), bf16[1024,192]{0,1:T(8,128)(2,1)}) %reduce-scatter.33.cloned.1.call-update) | async-done | bytes 393232 | tf_op jit(solution)/shard_map/reduce_scatter | solution.py:416
  (455 shorter events, 204.7 us)
Async XLA Ops:
  7.2 276.9 %copy-start = (bf16[1024,1536]{1,0:T(8,128)(2,1)S(1)}, bf16[1024,1536]{1,0:T(8,128)(2,1)}, u32[]{:S(2)}) copy-start(bf16[1024,1536]{1,0:T(8,128)(2,1)} %param.52) | copy-start | bytes 9437188
  7.2 55.2 %all-gather.3.cloned.1.call-start = ((), (), s32[]{:S(2)}) async-start(), calls=%async_computation.16 | async-start | bytes 1769472 | tf_op jit(solution)/shard_map/all_gather | solution.py:219
  7.3 65.1 %copy-start.81 = (s32[256]{0:T(256)}, s32[256]{0:T(256)S(1)}, u32[]{:S(2)}) copy-start(s32[256]{0:T(256)S(1)} %iota_add_fusion) | copy-start | bytes 3076
  12.9 59.5 %copy-start.77 = (s32[256]{0:T(256)}, s32[256]{0:T(256)S(1)}, u32[]{:S(2)}) copy-start(s32[256]{0:T(256)S(1)} %convert_reduce_fusion.6) | copy-start | bytes 3076
  14.2 107.9 %all-reduce.14.cloned.1.call-start = ((), (), s32[]{:S(2)}) async-start(), calls=%async_computation.17 | async-start | bytes 1572864 | tf_op jit(solution)/shard_map/psum | solution.py:231
  18.9 43.5 %copy-start.109 = (s32[5]{0:T(128)S(1)}, s32[5]{0:T(128)}, u32[]{:S(2)}) copy-start(s32[5]{0:T(128)} %param.34) | copy-start | bytes 64
  89.2 36.0 %copy-start.75 = (f32[1536]{0:T(1024)S(1)}, f32[1536]{0:T(1024)}, u32[]{:S(2)}) copy-start(f32[1536]{0:T(1024)} %param.40) | copy-start | bytes 18436
  89.2 79.2 %all-reduce.16.cloned.1.call-start = ((), (), s32[]{:S(2)}) async-start(), calls=%async_computation.18 | async-start | bytes 1572864 | tf_op jit(solution)/shard_map/psum | solution.py:247
  133.5 36.9 %copy-start.74 = (f32[1536]{0:T(1024)S(1)}, f32[1536]{0:T(1024)}, u32[]{:S(2)}) copy-start(f32[1536]{0:T(1024)} %param.44) | copy-start | bytes 18436
  133.6 86.0 %all-gather.5.cloned.1.call-start = ((), (), s32[]{:S(2)}) async-start(), calls=%async_computation.19 | async-start | bytes 1769472 | tf_op jit(solution)/shard_map/all_gather | solution.py:219
  174.1 104.3 %all-reduce.18.cloned.1.call-start = ((), (), s32[]{:S(2)}) async-start(), calls=%async_computation.20 | async-start | bytes 1572864 | tf_op jit(solution)/shard_map/psum | solution.py:231
  245.4 35.0 %copy-start.73 = (f32[1536]{0:T(1024)S(1)}, f32[1536]{0:T(1024)}, u32[]{:S(2)}) copy-start(f32[1536]{0:T(1024)} %param.49) | copy-start | bytes 18436
  245.4 78.9 %all-reduce.20.cloned.1.call-start = ((), (), s32[]{:S(2)}) async-start(), calls=%async_computation.21 | async-start | bytes 1572864 | tf_op jit(solution)/shard_map/psum | solution.py:271
  289.4 135.5 %reduce-scatter.17.cloned.1.call-start = ((), (), s32[]{:S(2)}) async-start(), calls=%async_computation.22 | async-start | bytes 1769472 | tf_op jit(solution)/shard_map/reduce_scatter | solution.py:287
  344.1 9.4 slice-start.2
  344.6 7.2 copy-start.31
  344.6 8.8 slice-start.3
  359.0 105.4 %all-reduce.22.cloned.1.call-start = ((), (), s32[]{:S(2)}) async-start(), calls=%async_computation.23 | async-start | bytes 1572864 | tf_op jit(solution)/shard_map/psum | solution.py:309
  429.4 35.0 %copy-start.90 = (f32[256]{0:T(256)S(1)}, f32[256]{0:T(256)}, u32[]{:S(2)}) copy-start(f32[256]{0:T(256)} %copy-done.89) | copy-start | bytes 3076
  430.7 36.6 %copy-start.101 = (f32[256]{0:T(256)S(1)}, f32[256]{0:T(256)}, u32[]{:S(2)}) copy-start(f32[256]{0:T(256)} %copy-done.100) | copy-start | bytes 3076
  430.8 80.1 %all-reduce.24.cloned.1.call-start = ((), (), s32[]{:S(2)}) async-start(), calls=%async_computation.24 | async-start | bytes 1572864 | tf_op jit(solution)/shard_map/psum | solution.py:271
  474.1 36.8 %copy-start.76 = (f32[1536]{0:T(1024)S(1)}, f32[1536]{0:T(1024)}, u32[]{:S(2)}) copy-start(f32[1536]{0:T(1024)} %param.40) | copy-start | bytes 18436
  474.1 36.8 %copy-start.88 = (f32[256]{0:T(256)S(1)}, f32[256]{0:T(256)}, u32[]{:S(2)}) copy-start(f32[256]{0:T(256)} %copy-done.87) | copy-start | bytes 3076
  476.0 137.2 %reduce-scatter.19.cloned.1.call-start = ((), (), s32[]{:S(2)}) async-start(), calls=%async_computation.25 | async-start | bytes 1769472 | tf_op jit(solution)/shard_map/reduce_scatter | solution.py:287
  532.1 8.7 slice-start
  532.6 7.2 copy-start.29
  532.7 8.1 slice-start.1
  547.3 132.3 %reduce-scatter.35.cloned.1.call-start = ((), (), s32[]{:S(2)}) async-start(), calls=%async_computation.33 | async-start | bytes 1327104 | tf_op jit(solution)/shard_map/reduce_scatter | solution.py:422
  550.2 195.7 %reduce-scatter.41.cloned.1.call-start = ((), (), s32[]{:S(2)}) async-start(), calls=%async_computation.36 | async-start | bytes 1327104 | tf_op jit(solution)/shard_map/reduce_scatter | solution.py:431
  553.5 257.7 %reduce-scatter.37.cloned.1.call-start = ((), (), s32[]{:S(2)}) async-start(), calls=%async_computation.34 | async-start | bytes 884736 | tf_op jit(solution)/shard_map/reduce_scatter | solution.py:425
  556.1 320.8 %reduce-scatter.39.cloned.1.call-start = ((), (), s32[]{:S(2)}) async-start(), calls=%async_computation.35 | async-start | bytes 884736 | tf_op jit(solution)/shard_map/reduce_scatter | solution.py:428
  558.6 395.1 %reduce-scatter.43.cloned.1.call-start = ((), (), s32[]{:S(2)}) async-start(), calls=%async_computation.37 | async-start | bytes 3538944 | tf_op jit(solution)/shard_map/reduce_scatter | solution.py:437
  562.6 467.9 %reduce-scatter.45.cloned.1.call-start = ((), (), s32[]{:S(2)}) async-start(), calls=%async_computation.38 | async-start | bytes 3538944 | tf_op jit(solution)/shard_map/reduce_scatter | solution.py:440
  566.8 540.8 %reduce-scatter.47.cloned.1.call-start = ((), (), s32[]{:S(2)}) async-start(), calls=%async_computation.39 | async-start | bytes 3538944 | tf_op jit(solution)/shard_map/reduce_scatter | solution.py:443
  571.0 602.9 %reduce-scatter.21.cloned.1.call-start = ((), (), s32[]{:S(2)}) async-start(), calls=%async_computation.26 | async-start | bytes 1327104 | tf_op jit(solution)/shard_map/reduce_scatter | solution.py:395
  574.8 665.6 %reduce-scatter.27.cloned.1.call-start = ((), (), s32[]{:S(2)}) async-start(), calls=%async_computation.29 | async-start | bytes 1327104 | tf_op jit(solution)/shard_map/reduce_scatter | solution.py:404
  578.0 707.3 %all-reduce.26.cloned.1.call-start = ((), (), s32[]{:S(2)}) async-start(), calls=%async_computation.40 | async-start | bytes 3145728 | tf_op jit(solution)/shard_map/psum | solution.py:247
  581.0 33.2 %copy-start.27 = (f32[256,96]{0,1:T(8,128)S(1)}, f32[256,96]{0,1:T(8,128)}, u32[]{:S(2)}) copy-start(f32[256,96]{0,1:T(8,128)} %copy-done.24) | copy-start | bytes 294916
  581.0 33.3 %copy-start.23 = (f32[256,96]{0,1:T(8,128)S(1)}, f32[256,96]{0,1:T(8,128)}, u32[]{:S(2)}) copy-start(f32[256,96]{0,1:T(8,128)} %copy-done.17) | copy-start | bytes 294916
  618.2 733.6 %reduce-scatter.23.cloned.1.call-start = ((), (), s32[]{:S(2)}) async-start(), calls=%async_computation.27 | async-start | bytes 884736 | tf_op jit(solution)/shard_map/reduce_scatter | solution.py:398
  620.8 796.2 %reduce-scatter.25.cloned.1.call-start = ((), (), s32[]{:S(2)}) async-start(), calls=%async_computation.28 | async-start | bytes 884736 | tf_op jit(solution)/shard_map/reduce_scatter | solution.py:401
  623.5 870.7 %reduce-scatter.29.cloned.1.call-start = ((), (), s32[]{:S(2)}) async-start(), calls=%async_computation.30 | async-start | bytes 3538944 | tf_op jit(solution)/shard_map/reduce_scatter | solution.py:410
  627.4 943.8 %reduce-scatter.31.cloned.1.call-start = ((), (), s32[]{:S(2)}) async-start(), calls=%async_computation.31 | async-start | bytes 3538944 | tf_op jit(solution)/shard_map/reduce_scatter | solution.py:413
  631.5 1016.7 %reduce-scatter.33.cloned.1.call-start = ((), (), s32[]{:S(2)}) async-start(), calls=%async_computation.32 | async-start | bytes 3538944 | tf_op jit(solution)/shard_map/reduce_scatter | solution.py:416
  955.6 329.6 %copy-start.97 = (f32[256]{0:T(256)S(1)}, f32[256]{0:T(256)}, u32[]{:S(2)}) copy-start(f32[256]{0:T(256)} %copy-done.95) | copy-start | bytes 3076
  1032.5 254.8 %copy-start.93 = (bf16[1536]{0:T(1024)(128)(2,1)S(1)}, bf16[1536]{0:T(1024)(128)(2,1)}, u32[]{:S(2)}) copy-start(bf16[1536]{0:T(1024)(128)(2,1)} %get-tuple-element.674) | copy-start | bytes 9220
  1032.5 254.8 %copy-start.94 = (bf16[1536]{0:T(1024)(128)(2,1)S(1)}, bf16[1536]{0:T(1024)(128)(2,1)}, u32[]{:S(2)}) copy-start(bf16[1536]{0:T(1024)(128)(2,1)} %get-tuple-element.676) | copy-start | bytes 9220
  1032.5 293.4 %copy-start.99 = (f32[256]{0:T(256)S(1)}, f32[256]{0:T(256)}, u32[]{:S(2)}) copy-start(f32[256]{0:T(256)} %copy-done.98) | copy-start | bytes 3076
  (95 other events, 231.9 us)
Sparse Core Ops, SparseCore 0:
  14.4 47.9 all-gather.2
  89.3 32.8 all-reduce.13
  133.7 34.6 all-reduce.15
  174.2 45.3 all-gather.4
  245.5 32.7 all-reduce.17
  289.6 34.6 all-reduce.19
  359.1 65.6 reduce-scatter.16
  430.9 33.4 all-reduce.21
  476.1 34.6 all-reduce.23
  547.4 65.7 reduce-scatter.18
  616.6 62.9 reduce-scatter.34
  682.9 62.9 reduce-scatter.40
  749.8 61.4 reduce-scatter.36
  815.3 61.4 reduce-scatter.38
  880.3 73.3 reduce-scatter.42
  957.1 73.3 reduce-scatter.44
  1034.0 73.5 reduce-scatter.46
  1110.8 63.1 reduce-scatter.20
  1177.4 62.9 reduce-scatter.26
  1243.2 42.0 all-reduce.25
  1289.1 62.6 reduce-scatter.22
  1355.5 61.4 reduce-scatter.24
  1420.6 73.5 reduce-scatter.28
  1497.6 73.5 reduce-scatter.30
  1574.8 73.3 reduce-scatter.32
where the time goes:
time: 1670 us; the launch traced here: 1660 us
  waiting for transfers between devices  1320 us (79%)
  matrix products  143 us (9%)
  other arithmetic  102 us (6%)
  blocking collectives  37.3 us (2%)
  local copies, waits for them, and re-layouts  31.6 us (2%)
  between operations  17.6 us (1%)
    psum x3, waiting for transfers between devices, layer_back(): lax.psum(partial_value.astype(jnp.bfloat16), 'tp').astype(jnp.float32)  103 us
    reduce_scatter x2, waiting for transfers between devices, layer_back(): lax.psum_scatter(terms.astype(jnp.bfloat16), 'blk', scatter_dimension=0,...  91.4 us
    all_gather x2, waiting for transfers between devices, layer_front(): gathered = lax.all_gather(local_pairs, 'blk', axis=0, tiled=True)  85.2 us
    psum x2, waiting for transfers between devices, ffn_output(): lax.psum(product(inner, weights[8]).astype(jnp.bfloat16), 'tp')  78 us
    reduce_scatter x1, waiting for transfers between devices, body(): lax.psum_scatter(grads_one[6].astype(jnp.bfloat16), 'blk', scatter_dimens...  75.6 us
    reduce_scatter x1, waiting for transfers between devices, body(): lax.psum_scatter(grads_two[6].astype(jnp.bfloat16), 'blk', scatter_dimens...  75.3 us
    reduce_scatter x1, waiting for transfers between devices, body(): lax.psum_scatter(grads_one[7].astype(jnp.bfloat16), 'blk', scatter_dimens...  75.1 us
    reduce_scatter x1, waiting for transfers between devices, body(): lax.psum_scatter(grads_one[8].astype(jnp.bfloat16), 'blk', scatter_dimens...  75.1 us
  transfers between devices with their start and end apart: 25, of which 25 were waited for; matrix products, arithmetic and copies ran while one was open for 6% of the time, Pallas kernels for 0%

commit v1 on v0

v1 whole, which is shorter than its diff:
```python
import functools

import jax
import jax.numpy as jnp
from jax import lax
from jax.experimental import pallas as pl
from jax.experimental.pallas import tpu as pltpu
from jax.sharding import PartitionSpec as P

HEAD_SIZE = 96
EPSILON = 1e-05
ROTARY_BASE = 100000.0
NEGATIVE = -1e30
SCALE = HEAD_SIZE ** (-0.5)
BF16 = jnp.bfloat16
F32 = jnp.float32


def product(left, right):
    return jnp.dot(left, right, preferred_element_type=F32)


def product_left(left, right):
    return lax.dot_general(left, right, (((0,), (0,)), ((), ())), preferred_element_type=F32)


def product_right(left, right):
    return lax.dot_general(left, right, (((1,), (1,)), ((), ())), preferred_element_type=F32)


def rms_norm(rows, gain):
    return rows * lax.rsqrt(jnp.mean(rows * rows, axis=-1, keepdims=True) + EPSILON) * gain


def rms_norm_back(rows, gain, incoming):
    scale = lax.rsqrt(jnp.mean(rows * rows, axis=-1, keepdims=True) + EPSILON)
    weighted = incoming * gain
    inner = jnp.mean(rows * weighted, axis=-1, keepdims=True)
    back = scale * weighted - rows * (scale * scale * scale * inner)
    return back, jnp.sum(incoming * rows * scale, axis=0)


def rotate(rows, cosine, sine):
    half = HEAD_SIZE // 2
    turned = jnp.concatenate([-rows[..., half:], rows[..., :half]], axis=-1)
    return rows * cosine + turned * sine


def unrotate(rows, cosine, sine):
    half = HEAD_SIZE // 2
    scaled = rows * sine
    return rows * cosine + jnp.concatenate([scaled[..., half:], -scaled[..., :half]], axis=-1)


def rotary_tables(positions):
    half = HEAD_SIZE // 2
    rates = ROTARY_BASE ** (-(jnp.arange(half).astype(F32) * 2.0 / HEAD_SIZE))
    angle = positions.astype(F32)[:, None] * rates[None, :]
    angle = jnp.concatenate([angle, angle], axis=-1)
    return jnp.cos(angle), jnp.sin(angle)


def first_tokens(lengths, index):
    bounds = jnp.cumsum(lengths)
    starts = bounds - lengths
    owner = jnp.sum((index[:, None] >= bounds[None, :]).astype(jnp.int32), axis=1)
    picks = owner[:, None] == jnp.arange(lengths.shape[0], dtype=jnp.int32)[None, :]
    return jnp.sum(jnp.where(picks, starts[None, :], 0), axis=1).astype(jnp.int32)


def swap(rows, axis, size, bit):
    return lax.ppermute(rows, axis, [(i, i ^ bit) for i in range(size)])


def sum_tp(partial, core):
    half = partial.shape[0] // 2
    keep = lax.dynamic_slice_in_dim(partial, core * half, half, 0)
    give = lax.dynamic_slice_in_dim(partial, (1 - core) * half, half, 0).astype(BF16)
    pair = (keep + swap(give, "tp", 4, 1).astype(F32)).astype(BF16)
    whole = (pair.astype(F32) + swap(pair, "tp", 4, 2).astype(F32)).astype(BF16)
    other = swap(whole, "tp", 4, 1)
    top = jnp.where(core == 0, whole, other)
    bottom = jnp.where(core == 0, other, whole)
    return jnp.concatenate([top, bottom], axis=0)


def line_gather(rows, blocks, step):
    slots = [rows, swap(rows, "blk", blocks, 1)]
    current = rows
    for _ in range(blocks // 2 - 1):
        pairs = [(i, i + step) for i in range(blocks) if 0 <= i + step < blocks]
        current = lax.ppermute(current, "blk", pairs)
        slots += [current, swap(current, "blk", blocks, 1)]
    return slots


def gather_rows(rows, core):
    half = rows.shape[0] // 2
    own = lax.all_gather(
        lax.dynamic_slice_in_dim(rows, core * half, half, 0), "blk", axis=0, tiled=True
    )
    return own, swap(own, "tp", 4, 1)


WHOLE = pl.BlockSpec(memory_space=pltpu.VMEM)
SCALARS = pl.BlockSpec(memory_space=pltpu.SMEM)


def head_rows(ref, head, group, tokens):
    parts = []
    for member in range(group):
        lane = (head * group + member) * HEAD_SIZE
        parts.append(ref[:tokens, lane : lane + HEAD_SIZE])
    return jnp.concatenate(parts, axis=0)


def wide(row, group):
    return jnp.concatenate([row] * group, axis=1)


def seen_mask(first_row, key_start, query_start, tokens, group):
    shape = (tokens, tokens)
    key = key_start + lax.broadcasted_iota(jnp.int32, shape, 0)
    query = query_start + lax.broadcasted_iota(jnp.int32, shape, 1)
    seen = (key <= query) & (key >= first_row)
    return jnp.concatenate([seen.astype(F32)] * group, axis=1) > 0.5


def earlier_block(own, slot):
    place = own // 2 - slot // 2
    block = place * 2 + jnp.bitwise_xor(lax.rem(own, 2), slot % 2)
    return block, (place >= 0) & (block <= own)


def later_block(own, slot, blocks):
    place = own // 2 + slot // 2
    block = place * 2 + jnp.bitwise_xor(lax.rem(own, 2), slot % 2)
    return block, (place < blocks // 2) & (block >= own)


def attend_kernel(blocks, heads, group, scalars, firsts, query, *refs):
    pairs = refs[:blocks]
    mixed_ref, log_ref, scores, top, total = refs[blocks:]
    tokens = query.shape[0]
    own = scalars[0]
    first_row = firsts[pl.ds(own, 1), :]
    for head in range(heads):
        rows = head_rows(query, head, group, tokens)
        top[...] = jnp.full_like(top, NEGATIVE)
        for slot in range(blocks):
            block, valid = earlier_block(own, slot)

            @pl.when(valid)
            def _():
                keys = pairs[slot][:, head * HEAD_SIZE : (head + 1) * HEAD_SIZE]
                found = product_right(keys, rows) * SCALE
                seen = seen_mask(first_row, block * tokens, own * tokens, tokens, group)
                found = jnp.where(seen, found, NEGATIVE)
                scores[slot] = found
                top[...] = jnp.maximum(top[...], jnp.max(found, axis=0, keepdims=True))

        highest = top[0:1, :]
        total[...] = jnp.zeros_like(total)
        top[...] = jnp.zeros_like(top)
        for slot in range(blocks):
            block, valid = earlier_block(own, slot)

            @pl.when(valid)
            def _():
                lane = (heads + head) * HEAD_SIZE
                values = pairs[slot][:, lane : lane + HEAD_SIZE]
                weights = jnp.exp(scores[slot] - highest)
                top[...] += jnp.sum(weights, axis=0, keepdims=True)
                total[...] += product_left(values, weights.astype(BF16))

        mass = top[0:1, :]
        result = (total[...] / mass).T
        logs = highest + jnp.log(mass)
        for member in range(group):
            lane = (head * group + member) * HEAD_SIZE
            part = slice(member * tokens, (member + 1) * tokens)
            mixed_ref[:, lane : lane + HEAD_SIZE] = result[part].astype(BF16)
            log_ref[head * group + member : head * group + member + 1, :] = logs[:, part]


def attend(query, pairs, firsts, own, heads, group):
    tokens, width = query.shape
    blocks = len(pairs)
    return pl.pallas_call(
        functools.partial(attend_kernel, blocks, heads, group),
        out_shape=(
            jax.ShapeDtypeStruct((tokens, width), BF16),
            jax.ShapeDtypeStruct((heads * group, tokens), F32),
        ),
        in_specs=[SCALARS] + [WHOLE] * (2 + blocks),
        out_specs=(WHOLE, WHOLE),
        scratch_shapes=[
            pltpu.VMEM((blocks, tokens, group * tokens), F32),
            pltpu.VMEM((8, group * tokens), F32),
            pltpu.VMEM((HEAD_SIZE, group * tokens), F32),
        ],
        compiler_params=pltpu.CompilerParams(vmem_limit_bytes=48 * 1024 * 1024),
        name="attend",
    )(own.reshape(1), firsts, query, *pairs)


def query_back_kernel(
    blocks, heads, group, scalars, firsts, query, back, logs, delta, cosine, sine, *refs
):
    pairs = refs[:blocks]
    out_ref, total = refs[blocks:]
    tokens = query.shape[0]
    own = scalars[0]
    first_row = firsts[pl.ds(own, 1), :]
    for head in range(heads):
        rows = head_rows(query, head, group, tokens)
        back_rows = head_rows(back, head, group, tokens)
        members = range(head * group, (head + 1) * group)
        log_row = jnp.concatenate([logs[m : m + 1, :] for m in members], axis=1)
        delta_row = jnp.concatenate([delta[m : m + 1, :] for m in members], axis=1)
        total[...] = jnp.zeros_like(total)
        for slot in range(blocks):
            block, valid = earlier_block(own, slot)

            @pl.when(valid)
            def _():
                lane = head * HEAD_SIZE
                keys = pairs[slot][:, lane : lane + HEAD_SIZE]
                lane = (heads + head) * HEAD_SIZE
                values = pairs[slot][:, lane : lane + HEAD_SIZE]
                found = product_right(keys, rows) * SCALE - log_row
                seen = seen_mask(first_row, block * tokens, own * tokens, tokens, group)
                probs = jnp.exp(jnp.where(seen, found, NEGATIVE))
                back_probs = product_right(values, back_rows)
                back_scores = (probs * (back_probs - delta_row) * SCALE).astype(BF16)
                total[...] += product_left(keys, back_scores)

        result = total[...].T
        for member in range(group):
            lane = (head * group + member) * HEAD_SIZE
            part = result[member * tokens : (member + 1) * tokens]
            out_ref[:, lane : lane + HEAD_SIZE] = unrotate(part, cosine[...], sine[...]).astype(
                BF16
            )


def query_back(query, back, logs, delta, pairs, firsts, own, tables, heads, group):
    tokens, width = query.shape
    blocks = len(pairs)
    return pl.pallas_call(
        functools.partial(query_back_kernel, blocks, heads, group),
        out_shape=jax.ShapeDtypeStruct((tokens, width), BF16),
        in_specs=[SCALARS] + [WHOLE] * (7 + blocks),
        out_specs=WHOLE,
        scratch_shapes=[pltpu.VMEM((HEAD_SIZE, group * tokens), F32)],
        compiler_params=pltpu.CompilerParams(vmem_limit_bytes=48 * 1024 * 1024),
        name="query_back",
    )(own.reshape(1), firsts, query, back, logs, delta, *tables, *pairs)


def split_rows(rows):
    high = rows.astype(BF16)
    return high, (rows - high.astype(F32)).astype(BF16)


def pack_rows(rows, extra):
    high, low = split_rows(extra)
    count, tokens = extra.shape
    both = jnp.concatenate([high, low], axis=0)
    both = jnp.pad(both, ((0, 16 - 2 * count), (0, rows.shape[1] - tokens)))
    return jnp.concatenate([rows, both], axis=0)


def pair_back_kernel(blocks, heads, group, scalars, firsts, pairs, cosine, sine, *refs):
    queries, backs = refs[:blocks], refs[blocks : 2 * blocks]
    out_ref, key_total, value_total = refs[2 * blocks :]
    tokens = pairs.shape[0]
    own = scalars[0]
    count = heads * group
    for head in range(heads):
        lane = head * HEAD_SIZE
        keys = pairs[:, lane : lane + HEAD_SIZE]
        value_lane = (heads + head) * HEAD_SIZE
        values = pairs[:, value_lane : value_lane + HEAD_SIZE]
        key_total[...] = jnp.zeros_like(key_total)
        value_total[...] = jnp.zeros_like(value_total)
        for slot in range(blocks):
            block, valid = later_block(own, slot, blocks)

            @pl.when(valid)
            def _():
                rows = head_rows(queries[slot], head, group, tokens)
                back_rows = head_rows(backs[slot], head, group, tokens)

                def extra(ref):
                    below = ref[tokens : tokens + 16, :tokens].astype(F32)
                    return jnp.concatenate(
                        [
                            below[m : m + 1, :] + below[count + m : count + m + 1, :]
                            for m in range(head * group, (head + 1) * group)
                        ],
                        axis=1,
                    )

                log_row = extra(queries[slot])
                delta_row = extra(backs[slot])
                first_row = firsts[pl.ds(block, 1), :]
                found = product_right(keys, rows) * SCALE - log_row
                seen = seen_mask(first_row, own * tokens, block * tokens, tokens, group)
                probs = jnp.exp(jnp.where(seen, found, NEGATIVE))
                back_probs = product_right(values, back_rows)
                back_scores = (probs * (back_probs - delta_row) * SCALE).astype(BF16)
                key_total[...] += product(back_scores, rows)
                value_total[...] += product(probs.astype(BF16), back_rows)

        out_ref[:, lane : lane + HEAD_SIZE] = unrotate(
            key_total[...], cosine[...], sine[...]
        ).astype(BF16)
        out_ref[:, value_lane : value_lane + HEAD_SIZE] = value_total[...].astype(BF16)


def pair_back(pairs, queries, backs, firsts, own, tables, heads, group):
    tokens, width = pairs.shape
    blocks = len(queries)
    return pl.pallas_call(
        functools.partial(pair_back_kernel, blocks, heads, group),
        out_shape=jax.ShapeDtypeStruct((tokens, width), BF16),
        in_specs=[SCALARS] + [WHOLE] * (4 + 2 * blocks),
        out_specs=WHOLE,
        scratch_shapes=[pltpu.VMEM((tokens, HEAD_SIZE), F32)] * 2,
        compiler_params=pltpu.CompilerParams(vmem_limit_bytes=48 * 1024 * 1024),
        name="pair_back",
    )(own.reshape(1), firsts, pairs, *tables, *queries, *backs)


def feedforward_weights_kernel(
    started, rows, incoming, rows_part, incoming_part, gate_weight, up_weight, down_weight, *refs
):
    before = refs[:3] if started else None
    gate_out, up_out, down_out = refs[-3:]

    @pl.when(pl.program_id(0) == 0)
    def _():
        if started:
            gate_out[...] = before[0][...]
            up_out[...] = before[1][...]
            down_out[...] = before[2][...]
        else:
            gate_out[...] = jnp.zeros_like(gate_out)
            up_out[...] = jnp.zeros_like(up_out)
            down_out[...] = jnp.zeros_like(down_out)

    gate = product(rows[...], gate_weight[...])
    up = product(rows[...], up_weight[...])
    back_inner = product_right(incoming[...], down_weight[...])
    inner, back_gate, back_up = swiglu_back(gate, up, back_inner)
    gate_out[...] += product_left(rows_part[...], back_gate)
    up_out[...] += product_left(rows_part[...], back_up)
    down_out[...] += product_left(inner, incoming_part[...])


def feedforward_weights(rows, incoming, place, blocks, weights, before=None):
    gate_weight, up_weight, down_weight = weights
    total, width = rows.shape
    hidden = gate_weight.shape[1]
    part = width // blocks
    rows_part = lax.dynamic_slice_in_dim(rows, place * part, part, 1)
    incoming_part = lax.dynamic_slice_in_dim(incoming, place * part, part, 1)
    step = 256
    once = pl.Buffered(1)
    fixed = lambda shape: pl.BlockSpec(shape, lambda i: (0, 0), pipeline_mode=once)
    moving = lambda columns: pl.BlockSpec((step, columns), lambda i: (i, 0))
    shapes = [(part, hidden), (part, hidden), (hidden, part)]
    started = before is not None
    return pl.pallas_call(
        functools.partial(feedforward_weights_kernel, started),
        grid=(total // step,),
        out_shape=tuple(jax.ShapeDtypeStruct(shape, F32) for shape in shapes),
        in_specs=[
            moving(width),
            moving(width),
            moving(part),
            moving(part),
            fixed((width, hidden)),
            fixed((width, hidden)),
            fixed((hidden, width)),
        ]
        + ([fixed(shape) for shape in shapes] if started else []),
        out_specs=tuple(fixed(shape) for shape in shapes),
        compiler_params=pltpu.CompilerParams(vmem_limit_bytes=48 * 1024 * 1024),
        cost_estimate=pl.CostEstimate(
            flops=6 * total * width * hidden, bytes_accessed=16000000, transcendentals=0
        ),
        name="feedforward_weights",
    )(
        rows,
        incoming,
        rows_part,
        incoming_part,
        gate_weight,
        up_weight,
        down_weight,
        *(before if started else ()),
    )


def swiglu_back(gate, up, back_inner):
    chance = 1.0 / (1.0 + jnp.exp(-gate))
    silu = gate * chance
    inner = (silu * up).astype(BF16)
    back_gate = (back_inner * up * (chance + silu * (1.0 - chance))).astype(BF16)
    back_up = (back_inner * silu).astype(BF16)
    return inner, back_gate, back_up


class Layout:
    def __init__(self, lengths, tokens):
        self.tokens = tokens
        self.blocks = lax.axis_size("blk")
        self.own = lax.axis_index("blk")
        self.core = lax.rem(lax.axis_index("tp"), 2)
        index = jnp.arange(tokens * self.blocks, dtype=jnp.int32)
        firsts = first_tokens(lengths, index)
        mine = lax.dynamic_slice_in_dim(index - firsts, self.own * tokens, tokens, 0)
        self.tables = rotary_tables(mine)
        self.firsts = firsts.reshape(self.blocks, tokens)


def attention_front(inputs, weights, layout):
    gain, query_weight, key_weight, value_weight, projection = weights[:5]
    tokens = layout.tokens
    heads = key_weight.shape[1] // HEAD_SIZE
    group = query_weight.shape[1] // HEAD_SIZE // heads
    cosine, sine = (table[:, None, :] for table in layout.tables)
    normed = rms_norm(inputs, gain).astype(BF16)

    def turned(weight):
        rows = product(normed, weight).reshape(tokens, -1, HEAD_SIZE)
        return rotate(rows, cosine, sine).astype(BF16).reshape(tokens, -1)

    query = turned(query_weight)
    pair = jnp.concatenate(
        [turned(key_weight), product(normed, value_weight).astype(BF16)], axis=1
    )
    pairs = line_gather(pair, layout.blocks, 2)
    mixed, logs = attend(query, pairs, layout.firsts, layout.own, heads, group)
    hidden = inputs + sum_tp(product(mixed, projection), layout.core).astype(F32)
    queries = line_gather(pack_rows(query, logs), layout.blocks, -2)
    return hidden, (normed, query, pairs, logs, mixed, queries, heads, group)


def feedforward_parts(inner_in, weights):
    gate = product(inner_in, weights[6])
    up = product(inner_in, weights[7])
    return gate, up


def attention_back(inputs, hidden, incoming, back_in, weights, layout, saved):
    gain, query_weight, key_weight, value_weight, projection = weights[:5]
    normed, query, pairs, logs, mixed, queries, heads, group = saved
    tokens = layout.tokens
    back_norm, gradient_feedforward_gain = rms_norm_back(hidden, weights[5], back_in)
    back_hidden = incoming + back_norm
    low = back_hidden.astype(BF16)
    back_mixed = product_right(low, projection).astype(BF16)
    delta = jnp.sum(
        (back_mixed.astype(F32) * mixed.astype(F32)).reshape(tokens, -1, HEAD_SIZE), axis=-1
    ).T
    backs = line_gather(pack_rows(back_mixed, delta), layout.blocks, -2)
    back_query = query_back(
        query, back_mixed, logs, delta, pairs, layout.firsts, layout.own, layout.tables, heads, group
    )
    back_pair = pair_back(
        pairs[0], queries, backs, layout.firsts, layout.own, layout.tables, heads, group
    )
    width = heads * HEAD_SIZE
    partial = (
        product_right(back_query, query_weight)
        + product_right(back_pair[:, :width], key_weight)
        + product_right(back_pair[:, width:], value_weight)
    )
    back_normed = sum_tp(partial, layout.core).astype(F32)
    back_inputs, gradient_attention_gain = rms_norm_back(inputs, gain, back_normed)
    back_all = jnp.concatenate([back_query, back_pair], axis=1)
    gradient_attention = product_left(normed, back_all).astype(BF16)
    gradient_projection = product_left(low, mixed).astype(BF16)
    share = lax.psum_scatter(
        jnp.concatenate([gradient_attention, gradient_projection], axis=1),
        "blk",
        scatter_dimension=0,
        tiled=True,
    ).astype(F32)
    ends = [0]
    for part in (query_weight.shape[1], width, width, query_weight.shape[1]):
        ends.append(ends[-1] + part)
    pieces = [share[:, ends[i] : ends[i + 1]] for i in range(4)]
    pieces[3] = pieces[3].T
    return (
        back_inputs + back_hidden,
        tuple(pieces),
        (gradient_attention_gain, gradient_feedforward_gain),
    )


def feedforward_share(own_rows, own_incoming, weights, layout):
    gradients = None
    for rows, incoming in zip(own_rows, own_incoming):
        gradients = feedforward_weights(
            rows, incoming, layout.own, layout.blocks, weights[6:9], gradients
        )
    return gradients


def body(tokens, lengths, *rest):
    first, second, cotangent = rest[:9], rest[9:18], rest[18]
    layout = Layout(lengths, tokens.shape[0])
    core = layout.core
    cotangents = gather_rows(cotangent, core)
    inputs_one = tokens.astype(F32)
    hidden_one, saved_one = attention_front(inputs_one, first, layout)
    inner_in_one = rms_norm(hidden_one, first[5]).astype(BF16)
    gate, up = feedforward_parts(inner_in_one, first)
    inner = (jax.nn.silu(gate) * up).astype(BF16)
    inputs_two = hidden_one + sum_tp(product(inner, first[8]), core).astype(F32)
    inner_ins_one = gather_rows(inner_in_one, core)
    hidden_two, saved_two = attention_front(inputs_two, second, layout)
    inner_in_two = rms_norm(hidden_two, second[5]).astype(BF16)
    inner_ins_two = gather_rows(inner_in_two, core)

    def back_feedforward(inner_in, incoming, weights, forward):
        gate, up = feedforward_parts(inner_in, weights)
        back_inner = product_right(incoming, weights[8])
        inner, back_gate, back_up = swiglu_back(gate, up, back_inner)
        partial = product_right(back_gate, weights[6]) + product_right(back_up, weights[7])
        back_in = sum_tp(partial, core).astype(F32)
        if not forward:
            return back_in, None
        return back_in, sum_tp(product(inner, weights[8]), core).astype(F32)

    back_in, last = back_feedforward(inner_in_two, cotangent, second, True)
    result = (hidden_two + last).astype(BF16)
    back_two, shares_two, gains_two = attention_back(
        inputs_two, hidden_two, cotangent.astype(F32), back_in, second, layout, saved_two
    )
    low_two = back_two.astype(BF16)
    lows = gather_rows(low_two, core)
    back_in, _ = back_feedforward(inner_in_one, low_two, first, False)
    back_one, shares_one, gains_one = attention_back(
        inputs_one, hidden_one, back_two, back_in, first, layout, saved_one
    )
    feed_two = feedforward_share(inner_ins_two, cotangents, second, layout)
    feed_one = feedforward_share(inner_ins_one, lows, first, layout)
    gains = jnp.stack([gains_one[0], gains_one[1], gains_two[0], gains_two[1]], axis=0)
    gains = gains.reshape(4, layout.blocks, -1).transpose(1, 0, 2)
    gains = jnp.sum(lax.all_to_all(gains, "blk", 0, 0, tiled=True), axis=0)
    return (
        (result, back_one)
        + (gains[0],)
        + shares_one
        + (gains[1],)
        + feed_one
        + (gains[2],)
        + shares_two
        + (gains[3],)
        + feed_two
    )


def solution(mesh):
    rows, columns = P("tp", None), P(None, "tp")
    layer = (P(), columns, columns, columns, rows, P(), columns, columns, rows)
    in_specs = (P("blk", None), P()) + layer + layer + (P("blk", None),)
    wide_out, tall_out = P("blk", "tp"), P("tp", "blk")
    layer_out = (
        P("blk"),
        wide_out,
        wide_out,
        wide_out,
        tall_out,
        P("blk"),
        wide_out,
        wide_out,
        tall_out,
    )
    out_specs = (P("blk", None), P("blk", None)) + layer_out + layer_out
    return jax.shard_map(body, mesh=mesh, in_specs=in_specs, out_specs=out_specs, check_vma=False)
```

time: 1670 us -> 602 us (0.36)
  waiting for transfers between devices: 1320 us -> 207 us
  Pallas kernels: 0 us -> 108 us
  matrix products: 143 us -> 36.8 us
  starting transfers between devices: 2.1 us -> 93.6 us
  other arithmetic: 102 us -> 43.5 us
  local copies, waits for them, and re-layouts: 31.6 us -> 86.2 us
  blocking collectives: 37.3 us -> 0 us
    reduce_scatter x16 -> x0, waiting for transfers between devices: 991 us -> none  [the longest x2 91.4 us: layer_back(): lax.psum_scatter(terms.astype(jnp.bfloat16), 'blk', scatter_dimension=0,...]
    psum x7 -> x0, waiting for transfers between devices: 246 us -> none  [the longest x3 103 us: layer_back(): lax.psum(partial_value.astype(jnp.bfloat16), 'tp').astype(jnp.float32)]
    ppermute x0 -> x70, waiting for transfers between devices: none -> 204 us  [the longest x52 124 us: swap(): return lax.ppermute(rows, axis, [(i, i ^ bit) for i in range(size)])]
    pallas_call x0 -> x10, Pallas kernels: none -> 108 us  [the longest x4 71.9 us: feedforward_weights(): pl.pallas_call(functools.partial(feedforward_weights_kernel, started), gr...]
    ppermute x0 -> x70, starting transfers between devices: none -> 89.2 us  [the longest x18 46.5 us: line_gather(): current = lax.ppermute(current, 'blk', pairs)]
    all_gather x2 -> x4, waiting for transfers between devices: 85.2 us -> 0.08 us  [gather_rows(): lax.all_gather(lax.dynamic_slice_in_dim(rows, core * half, half, 0), 'blk...]
    dot_general x28 -> x14, matrix products: 76.9 us -> 18.4 us  [product(): return jnp.dot(left, right, preferred_element_type=F32)]
    dot_general x14 -> x4, matrix products: 45.2 us -> 3.95 us  [product_left(): lax.dot_general(left, right, (((0,), (0,)), ((), ())), preferred_element_...]
  transfers between devices with their start and end apart: 25 -> 77, of which waited for: 25 -> 45; matrix products, arithmetic and copies ran while one was open for 6% -> 19% of each run, Pallas kernels for 0% -> 18%
where the time goes in v1:
time: 602 us; the launch traced here: 592 us
  waiting for transfers between devices  207 us (34%)
  Pallas kernels  108 us (18%)
  starting transfers between devices  93.6 us (16%)
  local copies, waits for them, and re-layouts  86.2 us (14%)
  other arithmetic  43.5 us (7%)
  matrix products  36.8 us (6%)
  between operations  17 us (3%)
    ppermute x52, waiting for transfers between devices, swap(): return lax.ppermute(rows, axis, [(i, i ^ bit) for i in range(size)])  124 us
    ppermute x18, waiting for transfers between devices, line_gather(): current = lax.ppermute(current, 'blk', pairs)  79.5 us
    pallas_call x4, Pallas kernels, feedforward_weights(): pl.pallas_call(functools.partial(feedforward_weights_kernel, started), gr...  71.9 us
    unnamed x278, local copies, waits for them, and re-layouts  54.9 us
    ppermute x18, starting transfers between devices, line_gather(): current = lax.ppermute(current, 'blk', pairs)  46.5 us
    ppermute x52, starting transfers between devices, swap(): return lax.ppermute(rows, axis, [(i, i ^ bit) for i in range(size)])  42.7 us
    pallas_call x2, Pallas kernels, pair_back(): pl.pallas_call(functools.partial(pair_back_kernel, blocks, heads, group),...  25.2 us
    dot_general x14, matrix products, product(): return jnp.dot(left, right, preferred_element_type=F32)  18.4 us
  transfers between devices with their start and end apart: 77, of which 45 were waited for; matrix products, arithmetic and copies ran while one was open for 19% of the time, Pallas kernels for 18%

profile of v1, /device:TPU:0, one launch (start us, length us, event | category | flops | bytes accessed | tf_op | source)
XLA Modules:
  0.0 591.6 jit_solution(15407570035249358171)
XLA Ops:
  16.7 3.0 collective-permute-start
  19.8 3.5 collective-permute-start.1
  27.1 4.4 collective-permute-start.3
  31.5 3.1 collective-permute-done.3.refs_4_
  34.6 4.4 collective-permute-start.5
  44.0 4.1 collective-permute-done.2.refs_3_
  61.0 9.7 %collective-permute-done.8 = bf16[128,1536]{1,0:T(8,128)(2,1)S(1)} collective-permute-done((bf16[128,1536]{1,0:T(8,128)(2,1)S(1)}, bf16[128,1536]{1,0:T(8,128)(2,1)S(1)}, u32[]{:S(2)}, u32[]{:S(2)}) %collective-permute-start.8) | collective-permute-done | bytes 393248 | tf_op jit(solution)/shard_map/ppermute | solution.py:72
  85.9 9.7 %collective-permute-done.11 = bf16[128,1536]{1,0:T(8,128)(2,1)S(1)} collective-permute-done((bf16[128,1536]{1,0:T(8,128)(2,1)S(1)}, bf16[128,1536]{1,0:T(8,128)(2,1)S(1)}, u32[]{:S(2)}, u32[]{:S(2)}) %collective-permute-start.11) | collective-permute-done | bytes 393248 | tf_op jit(solution)/shard_map/ppermute | solution.py:72
  110.3 5.7 collective-permute-start.14
  116.0 2.8 fusion.109
  120.7 4.3 collective-permute-done.14.refs_2_
  125.0 7.7 %collective-permute-start.16 = (bf16[256,384]{1,0:T(8,128)(2,1)S(1)}, bf16[256,384]{1,0:T(8,128)(2,1)S(1)}, u32[]{:S(2)}, u32[]{:S(2)}) collective-permute-start(bf16[256,384]{1,0:T(8,128)(2,1)S(1)} %collective-permute-done.14.refs_2_), channel_id=1, source_target_pairs={{0,8},{4,12},{8,16},{12,20},{16,24},{20,28},{1,9},{5,13},{9,17},{1... | collective-permute-start | bytes 589832 | tf_op jit(solution)/shard_map/ppermute | solution.py:92
  135.9 5.4 collective-permute-start.18
  151.1 4.8 collective-permute-done.15.refs_3_
  155.9 8.4 %collective-permute-done.17.refs_5_ = bf16[256,384]{1,0:T(8,128)(2,1)S(1)} collective-permute-done((bf16[256,384]{1,0:T(8,128)(2,1)S(1)}, bf16[256,384]{1,0:T(8,128)(2,1)S(1)}, u32[]{:S(2)}, u32[]{:S(2)}) %collective-permute-start.17) | collective-permute-done | bytes 196640 | tf_op jit(solution)/shard_map/ppermute | solution.py:72
  164.4 4.6 collective-permute-done.19.refs_7_
  169.9 3.1 attend.3
  180.1 6.9 %collective-permute-done.21 = bf16[128,1536]{1,0:T(8,128)(2,1)} collective-permute-done((bf16[128,1536]{1,0:T(8,128)(2,1)S(1)}, bf16[128,1536]{1,0:T(8,128)(2,1)}, u32[]{:S(2)}, u32[]{:S(2)}) %collective-permute-start.21) | collective-permute-done | bytes 393248 | tf_op jit(solution)/shard_map/ppermute | solution.py:72
  202.9 8.9 %collective-permute-done.27 = bf16[128,1536]{1,0:T(8,128)(2,1)S(1)} collective-permute-done((bf16[128,1536]{1,0:T(8,128)(2,1)S(1)}, bf16[128,1536]{1,0:T(8,128)(2,1)S(1)}, u32[]{:S(2)}, u32[]{:S(2)}) %collective-permute-start.27) | collective-permute-done | bytes 393248 | tf_op jit(solution)/shard_map/ppermute | solution.py:72
  212.1 7.7 %collective-permute-done.24 = bf16[128,1536]{1,0:T(8,128)(2,1)S(1)} collective-permute-done((bf16[128,1536]{1,0:T(8,128)(2,1)S(1)}, bf16[128,1536]{1,0:T(8,128)(2,1)S(1)}, u32[]{:S(2)}, u32[]{:S(2)}) %collective-permute-start.24) | collective-permute-done | bytes 393248 | tf_op jit(solution)/shard_map/ppermute | solution.py:72
  230.2 16.9 %collective-permute-done.37.refs_10_ = bf16[272,384]{1,0:T(8,128)(2,1)S(1)} collective-permute-done((bf16[272,384]{1,0:T(8,128)(2,1)S(1)}, bf16[272,384]{1,0:T(8,128)(2,1)S(1)}, u32[]{:S(2)}, u32[]{:S(2)}) %collective-permute-start.37) | collective-permute-done | bytes 208928 | tf_op jit(solution)/shard_map/ppermute | solution.py:92
  249.1 3.3 collective-permute-start.29
  252.4 4.8 collective-permute-done.32.refs_4_
  265.0 3.9 collective-permute-done.34.refs_6_
  275.9 3.1 query_back.2
  279.1 5.7 collective-permute-done.36.refs_9_
  284.7 5.7 collective-permute-done.38.refs_11_
  290.4 3.5 collective-permute-done.40.refs_13_
  297.1 12.5 %pair_back.2 = bf16[256,384]{1,0:T(8,128)(2,1)S(1)} custom-call(s32[1]{0:T(128)} %bitcast.scalars, s32[8,256]{1,0:T(8,128)S(1)} %reshape.268.firsts, bf16[256,384]{1,0:T(8,128)(2,1)S(1)} %pad_maximum_fusion.12.refs_0_.pairs, f32[256,96]{1,0:T(8,128)S(1)} %get-tuple-element.196.cosine, f32[256,96]{1,0:T(8,128)S(1)} %get-tuple-element.197.sine, ...), custom_call_target="tpu_custom_call" | custom-call | tf_op jit(solution)/shard_map/pair_back/pallas_call | solution.py:325
  316.1 9.7 %collective-permute-done.44 = bf16[128,1536]{1,0:T(8,128)(2,1)S(1)} collective-permute-done((bf16[128,1536]{1,0:T(8,128)(2,1)S(1)}, bf16[128,1536]{1,0:T(8,128)(2,1)S(1)}, u32[]{:S(2)}, u32[]{:S(2)}) %collective-permute-start.44) | collective-permute-done | bytes 393248 | tf_op jit(solution)/shard_map/ppermute | solution.py:72
  332.3 3.3 fusion.114
  345.5 5.8 copy.179
  356.5 8.2 %collective-permute-done.50.refs_2_ = bf16[272,384]{1,0:T(8,128)(2,1)S(1)} collective-permute-done((bf16[272,384]{1,0:T(8,128)(2,1)S(1)}, bf16[272,384]{1,0:T(8,128)(2,1)S(1)}, u32[]{:S(2)}, u32[]{:S(2)}) %collective-permute-start.50) | collective-permute-done | bytes 208928 | tf_op jit(solution)/shard_map/ppermute | solution.py:92
  373.3 10.5 %collective-permute-done.52.refs_4_ = bf16[272,384]{1,0:T(8,128)(2,1)} collective-permute-done((bf16[272,384]{1,0:T(8,128)(2,1)S(1)}, bf16[272,384]{1,0:T(8,128)(2,1)}, u32[]{:S(2)}, u32[]{:S(2)}) %collective-permute-start.52) | collective-permute-done | bytes 208928 | tf_op jit(solution)/shard_map/ppermute | solution.py:92
  385.1 11.4 %collective-permute-done.57.refs_10_ = bf16[272,384]{1,0:T(8,128)(2,1)} collective-permute-done((bf16[272,384]{1,0:T(8,128)(2,1)S(1)}, bf16[272,384]{1,0:T(8,128)(2,1)}, u32[]{:S(2)}, u32[]{:S(2)}) %collective-permute-start.57) | collective-permute-done | bytes 208928 | tf_op jit(solution)/shard_map/ppermute | solution.py:92
  400.6 4.0 collective-permute-done.54.refs_6_
  426.3 3.4 collective-permute-done.58.refs_11_
  429.7 4.9 collective-permute-done.60.refs_13_
  434.6 4.5 collective-permute-done.62.refs_15_
  439.1 12.7 %pair_back.3 = bf16[256,384]{1,0:T(8,128)(2,1)S(1)} custom-call(s32[1]{0:T(128)} %bitcast.scalars, s32[8,256]{1,0:T(8,128)S(1)} %reshape.268.firsts, bf16[256,384]{1,0:T(8,128)(2,1)S(1)} %pad_maximum_fusion.11.refs_0_.pairs, f32[256,96]{1,0:T(8,128)S(1)} %get-tuple-element.196.cosine, f32[256,96]{1,0:T(8,128)S(1)} %get-tuple-element.197.sine, ...), custom_call_target="tpu_custom_call" | custom-call | tf_op jit(solution)/shard_map/pair_back/pallas_call | solution.py:325
  462.6 5.8 copy.177
  473.2 17.7 %feedforward_weights.6 = (f32[192,1024]{1,0:T(8,128)S(1)}, f32[192,1024]{1,0:T(8,128)S(1)}, f32[1024,192]{1,0:T(8,128)S(1)}) custom-call(bf16[1024,1536]{1,0:T(8,128)(2,1)} %all-gather.9.cloned.1.call-done.rows, bf16[1024,1536]{1,0:T(8,128)(2,1)} %all-gather.11.cloned.1.call-done.incoming, bf16[1024,192]{1,0:T(8,128)(2,1)S(1)} %constant_dynamic-slice_fusion.rows_part, ...), custom_call_target="tpu_custom_call" | custom-call | flops 9663676416 | bytes 16000000 | tf_op jit(solution)/shard_map/feedforward_weights/pallas_call | solution.py:375
  493.3 3.6 all-to-all-start
  497.1 3.2 fusion.10
  500.2 3.3 all-to-all-done
  507.8 18.3 %feedforward_weights.7 = (f32[192,1024]{1,0:T(8,128)}, f32[192,1024]{1,0:T(8,128)}, f32[1024,192]{1,0:T(8,128)S(1)}) custom-call(bf16[1024,1536]{1,0:T(8,128)(2,1)} %collective-permute-done.68.rows, bf16[1024,1536]{1,0:T(8,128)(2,1)} %collective-permute-done.69.incoming, bf16[1024,192]{1,0:T(8,128)(2,1)S(1)} %constant_dynamic-slice_fusion.2.rows_part, ...), custom_call_target="tpu_custom_call" | custom-call | flops 9663676416 | bytes 16000000 | tf_op jit(solution)/shard_map/feedforward_weights/pallas_call | solution.py:375
  528.7 17.5 %feedforward_weights.4 = (f32[192,1024]{1,0:T(8,128)S(1)}, f32[192,1024]{1,0:T(8,128)S(1)}, f32[1024,192]{1,0:T(8,128)S(1)}) custom-call(bf16[1024,1536]{1,0:T(8,128)(2,1)} %all-gather.5.cloned.1.call-done.rows, bf16[1024,1536]{1,0:T(8,128)(2,1)} %all-gather.7.cloned.1.call-done.incoming, bf16[1024,192]{1,0:T(8,128)(2,1)S(1)} %copy-done.25, ...), custom_call_target="tpu_custom_call" | custom-call | flops 9663676416 | bytes 16000000 | tf_op jit(solution)/shard_map/feedforward_weights/pallas_call | solution.py:375
  558.4 18.3 %feedforward_weights.5 = (f32[192,1024]{1,0:T(8,128)}, f32[192,1024]{1,0:T(8,128)}, f32[1024,192]{1,0:T(8,128)S(1)}) custom-call(bf16[1024,1536]{1,0:T(8,128)(2,1)} %collective-permute-done.66.rows, bf16[1024,1536]{1,0:T(8,128)(2,1)} %collective-permute-done.67.incoming, bf16[1024,192]{1,0:T(8,128)(2,1)S(1)} %constant_dynamic-slice_fusion.8.rows_part, ...), custom_call_target="tpu_custom_call" | custom-call | flops 9663676416 | bytes 16000000 | tf_op jit(solution)/shard_map/feedforward_weights/pallas_call | solution.py:375
  (571 shorter events, 236.8 us)
Async XLA Ops:
  7.2 358.8 %all-gather.11.cloned.1.call-start = ((), (), s32[]{:S(2)}) async-start(), calls=%async_computation.6 | async-start | bytes 3538944 | tf_op jit(solution)/shard_map/all_gather | solution.py:99
  16.7 27.3 %collective-permute-start = (bf16[256,384]{1,0:T(8,128)(2,1)S(1)}, bf16[256,384]{1,0:T(8,128)(2,1)S(1)}, u32[]{:S(2)}, u32[]{:S(2)}) collective-permute-start(bf16[256,384]{1,0:T(8,128)(2,1)S(1)} %pad_maximum_fusion.11.refs_0_.pairs), channel_id=1, source_target_pairs={{0,4},{4,0},{8,12},{12,8},{16,20},{20,16},{24,28},{28,24},{1,5},{5... | collective-permute-start | bytes 589832 | tf_op jit(solution)/shard_map/ppermute | solution.py:72
  59.4 11.2 %collective-permute-start.8 = (bf16[128,1536]{1,0:T(8,128)(2,1)S(1)}, bf16[128,1536]{1,0:T(8,128)(2,1)S(1)}, u32[]{:S(2)}, u32[]{:S(2)}) collective-permute-start(bf16[128,1536]{1,0:T(8,128)(2,1)S(1)} %add_convert_fusion.16), channel_id=1, source_target_pairs={{0,2},{1,3},{2,0},{3,1},{4,6},{5,7},{6,4},{7,5},{8,10},{9,11},{10,... | collective-permute-start | bytes 1179656 | tf_op jit(solution)/shard_map/ppermute | solution.py:72
  84.4 11.2 %collective-permute-start.11 = (bf16[128,1536]{1,0:T(8,128)(2,1)S(1)}, bf16[128,1536]{1,0:T(8,128)(2,1)S(1)}, u32[]{:S(2)}, u32[]{:S(2)}) collective-permute-start(bf16[128,1536]{1,0:T(8,128)(2,1)S(1)} %add_convert_fusion.14), channel_id=1, source_target_pairs={{0,2},{1,3},{2,0},{3,1},{4,6},{5,7},{6,4},{7,5},{8,10},{9,11},{10,... | collective-permute-start | bytes 1179656 | tf_op jit(solution)/shard_map/ppermute | solution.py:72
  97.2 315.4 %all-gather.5.cloned.1.call-start = ((), (), s32[]{:S(2)}) async-start(), calls=%async_computation.3 | async-start | bytes 3538944 | tf_op jit(solution)/shard_map/all_gather | solution.py:99
  108.6 42.5 %collective-permute-start.13 = (bf16[256,384]{1,0:T(8,128)(2,1)S(1)}, bf16[256,384]{1,0:T(8,128)(2,1)S(1)}, u32[]{:S(2)}, u32[]{:S(2)}) collective-permute-start(bf16[256,384]{1,0:T(8,128)(2,1)S(1)} %pad_maximum_fusion.12.refs_0_.pairs), channel_id=1, source_target_pairs={{0,4},{4,0},{8,12},{12,8},{16,20},{20,16},{24,28},{28,24},{1,5},{5... | collective-permute-start | bytes 589832 | tf_op jit(solution)/shard_map/ppermute | solution.py:72
  110.3 14.7 %collective-permute-start.14 = (bf16[256,384]{1,0:T(8,128)(2,1)S(1)}, bf16[256,384]{1,0:T(8,128)(2,1)S(1)}, u32[]{:S(2)}, u32[]{:S(2)}) collective-permute-start(bf16[256,384]{1,0:T(8,128)(2,1)S(1)} %pad_maximum_fusion.12.refs_0_.pairs), channel_id=1, source_target_pairs={{0,8},{4,12},{8,16},{12,20},{16,24},{20,28},{1,9},{5,13},{9,17},{1... | collective-permute-start | bytes 589832 | tf_op jit(solution)/shard_map/ppermute | solution.py:92
  135.9 12.4 %collective-permute-start.18 = (bf16[256,384]{1,0:T(8,128)(2,1)S(1)}, bf16[256,384]{1,0:T(8,128)(2,1)}, u32[]{:S(2)}, u32[]{:S(2)}) collective-permute-start(bf16[256,384]{1,0:T(8,128)(2,1)S(1)} %collective-permute-done.16.refs_4_), channel_id=1, source_target_pairs={{0,8},{4,12},{8,16},{12,20},{16,24},{20,28},{1,9},{5,13},{9,17},{1... | collective-permute-start | bytes 589832 | tf_op jit(solution)/shard_map/ppermute | solution.py:92
  144.0 11.9 %collective-permute-start.15 = (bf16[256,384]{1,0:T(8,128)(2,1)S(1)}, bf16[256,384]{1,0:T(8,128)(2,1)S(1)}, u32[]{:S(2)}, u32[]{:S(2)}) collective-permute-start(bf16[256,384]{1,0:T(8,128)(2,1)S(1)} %collective-permute-done.14.refs_2_), channel_id=1, source_target_pairs={{0,4},{4,0},{8,12},{12,8},{16,20},{20,16},{24,28},{28,24},{1,5},{5... | collective-permute-start | bytes 589832 | tf_op jit(solution)/shard_map/ppermute | solution.py:72
  145.0 19.3 %collective-permute-start.17 = (bf16[256,384]{1,0:T(8,128)(2,1)S(1)}, bf16[256,384]{1,0:T(8,128)(2,1)S(1)}, u32[]{:S(2)}, u32[]{:S(2)}) collective-permute-start(bf16[256,384]{1,0:T(8,128)(2,1)S(1)} %collective-permute-done.16.refs_4_), channel_id=1, source_target_pairs={{0,4},{4,0},{8,12},{12,8},{16,20},{20,16},{24,28},{28,24},{1,5},{5... | collective-permute-start | bytes 589832 | tf_op jit(solution)/shard_map/ppermute | solution.py:72
  148.3 20.7 %collective-permute-start.19 = (bf16[256,384]{1,0:T(8,128)(2,1)}, bf16[256,384]{1,0:T(8,128)(2,1)S(1)}, u32[]{:S(2)}, u32[]{:S(2)}) collective-permute-start(bf16[256,384]{1,0:T(8,128)(2,1)} %collective-permute-done.18.refs_6_), channel_id=1, source_target_pairs={{0,4},{4,0},{8,12},{12,8},{16,20},{20,16},{24,28},{28,24},{1,5},{5... | collective-permute-start | bytes 589832 | tf_op jit(solution)/shard_map/ppermute | solution.py:72
  175.6 11.3 %collective-permute-start.21 = (bf16[128,1536]{1,0:T(8,128)(2,1)S(1)}, bf16[128,1536]{1,0:T(8,128)(2,1)}, u32[]{:S(2)}, u32[]{:S(2)}) collective-permute-start(bf16[128,1536]{1,0:T(8,128)(2,1)S(1)} %add_convert_fusion.12), channel_id=1, source_target_pairs={{0,2},{1,3},{2,0},{3,1},{4,6},{5,7},{6,4},{7,5},{8,10},{9,11},{10,... | collective-permute-start | bytes 1179656 | tf_op jit(solution)/shard_map/ppermute | solution.py:72
  180.0 290.0 %all-gather.9.cloned.1.call-start = ((), (), s32[]{:S(2)}) async-start(), calls=%async_computation.5 | async-start | bytes 3538944 | tf_op jit(solution)/shard_map/all_gather | solution.py:99
  188.2 40.6 %collective-permute-start.30 = (bf16[272,384]{1,0:T(8,128)(2,1)S(1)}, bf16[272,384]{1,0:T(8,128)(2,1)}, u32[]{:S(2)}, u32[]{:S(2)}) collective-permute-start(bf16[272,384]{1,0:T(8,128)(2,1)S(1)} %pad_maximum_fusion.7.refs_0_), channel_id=1, source_target_pairs={{8,0},{12,4},{16,8},{20,12},{24,16},{28,20},{9,1},{13,5},{17,9},{2... | collective-permute-start | bytes 626696 | tf_op jit(solution)/shard_map/ppermute | solution.py:92
  199.9 12.0 %collective-permute-start.27 = (bf16[128,1536]{1,0:T(8,128)(2,1)S(1)}, bf16[128,1536]{1,0:T(8,128)(2,1)S(1)}, u32[]{:S(2)}, u32[]{:S(2)}) collective-permute-start(bf16[128,1536]{1,0:T(8,128)(2,1)S(1)} %add_convert_fusion.8), channel_id=1, source_target_pairs={{0,2},{1,3},{2,0},{3,1},{4,6},{5,7},{6,4},{7,5},{8,10},{9,11},{10,... | collective-permute-start | bytes 1179656 | tf_op jit(solution)/shard_map/ppermute | solution.py:72
  201.5 18.3 %collective-permute-start.24 = (bf16[128,1536]{1,0:T(8,128)(2,1)S(1)}, bf16[128,1536]{1,0:T(8,128)(2,1)S(1)}, u32[]{:S(2)}, u32[]{:S(2)}) collective-permute-start(bf16[128,1536]{1,0:T(8,128)(2,1)S(1)} %add_convert_fusion.10), channel_id=1, source_target_pairs={{0,2},{1,3},{2,0},{3,1},{4,6},{5,7},{6,4},{7,5},{8,10},{9,11},{10,... | collective-permute-start | bytes 1179656 | tf_op jit(solution)/shard_map/ppermute | solution.py:72
  227.6 19.5 %collective-permute-start.37 = (bf16[272,384]{1,0:T(8,128)(2,1)S(1)}, bf16[272,384]{1,0:T(8,128)(2,1)S(1)}, u32[]{:S(2)}, u32[]{:S(2)}) collective-permute-start(bf16[272,384]{1,0:T(8,128)(2,1)S(1)} %pad_maximum_fusion.8.refs_8_), channel_id=1, source_target_pairs={{8,0},{12,4},{16,8},{20,12},{24,16},{28,20},{9,1},{13,5},{17,9},{2... | collective-permute-start | bytes 626696 | tf_op jit(solution)/shard_map/ppermute | solution.py:92
  228.9 28.4 %collective-permute-start.32 = (bf16[272,384]{1,0:T(8,128)(2,1)}, bf16[272,384]{1,0:T(8,128)(2,1)}, u32[]{:S(2)}, u32[]{:S(2)}) collective-permute-start(bf16[272,384]{1,0:T(8,128)(2,1)} %collective-permute-done.30.refs_2_), channel_id=1, source_target_pairs={{8,0},{12,4},{16,8},{20,12},{24,16},{28,20},{9,1},{13,5},{17,9},{2... | collective-permute-start | bytes 626696 | tf_op jit(solution)/shard_map/ppermute | solution.py:92
  247.8 13.9 %collective-permute-start.39 = (bf16[272,384]{1,0:T(8,128)(2,1)S(1)}, bf16[272,384]{1,0:T(8,128)(2,1)}, u32[]{:S(2)}, u32[]{:S(2)}) collective-permute-start(bf16[272,384]{1,0:T(8,128)(2,1)S(1)} %collective-permute-done.37.refs_10_), channel_id=1, source_target_pairs={{8,0},{12,4},{16,8},{20,12},{24,16},{28,20},{9,1},{13,5},{17,9},{2... | collective-permute-start | bytes 626696 | tf_op jit(solution)/shard_map/ppermute | solution.py:92
  249.1 19.9 %collective-permute-start.29 = (bf16[272,384]{1,0:T(8,128)(2,1)S(1)}, bf16[272,384]{1,0:T(8,128)(2,1)}, u32[]{:S(2)}, u32[]{:S(2)}) collective-permute-start(bf16[272,384]{1,0:T(8,128)(2,1)S(1)} %pad_maximum_fusion.7.refs_0_), channel_id=1, source_target_pairs={{0,4},{4,0},{8,12},{12,8},{16,20},{20,16},{24,28},{28,24},{1,5},{5... | collective-permute-start | bytes 626696 | tf_op jit(solution)/shard_map/ppermute | solution.py:72
  252.4 18.6 %collective-permute-start.31 = (bf16[272,384]{1,0:T(8,128)(2,1)}, bf16[272,384]{1,0:T(8,128)(2,1)}, u32[]{:S(2)}, u32[]{:S(2)}) collective-permute-start(bf16[272,384]{1,0:T(8,128)(2,1)} %collective-permute-done.30.refs_2_), channel_id=1, source_target_pairs={{0,4},{4,0},{8,12},{12,8},{16,20},{20,16},{24,28},{28,24},{1,5},{5... | collective-permute-start | bytes 626696 | tf_op jit(solution)/shard_map/ppermute | solution.py:72
  257.2 13.8 %collective-permute-start.33 = (bf16[272,384]{1,0:T(8,128)(2,1)}, bf16[272,384]{1,0:T(8,128)(2,1)}, u32[]{:S(2)}, u32[]{:S(2)}) collective-permute-start(bf16[272,384]{1,0:T(8,128)(2,1)} %collective-permute-done.32.refs_4_), channel_id=1, source_target_pairs={{0,4},{4,0},{8,12},{12,8},{16,20},{20,16},{24,28},{28,24},{1,5},{5... | collective-permute-start | bytes 626696 | tf_op jit(solution)/shard_map/ppermute | solution.py:72
  261.7 11.3 %collective-permute-start.41 = (bf16[272,384]{1,0:T(8,128)(2,1)}, bf16[272,384]{1,0:T(8,128)(2,1)}, u32[]{:S(2)}, u32[]{:S(2)}) collective-permute-start(bf16[272,384]{1,0:T(8,128)(2,1)} %collective-permute-done.39.refs_12_), channel_id=1, source_target_pairs={{8,0},{12,4},{16,8},{20,12},{24,16},{28,20},{9,1},{13,5},{17,9},{2... | collective-permute-start | bytes 626696 | tf_op jit(solution)/shard_map/ppermute | solution.py:92
  264.8 232.2 %all-gather.7.cloned.1.call-start = ((), (), s32[]{:S(2)}) async-start(), calls=%async_computation.4 | async-start | bytes 3538944 | tf_op jit(solution)/shard_map/all_gather | solution.py:99
  269.0 15.7 %collective-permute-start.36 = (bf16[272,384]{1,0:T(8,128)(2,1)S(1)}, bf16[272,384]{1,0:T(8,128)(2,1)S(1)}, u32[]{:S(2)}, u32[]{:S(2)}) collective-permute-start(bf16[272,384]{1,0:T(8,128)(2,1)S(1)} %pad_maximum_fusion.8.refs_8_), channel_id=1, source_target_pairs={{0,4},{4,0},{8,12},{12,8},{16,20},{20,16},{24,28},{28,24},{1,5},{5... | collective-permute-start | bytes 626696 | tf_op jit(solution)/shard_map/ppermute | solution.py:72
  271.0 19.4 %collective-permute-start.38 = (bf16[272,384]{1,0:T(8,128)(2,1)}, bf16[272,384]{1,0:T(8,128)(2,1)S(1)}, u32[]{:S(2)}, u32[]{:S(2)}) collective-permute-start(bf16[272,384]{1,0:T(8,128)(2,1)} %copy-done.32), channel_id=1, source_target_pairs={{0,4},{4,0},{8,12},{12,8},{16,20},{20,16},{24,28},{28,24},{1,5},{5... | collective-permute-start | bytes 626696 | tf_op jit(solution)/shard_map/ppermute | solution.py:72
  271.1 22.8 %collective-permute-start.40 = (bf16[272,384]{1,0:T(8,128)(2,1)}, bf16[272,384]{1,0:T(8,128)(2,1)S(1)}, u32[]{:S(2)}, u32[]{:S(2)}) collective-permute-start(bf16[272,384]{1,0:T(8,128)(2,1)} %collective-permute-done.39.refs_12_), channel_id=1, source_target_pairs={{0,4},{4,0},{8,12},{12,8},{16,20},{20,16},{24,28},{28,24},{1,5},{5... | collective-permute-start | bytes 626696 | tf_op jit(solution)/shard_map/ppermute | solution.py:72
  273.0 23.1 %collective-permute-start.42 = (bf16[272,384]{1,0:T(8,128)(2,1)}, bf16[272,384]{1,0:T(8,128)(2,1)S(1)}, u32[]{:S(2)}, u32[]{:S(2)}) collective-permute-start(bf16[272,384]{1,0:T(8,128)(2,1)} %collective-permute-done.41.refs_14_), channel_id=1, source_target_pairs={{0,4},{4,0},{8,12},{12,8},{16,20},{20,16},{24,28},{28,24},{1,5},{5... | collective-permute-start | bytes 626696 | tf_op jit(solution)/shard_map/ppermute | solution.py:72
  331.8 216.2 %reduce-scatter.9.cloned.1.call-start = ((), (), s32[]{:S(2)}) async-start(), calls=%async_computation.8 | async-start | bytes 3981312
  342.0 11.4 %collective-permute-start.47 = (bf16[128,1536]{1,0:T(8,128)(2,1)S(1)}, bf16[128,1536]{1,0:T(8,128)(2,1)}, u32[]{:S(2)}, u32[]{:S(2)}) collective-permute-start(bf16[128,1536]{1,0:T(8,128)(2,1)S(1)} %add_convert_fusion.4), channel_id=1, source_target_pairs={{0,2},{1,3},{2,0},{3,1},{4,6},{5,7},{6,4},{7,5},{8,10},{9,11},{10,... | collective-permute-start | bytes 1179656 | tf_op jit(solution)/shard_map/ppermute | solution.py:72
  351.3 226.6 %reduce-scatter.7.cloned.1.call-start = ((), (), s32[]{:S(2)}) async-start(), calls=%async_computation.7 | async-start | bytes 3981312
  364.7 19.2 %collective-permute-start.52 = (bf16[272,384]{1,0:T(8,128)(2,1)S(1)}, bf16[272,384]{1,0:T(8,128)(2,1)}, u32[]{:S(2)}, u32[]{:S(2)}) collective-permute-start(bf16[272,384]{1,0:T(8,128)(2,1)S(1)} %collective-permute-done.50.refs_2_), channel_id=1, source_target_pairs={{8,0},{12,4},{16,8},{20,12},{24,16},{28,20},{9,1},{13,5},{17,9},{2... | collective-permute-start | bytes 626696 | tf_op jit(solution)/shard_map/ppermute | solution.py:92
  366.0 48.8 %collective-permute-start.69 = (bf16[1024,1536]{1,0:T(8,128)(2,1)}, bf16[1024,1536]{1,0:T(8,128)(2,1)}, u32[]{:S(2)}, u32[]{:S(2)}) collective-permute-start(bf16[1024,1536]{1,0:T(8,128)(2,1)} %all-gather.11.cloned.1.call-done.incoming), channel_id=1, source_target_pairs={{0,1},{1,0},{2,3},{3,2},{4,5},{5,4},{6,7},{7,6},{8,9},{9,8},{10,11... | collective-permute-start | bytes 9437192 | tf_op jit(solution)/shard_map/ppermute | solution.py:72
  372.0 24.6 %collective-permute-start.57 = (bf16[272,384]{1,0:T(8,128)(2,1)S(1)}, bf16[272,384]{1,0:T(8,128)(2,1)}, u32[]{:S(2)}, u32[]{:S(2)}) collective-permute-start(bf16[272,384]{1,0:T(8,128)(2,1)S(1)} %pad_maximum_fusion.10.refs_8_), channel_id=1, source_target_pairs={{8,0},{12,4},{16,8},{20,12},{24,16},{28,20},{9,1},{13,5},{17,9},{2... | collective-permute-start | bytes 626696 | tf_op jit(solution)/shard_map/ppermute | solution.py:92
  373.3 25.3 %collective-permute-start.49 = (bf16[272,384]{1,0:T(8,128)(2,1)S(1)}, bf16[272,384]{1,0:T(8,128)(2,1)S(1)}, u32[]{:S(2)}, u32[]{:S(2)}) collective-permute-start(bf16[272,384]{1,0:T(8,128)(2,1)S(1)} %pad_maximum_fusion.9.refs_0_), channel_id=1, source_target_pairs={{0,4},{4,0},{8,12},{12,8},{16,20},{20,16},{24,28},{28,24},{1,5},{5... | collective-permute-start | bytes 626696 | tf_op jit(solution)/shard_map/ppermute | solution.py:72
  383.8 20.8 %collective-permute-start.54 = (bf16[272,384]{1,0:T(8,128)(2,1)}, bf16[272,384]{1,0:T(8,128)(2,1)S(1)}, u32[]{:S(2)}, u32[]{:S(2)}) collective-permute-start(bf16[272,384]{1,0:T(8,128)(2,1)} %collective-permute-done.52.refs_4_), channel_id=1, source_target_pairs={{8,0},{12,4},{16,8},{20,12},{24,16},{28,20},{9,1},{13,5},{17,9},{2... | collective-permute-start | bytes 626696 | tf_op jit(solution)/shard_map/ppermute | solution.py:92
  396.6 12.4 %collective-permute-start.59 = (bf16[272,384]{1,0:T(8,128)(2,1)}, bf16[272,384]{1,0:T(8,128)(2,1)}, u32[]{:S(2)}, u32[]{:S(2)}) collective-permute-start(bf16[272,384]{1,0:T(8,128)(2,1)} %collective-permute-done.57.refs_10_), channel_id=1, source_target_pairs={{8,0},{12,4},{16,8},{20,12},{24,16},{28,20},{9,1},{13,5},{17,9},{2... | collective-permute-start | bytes 626696 | tf_op jit(solution)/shard_map/ppermute | solution.py:92
  397.8 14.8 %collective-permute-start.51 = (bf16[272,384]{1,0:T(8,128)(2,1)S(1)}, bf16[272,384]{1,0:T(8,128)(2,1)}, u32[]{:S(2)}, u32[]{:S(2)}) collective-permute-start(bf16[272,384]{1,0:T(8,128)(2,1)S(1)} %collective-permute-done.50.refs_2_), channel_id=1, source_target_pairs={{0,4},{4,0},{8,12},{12,8},{16,20},{20,16},{24,28},{28,24},{1,5},{5... | collective-permute-start | bytes 626696 | tf_op jit(solution)/shard_map/ppermute | solution.py:72
  399.3 13.4 %collective-permute-start.53 = (bf16[272,384]{1,0:T(8,128)(2,1)}, bf16[272,384]{1,0:T(8,128)(2,1)}, u32[]{:S(2)}, u32[]{:S(2)}) collective-permute-start(bf16[272,384]{1,0:T(8,128)(2,1)} %collective-permute-done.52.refs_4_), channel_id=1, source_target_pairs={{0,4},{4,0},{8,12},{12,8},{16,20},{20,16},{24,28},{28,24},{1,5},{5... | collective-permute-start | bytes 626696 | tf_op jit(solution)/shard_map/ppermute | solution.py:72
  412.6 55.9 %collective-permute-start.66 = (bf16[1024,1536]{1,0:T(8,128)(2,1)}, bf16[1024,1536]{1,0:T(8,128)(2,1)}, u32[]{:S(2)}, u32[]{:S(2)}) collective-permute-start(bf16[1024,1536]{1,0:T(8,128)(2,1)} %all-gather.5.cloned.1.call-done.rows), channel_id=1, source_target_pairs={{0,1},{1,0},{2,3},{3,2},{4,5},{5,4},{6,7},{7,6},{8,9},{9,8},{10,11... | collective-permute-start | bytes 9437192 | tf_op jit(solution)/shard_map/ppermute | solution.py:72
  412.7 13.5 %collective-permute-start.56 = (bf16[272,384]{1,0:T(8,128)(2,1)S(1)}, bf16[272,384]{1,0:T(8,128)(2,1)}, u32[]{:S(2)}, u32[]{:S(2)}) collective-permute-start(bf16[272,384]{1,0:T(8,128)(2,1)S(1)} %pad_maximum_fusion.10.refs_8_), channel_id=1, source_target_pairs={{0,4},{4,0},{8,12},{12,8},{16,20},{20,16},{24,28},{28,24},{1,5},{5... | collective-permute-start | bytes 626696 | tf_op jit(solution)/shard_map/ppermute | solution.py:72
  414.3 15.4 %collective-permute-start.58 = (bf16[272,384]{1,0:T(8,128)(2,1)}, bf16[272,384]{1,0:T(8,128)(2,1)}, u32[]{:S(2)}, u32[]{:S(2)}) collective-permute-start(bf16[272,384]{1,0:T(8,128)(2,1)} %collective-permute-done.57.refs_10_), channel_id=1, source_target_pairs={{0,4},{4,0},{8,12},{12,8},{16,20},{20,16},{24,28},{28,24},{1,5},{5... | collective-permute-start | bytes 626696 | tf_op jit(solution)/shard_map/ppermute | solution.py:72
  414.8 19.7 %collective-permute-start.60 = (bf16[272,384]{1,0:T(8,128)(2,1)}, bf16[272,384]{1,0:T(8,128)(2,1)}, u32[]{:S(2)}, u32[]{:S(2)}) collective-permute-start(bf16[272,384]{1,0:T(8,128)(2,1)} %collective-permute-done.59.refs_12_), channel_id=1, source_target_pairs={{0,4},{4,0},{8,12},{12,8},{16,20},{20,16},{24,28},{28,24},{1,5},{5... | collective-permute-start | bytes 626696 | tf_op jit(solution)/shard_map/ppermute | solution.py:72
  418.1 21.0 %collective-permute-start.62 = (bf16[272,384]{1,0:T(8,128)(2,1)}, bf16[272,384]{1,0:T(8,128)(2,1)}, u32[]{:S(2)}, u32[]{:S(2)}) collective-permute-start(bf16[272,384]{1,0:T(8,128)(2,1)} %collective-permute-done.61.refs_14_), channel_id=1, source_target_pairs={{0,4},{4,0},{8,12},{12,8},{16,20},{20,16},{24,28},{28,24},{1,5},{5... | collective-permute-start | bytes 626696 | tf_op jit(solution)/shard_map/ppermute | solution.py:72
  459.0 12.4 %collective-permute-start.64 = (bf16[128,1536]{1,0:T(8,128)(2,1)}, bf16[128,1536]{1,0:T(8,128)(2,1)}, u32[]{:S(2)}, u32[]{:S(2)}) collective-permute-start(bf16[128,1536]{1,0:T(8,128)(2,1)} %add_convert_fusion.2), channel_id=1, source_target_pairs={{0,2},{1,3},{2,0},{3,1},{4,6},{5,7},{6,4},{7,5},{8,10},{9,11},{10,... | collective-permute-start | bytes 1179656 | tf_op jit(solution)/shard_map/ppermute | solution.py:72
  470.0 34.1 %collective-permute-start.68 = (bf16[1024,1536]{1,0:T(8,128)(2,1)}, bf16[1024,1536]{1,0:T(8,128)(2,1)}, u32[]{:S(2)}, u32[]{:S(2)}) collective-permute-start(bf16[1024,1536]{1,0:T(8,128)(2,1)} %all-gather.9.cloned.1.call-done.rows), channel_id=1, source_target_pairs={{0,1},{1,0},{2,3},{3,2},{4,5},{5,4},{6,7},{7,6},{8,9},{9,8},{10,11... | collective-permute-start | bytes 9437192 | tf_op jit(solution)/shard_map/ppermute | solution.py:72
  472.7 18.3 %collective-permute-start.65 = (bf16[128,1536]{1,0:T(8,128)(2,1)S(1)}, bf16[128,1536]{1,0:T(8,128)(2,1)S(1)}, u32[]{:S(2)}, u32[]{:S(2)}) collective-permute-start(bf16[128,1536]{1,0:T(8,128)(2,1)S(1)} %add_convert_fusion.1), channel_id=1, source_target_pairs={{0,1},{1,0},{2,3},{3,2},{4,5},{5,4},{6,7},{7,6},{8,9},{9,8},{10,11... | collective-permute-start | bytes 1179656 | tf_op jit(solution)/shard_map/ppermute | solution.py:72
  497.0 57.8 %collective-permute-start.67 = (bf16[1024,1536]{1,0:T(8,128)(2,1)}, bf16[1024,1536]{1,0:T(8,128)(2,1)}, u32[]{:S(2)}, u32[]{:S(2)}) collective-permute-start(bf16[1024,1536]{1,0:T(8,128)(2,1)} %all-gather.7.cloned.1.call-done.incoming), channel_id=1, source_target_pairs={{0,1},{1,0},{2,3},{3,2},{4,5},{5,4},{6,7},{7,6},{8,9},{9,8},{10,11... | collective-permute-start | bytes 9437192 | tf_op jit(solution)/shard_map/ppermute | solution.py:72
  (161 other events, 1276.3 us)
Sparse Core Ops, SparseCore 0:
  97.4 81.2 all-gather.10
  180.9 74.8 all-gather.4
  264.9 66.2 all-gather.8
  333.2 69.5 all-gather.6
  406.3 87.9 reduce-scatter.8
  497.7 78.6 reduce-scatter.6

commit v2 on v1

v2 whole, which is shorter than its diff:
```python
import functools

import jax
import jax.numpy as jnp
from jax import lax
from jax.experimental import pallas as pl
from jax.experimental.pallas import tpu as pltpu
from jax.sharding import PartitionSpec as P

HEAD_SIZE = 96
EPSILON = 1e-05
ROTARY_BASE = 100000.0
NEGATIVE = -1e30
SCALE = HEAD_SIZE ** (-0.5)
BF16 = jnp.bfloat16
F32 = jnp.float32


def product(left, right):
    return jnp.dot(left, right, preferred_element_type=F32)


def product_left(left, right):
    return lax.dot_general(left, right, (((0,), (0,)), ((), ())), preferred_element_type=F32)


def product_right(left, right):
    return lax.dot_general(left, right, (((1,), (1,)), ((), ())), preferred_element_type=F32)


def rms_norm(rows, gain):
    return rows * lax.rsqrt(jnp.mean(rows * rows, axis=-1, keepdims=True) + EPSILON) * gain


def rms_norm_back(rows, gain, incoming):
    scale = lax.rsqrt(jnp.mean(rows * rows, axis=-1, keepdims=True) + EPSILON)
    weighted = incoming * gain
    inner = jnp.mean(rows * weighted, axis=-1, keepdims=True)
    back = scale * weighted - rows * (scale * scale * scale * inner)
    return back, jnp.sum(incoming * rows * scale, axis=0, keepdims=True)


def rotate(rows, cosine, sine):
    half = HEAD_SIZE // 2
    turned = jnp.concatenate([-rows[..., half:], rows[..., :half]], axis=-1)
    return rows * cosine + turned * sine


def unrotate(rows, cosine, sine):
    half = HEAD_SIZE // 2
    scaled = rows * sine
    return rows * cosine + jnp.concatenate([scaled[..., half:], -scaled[..., :half]], axis=-1)


def rotary_tables(positions):
    half = HEAD_SIZE // 2
    rates = ROTARY_BASE ** (-(jnp.arange(half).astype(F32) * 2.0 / HEAD_SIZE))
    angle = positions.astype(F32)[:, None] * rates[None, :]
    angle = jnp.concatenate([angle, angle], axis=-1)
    return jnp.cos(angle), jnp.sin(angle)


def first_tokens(lengths, index):
    bounds = jnp.cumsum(lengths)
    starts = bounds - lengths
    owner = jnp.sum((index[:, None] >= bounds[None, :]).astype(jnp.int32), axis=1)
    picks = owner[:, None] == jnp.arange(lengths.shape[0], dtype=jnp.int32)[None, :]
    return jnp.sum(jnp.where(picks, starts[None, :], 0), axis=1).astype(jnp.int32)


def swap(rows, axis, size, bit):
    return lax.ppermute(rows, axis, [(i, i ^ bit) for i in range(size)])


def tie(*values):
    return lax.optimization_barrier(values)


def sum_tp(send, keep, beside=None):
    pair = (keep + swap(send, "tp", 4, 1).astype(F32)).astype(BF16)
    moved = swap(pair, "tp", 4, 2)
    done = None
    if beside is not None:
        moved, done = tie(moved, beside(pair))
    whole = (pair.astype(F32) + moved.astype(F32)).astype(BF16)
    pieces = whole, swap(whole, "tp", 4, 1)
    return pieces if beside is None else (pieces, done)


def slot_block(own, slot):
    return (own // 2 - slot // 2) * 2 + own % 2 + slot % 2 * (1 - 2 * (own % 2))


def gather_pairs(rows, blocks):
    slots = []
    for far in range(blocks // 2):
        pairs = [(i, i + 2 * far) for i in range(blocks - 2 * far)]
        slots.append(lax.ppermute(rows, "blk", pairs) if far else rows)
    return [part for near in slots for part in (near, swap(near, "blk", blocks, 1))]


def send_back(even, odd, first, blocks):
    other = swap(odd, "blk", blocks, 1)
    rows = even[0].shape[0]
    received = []
    for index, term in enumerate(even):
        theirs = other[index * rows : (index + 1) * rows]
        both = (term.astype(F32) + theirs.astype(F32)).astype(BF16)
        far = first // 2 + index
        pairs = [(i, i - 2 * far) for i in range(2 * far, blocks)]
        received.append(lax.ppermute(both, "blk", pairs) if far else both)
    return received


def sum_blocks(partial, blocks):
    rows, columns = partial.shape
    parts = lax.all_to_all(partial, "blk", 0, 0, tiled=True).reshape(blocks, -1, columns)
    return jnp.sum(parts.astype(F32), axis=0)


def sum_pair(keep, send, blocks):
    return (keep.astype(F32) + swap(send, "blk", blocks, 1).astype(F32)).astype(BF16)


def scatter_blocks(both, blocks):
    groups = [list(range(parity, blocks, 2)) for parity in range(2)]
    return lax.psum_scatter(
        both, "blk", scatter_dimension=0, axis_index_groups=groups, tiled=True
    )


def gather_rows(half):
    own = lax.all_gather(half, "blk", axis=0, tiled=True)
    return own, swap(own, "tp", 4, 1)


WHOLE = pl.BlockSpec(memory_space=pltpu.VMEM)
SCALARS = pl.BlockSpec(memory_space=pltpu.SMEM)
MEGA = 1024 * 1024
TIMES = dict(
    front=2.5,
    attend=8,
    feed_forward=7,
    feed_both=9,
    feed_back=12,
    middle_back=2.5,
    attend_back=6,
    pair_back=2,
    inputs_back=3,
    feedforward_prepare=11,
    feedforward_weights=17.5,
    feedforward_finish=10.5,
    attention_weights=2.5,
    split_share=1,
)


def cost(name):
    return pl.CostEstimate(
        flops=int(TIMES[name] * TIME_FLOPS), bytes_accessed=0, transcendentals=0
    )


TIME_FLOPS = 1.1e9


def shaped(*shapes):
    return tuple(jax.ShapeDtypeStruct(shape, kind) for shape, kind in shapes)


def call(kernel, name, info, arrays, outs, scratch=(), limit=32, **more):
    more.setdefault("in_specs", [SCALARS] + [WHOLE] * len(arrays))
    more.setdefault("out_specs", (WHOLE,) * len(outs))
    return pl.pallas_call(
        kernel,
        out_shape=shaped(*outs),
        scratch_shapes=list(scratch),
        compiler_params=pltpu.CompilerParams(vmem_limit_bytes=limit * MEGA),
        cost_estimate=cost(name),
        name=name,
        **more,
    )(info, *arrays)


def halves(info, half):
    start = pl.multiple_of(info[1] * half, half)
    return pl.ds(start, half), pl.ds(pl.multiple_of(half - start, half), half)


def join(info, pieces, put):
    whole, other = pieces
    mine, theirs = halves(info, whole.shape[0])
    put(mine, whole[...].astype(F32))
    put(theirs, other[...].astype(F32))


def part(info, total, send, keep):
    mine, theirs = halves(info, keep.shape[0])
    keep[...] = total[mine, :]
    send[...] = total[theirs, :].astype(BF16)


def both_halves(tokens, width):
    return ((tokens // 2, width), BF16), ((tokens // 2, width), F32)


def front_kernel(joined, info, base, *refs):
    if joined:
        whole, other = refs[:2]
        refs = refs[2:]
    gain, query_weight, key_weight, value_weight, cosine, sine = refs[:6]
    normed, query, pair = refs[6:9]
    if joined:
        inputs = refs[9]

        def put(rows, values):
            inputs[rows, :] = base[rows, :] + values

        join(info, (whole, other), put)
        source = inputs[...]
    else:
        source = base[...].astype(F32)
    normed[...] = rms_norm(source, gain[...]).astype(BF16)

    def turned(weight, out):
        rows = product(normed[...], weight[...])
        for lane in range(0, weight.shape[1], HEAD_SIZE):
            piece = rows[:, lane : lane + HEAD_SIZE]
            out[:, lane : lane + HEAD_SIZE] = rotate(piece, cosine[...], sine[...]).astype(BF16)

    turned(key_weight, pair)
    pair[:, key_weight.shape[1] :] = product(normed[...], value_weight[...]).astype(BF16)
    turned(query_weight, query)


def front(base, pieces, weights, layout):
    tokens, width = base.shape
    wide, narrow = weights[1].shape[1], weights[2].shape[1]
    joined = pieces is not None
    arrays = (base,) + (pieces if joined else ()) + (weights[0].reshape(1, -1),)
    arrays += tuple(weights[1:4]) + layout.tables
    outs = [((tokens, width), BF16), ((tokens, wide), BF16), ((tokens, 2 * narrow), BF16)]
    if joined:
        outs.append(((tokens, width), F32))
    return call(functools.partial(front_kernel, joined), "front", layout.info, arrays, outs)


def feed_specs(arrays, weights, chunk):
    width = weights[0].shape[0]
    across = pl.BlockSpec((width, chunk), lambda i: (0, i))
    down = pl.BlockSpec((chunk, width), lambda i: (i, 0))
    return [SCALARS] + [fixed(array.shape) for array in arrays] + [across, across, down]


def feed_call(kernel, name, layout, arrays, weights, outs, scratch):
    chunk = 256
    return call(
        kernel,
        name,
        layout.info,
        tuple(arrays) + tuple(weights),
        outs,
        scratch,
        limit=40,
        grid=(weights[0].shape[1] // chunk,),
        in_specs=feed_specs(arrays, weights, chunk),
        out_specs=tuple(fixed(shape) for shape, _ in outs),
    )


def feed_start(info, base, pieces, gain, hidden, inner_in, half):
    def put(rows, values):
        hidden[rows, :] = base[rows, :].astype(F32) + values

    join(info, pieces, put)
    inner_in[...] = rms_norm(hidden[...], gain[...]).astype(BF16)
    half[...] = inner_in[halves(info, half.shape[0])[0], :]


def feed_forward_kernel(
    info, base, whole, other, gain, beside, gate_weight, up_weight, down_weight, *refs
):
    hidden, inner_in, half, send, keep, total = refs

    @pl.when(pl.program_id(0) == 0)
    def _():
        width = base.shape[1]
        feed_start(info, base, (whole, other), gain, hidden, inner_in, half.at[:, :width])
        half[:, width:] = beside[halves(info, half.shape[0])[0], :]
        total[...] = jnp.zeros_like(total)

    gate = product(inner_in[...], gate_weight[...])
    up = product(inner_in[...], up_weight[...])
    inner = (gate / (1.0 + jnp.exp(-gate)) * up).astype(BF16)
    total[...] += product(inner, down_weight[...])

    @pl.when(pl.program_id(0) == pl.num_programs(0) - 1)
    def _():
        part(info, total, send, keep)


def feed_forward(base, pieces, beside, weights, layout):
    tokens, width = base.shape
    outs = [((tokens, width), F32), ((tokens, width), BF16), ((tokens // 2, 2 * width), BF16)]
    outs += both_halves(tokens, width)
    arrays = (base, *pieces, weights[5].reshape(1, -1), beside)
    scratch = [pltpu.VMEM((tokens, width), F32)]
    return feed_call(
        feed_forward_kernel, "feed_forward", layout, arrays, weights[6:9], outs, scratch
    )


def feed_both_kernel(
    info, base, whole, other, gain, incoming, gate_weight, up_weight, down_weight, *refs
):
    hidden, half, send, keep, back_send, back_keep, inner_in, total, back_total = refs

    @pl.when(pl.program_id(0) == 0)
    def _():
        feed_start(info, base, (whole, other), gain, hidden, inner_in, half)
        total[...] = jnp.zeros_like(total)
        back_total[...] = jnp.zeros_like(back_total)

    gate = product(inner_in[...], gate_weight[...])
    up = product(inner_in[...], up_weight[...])
    back_inner = product_right(incoming[...], down_weight[...])
    inner, back_gate, back_up = swiglu_back(gate, up, back_inner)
    total[...] += product(inner, down_weight[...])
    back_total[...] += product_right(back_gate, gate_weight[...])
    back_total[...] += product_right(back_up, up_weight[...])

    @pl.when(pl.program_id(0) == pl.num_programs(0) - 1)
    def _():
        part(info, total, send, keep)
        part(info, back_total, back_send, back_keep)


def feed_both(base, pieces, incoming, weights, layout):
    tokens, width = base.shape
    outs = [((tokens, width), F32), ((tokens // 2, width), BF16)]
    outs += both_halves(tokens, width) * 2
    arrays = (base, *pieces, weights[5].reshape(1, -1), incoming)
    scratch = [pltpu.VMEM((tokens, width), BF16)] + [pltpu.VMEM((tokens, width), F32)] * 2
    return feed_call(feed_both_kernel, "feed_both", layout, arrays, weights[6:9], outs, scratch)


def feed_back_kernel(
    info,
    rows,
    gain,
    back_hidden,
    whole,
    other,
    inner_in,
    gate_weight,
    up_weight,
    down_weight,
    *refs,
):
    gradient, half, back_gain, send, keep, low, total = refs

    @pl.when(pl.program_id(0) == 0)
    def _():
        def put(place, values):
            total[place, :] = values

        join(info, (whole, other), put)
        back, gains = rms_norm_back(rows[...], gain[...], total[...])
        back_gain[...] = gains
        gradient[...] = back + back_hidden[...]
        low[...] = gradient[...].astype(BF16)
        half[...] = low[halves(info, half.shape[0])[0], :]
        total[...] = jnp.zeros_like(total)

    gate = product(inner_in[...], gate_weight[...])
    up = product(inner_in[...], up_weight[...])
    back_inner = product_right(low[...], down_weight[...])
    _, back_gate, back_up = swiglu_back(gate, up, back_inner)
    total[...] += product_right(back_gate, gate_weight[...])
    total[...] += product_right(back_up, up_weight[...])

    @pl.when(pl.program_id(0) == pl.num_programs(0) - 1)
    def _():
        part(info, total, send, keep)


def feed_back(rows, gain, back_hidden, pieces, inner_in, weights, layout):
    tokens, width = rows.shape
    outs = [((tokens, width), F32), ((tokens // 2, width), BF16), ((1, width), F32)]
    outs += both_halves(tokens, width)
    arrays = (rows, gain.reshape(1, -1), back_hidden, *pieces, inner_in)
    scratch = [pltpu.VMEM((tokens, width), BF16), pltpu.VMEM((tokens, width), F32)]
    return feed_call(feed_back_kernel, "feed_back", layout, arrays, weights[6:9], outs, scratch)


def middle_back_kernel(info, hidden, incoming, whole, other, gain, projection, mixed, *refs):
    back_hidden, low, back_mixed, delta, back_gain = refs

    def put(place, values):
        back_hidden[place, :] = values

    join(info, (whole, other), put)
    back, gains = rms_norm_back(hidden[...], gain[...], back_hidden[...])
    back_gain[...] = gains
    back_hidden[...] = back + incoming[...].astype(F32)
    low[...] = back_hidden[...].astype(BF16)
    back_mixed[...] = product_right(low[...], projection[...]).astype(BF16)
    both = back_mixed[...].astype(F32) * mixed[...].astype(F32)
    for head in range(both.shape[1] // HEAD_SIZE):
        piece = both[:, head * HEAD_SIZE : (head + 1) * HEAD_SIZE].T
        delta[head : head + 1, :] = jnp.sum(piece, axis=0, keepdims=True)


def middle_back(hidden, incoming, pieces, weights, mixed, layout):
    tokens, width = hidden.shape
    wide = mixed.shape[1]
    outs = [
        ((tokens, width), F32),
        ((tokens, width), BF16),
        ((tokens, wide), BF16),
        ((wide // HEAD_SIZE, tokens), F32),
        ((1, width), F32),
    ]
    arrays = (hidden, incoming, *pieces, weights[5].reshape(1, -1), weights[4], mixed)
    return call(middle_back_kernel, "middle_back", layout.info, arrays, outs)


def pair_back_kernel(blocks, info, back_query, query_weight, key_weight, value_weight, *refs):
    cosine, sine = refs[:2]
    received = refs[2 : 2 + blocks]
    pair, send, keep, total = refs[2 + blocks :]
    width = key_weight.shape[1]
    sums = received[0][...].astype(F32)
    for term in received[1:]:
        sums += term[...].astype(F32)
    for lane in range(0, width, HEAD_SIZE):
        piece = sums[:, lane : lane + HEAD_SIZE]
        pair[:, lane : lane + HEAD_SIZE] = unrotate(piece, cosine[...], sine[...]).astype(BF16)
    pair[:, width:] = sums[:, width:].astype(BF16)
    total[...] = product_right(back_query[...], query_weight[...])
    total[...] += product_right(pair[:, :width], key_weight[...])
    total[...] += product_right(pair[:, width:], value_weight[...])
    part(info, total, send, keep)


def pair_back(received, back_query, weights, layout):
    tokens = back_query.shape[0]
    width = weights[1].shape[0]
    outs = [((tokens, received[0].shape[1]), BF16), *both_halves(tokens, width)]
    return call(
        functools.partial(pair_back_kernel, len(received)),
        "pair_back",
        layout.info,
        (back_query, *weights[1:4], *layout.tables, *received),
        outs,
        [pltpu.VMEM((tokens, width), F32)],
    )


def inputs_back_kernel(info, rows, gain, back_hidden, whole, other, gradient, back_gain):
    def put(place, values):
        gradient[place, :] = values

    join(info, (whole, other), put)
    back, gains = rms_norm_back(rows[...].astype(F32), gain[...], gradient[...])
    back_gain[...] = gains
    gradient[...] = back + back_hidden[...]


def inputs_back(rows, gain, back_hidden, pieces, layout):
    tokens, width = rows.shape
    outs = [((tokens, width), F32), ((1, width), F32)]
    arrays = (rows, gain.reshape(1, -1), back_hidden, *pieces)
    return call(inputs_back_kernel, "inputs_back", layout.info, arrays, outs)


def head_rows(ref, head, group, tokens):
    parts = []
    for member in range(group):
        lane = (head * group + member) * HEAD_SIZE
        parts.append(ref[:tokens, lane : lane + HEAD_SIZE])
    return jnp.concatenate(parts, axis=0)


def wide(row, group):
    return jnp.concatenate([row] * group, axis=1)


def seen_mask(first_row, key_start, query_start, tokens, group):
    shape = (tokens, tokens)
    key = key_start + lax.broadcasted_iota(jnp.int32, shape, 0)
    query = query_start + lax.broadcasted_iota(jnp.int32, shape, 1)
    seen = (key <= query) & (key >= first_row)
    return jnp.concatenate([seen.astype(F32)] * group, axis=1) > 0.5


def earlier_block(own, slot):
    block = slot_block(own, slot)
    return block, (block >= 0) & (block <= own)


def attend_kernel(blocks, heads, group, info, firsts, query, projection, *refs):
    pairs = refs[:blocks]
    mixed_ref, log_ref, send, keep, scores, top, total, partial = refs[blocks:]
    tokens = query.shape[0]
    own = info[0]
    first_row = firsts[pl.ds(own, 1), :]
    for head in range(heads):
        rows = head_rows(query, head, group, tokens)
        top[...] = jnp.full_like(top, NEGATIVE)
        for slot in range(blocks):
            block, valid = earlier_block(own, slot)

            @pl.when(valid)
            def _():
                keys = pairs[slot][:, head * HEAD_SIZE : (head + 1) * HEAD_SIZE]
                found = product_right(keys, rows) * SCALE
                seen = seen_mask(first_row, block * tokens, own * tokens, tokens, group)
                found = jnp.where(seen, found, NEGATIVE)
                scores[slot] = found
                top[...] = jnp.maximum(top[...], jnp.max(found, axis=0, keepdims=True))

        highest = top[0:1, :]
        total[...] = jnp.zeros_like(total)
        top[...] = jnp.zeros_like(top)
        for slot in range(blocks):
            block, valid = earlier_block(own, slot)

            @pl.when(valid)
            def _():
                lane = (heads + head) * HEAD_SIZE
                values = pairs[slot][:, lane : lane + HEAD_SIZE]
                weights = jnp.exp(scores[slot] - highest)
                top[...] += jnp.sum(weights, axis=0, keepdims=True)
                total[...] += product_left(values, weights.astype(BF16))

        mass = top[0:1, :]
        result = (total[...] / mass).T
        logs = highest + jnp.log(mass)
        for member in range(group):
            lane = (head * group + member) * HEAD_SIZE
            span = slice(member * tokens, (member + 1) * tokens)
            mixed_ref[:, lane : lane + HEAD_SIZE] = result[span].astype(BF16)
            log_ref[head * group + member : head * group + member + 1, :] = logs[:, span]


    partial[...] = product(mixed_ref[...], projection[...])
    part(info, partial, send, keep)


def attend(query, pairs, projection, layout, heads, group):
    tokens, wide = query.shape
    width = projection.shape[1]
    blocks = len(pairs)
    outs = [((tokens, wide), BF16), ((heads * group, tokens), F32), *both_halves(tokens, width)]
    scratch = [
        pltpu.VMEM((blocks, tokens, group * tokens), F32),
        pltpu.VMEM((8, group * tokens), F32),
        pltpu.VMEM((HEAD_SIZE, group * tokens), F32),
        pltpu.VMEM((tokens, width), F32),
    ]
    return call(
        functools.partial(attend_kernel, blocks, heads, group),
        "attend",
        layout.info,
        (layout.firsts, query, projection, *pairs),
        outs,
        scratch,
        limit=40,
    )


def attend_back_kernel(
    first, count, heads, group, last, info, firsts, query, back, logs, delta, cosine, sine, *refs
):
    pairs = refs[:count]
    refs = refs[count:]
    evens = count // 2
    started = len(refs) > evens + 2 + last
    if started:
        before, refs = refs[0], refs[1:]
    even, odd, out_ref = refs[:evens], refs[evens], refs[evens + 1]
    total = refs[evens + 2] if last else out_ref
    tokens = query.shape[0]
    own = info[0]
    first_row = firsts[pl.ds(own, 1), :]

    def put(index, lane, values):
        columns = slice(lane, lane + HEAD_SIZE)
        if index % 2:
            start = index // 2 * tokens
            odd[start : start + tokens, columns] = values.astype(BF16)
        else:
            even[index // 2][:, columns] = values.astype(BF16)

    for head in range(heads):
        rows = head_rows(query, head, group, tokens)
        back_rows = head_rows(back, head, group, tokens)
        members = range(head * group, (head + 1) * group)
        log_row = jnp.concatenate([logs[m : m + 1, :] for m in members], axis=1)
        delta_row = jnp.concatenate([delta[m : m + 1, :] for m in members], axis=1)
        if started:
            total[head] = before[head]
        else:
            total[head] = jnp.zeros(total.shape[1:], F32)
        lane = head * HEAD_SIZE
        value_lane = (heads + head) * HEAD_SIZE
        for index in range(count):
            block, valid = earlier_block(own, first + index)

            @pl.when(valid)
            def _():
                keys = pairs[index][:, lane : lane + HEAD_SIZE]
                values = pairs[index][:, value_lane : value_lane + HEAD_SIZE]
                found = product_right(keys, rows) * SCALE - log_row
                seen = seen_mask(first_row, block * tokens, own * tokens, tokens, group)
                probs = jnp.exp(jnp.where(seen, found, NEGATIVE))
                back_probs = product_right(values, back_rows)
                back_scores = (probs * (back_probs - delta_row) * SCALE).astype(BF16)
                total[head] += product_left(keys, back_scores)
                put(index, lane, product(back_scores, rows))
                put(index, value_lane, product(probs.astype(BF16), back_rows))

            @pl.when(jnp.logical_not(valid))
            def _():
                empty = jnp.zeros((tokens, HEAD_SIZE), F32)
                put(index, lane, empty)
                put(index, value_lane, empty)

        if last:
            result = total[head].T
            for member in range(group):
                out_lane = (head * group + member) * HEAD_SIZE
                piece = result[member * tokens : (member + 1) * tokens]
                out_ref[:, out_lane : out_lane + HEAD_SIZE] = unrotate(
                    piece, cosine[...], sine[...]
                ).astype(BF16)


def attend_back(first, query, back, logs, delta, pairs, before, last, layout, heads, group):
    tokens, width = query.shape
    count = len(pairs)
    state = (heads, HEAD_SIZE, group * tokens)
    earlier = [] if before is None else [before]
    columns = pairs[0].shape[1]
    outs = [((tokens, columns), BF16)] * (count // 2) + [((count // 2 * tokens, columns), BF16)]
    outs.append(((tokens, width), BF16) if last else (state, F32))
    return call(
        functools.partial(attend_back_kernel, first, count, heads, group, last),
        "attend_back",
        layout.info,
        (layout.firsts, query, back, logs, delta, *layout.tables, *pairs, *earlier),
        outs,
        [pltpu.VMEM(state, F32)] if last else [],
    )


def attention_back(query, back_mixed, logs, delta, pairs, layout, heads, group, beside):
    blocks = layout.blocks
    half = blocks // 2
    *even, odd, state = attend_back(
        half, query, back_mixed, logs, delta, pairs[half:], None, False, layout, heads, group
    )
    received = send_back(even, odd, half, blocks)
    *even, odd, back_query = attend_back(
        0, query, back_mixed, logs, delta, pairs[:half], state, True, layout, heads, group
    )
    received = send_back(even, odd, 0, blocks) + received
    received, done = tie(tuple(received), beside(back_query))
    return back_query, received, done


def attention_weights_kernel(blocks, info, low, mixed, normed, back_query, *refs):
    back_pair = refs[0] if len(refs) == 3 else None
    keep, send = refs[-2:]
    wide = mixed.shape[1]
    size = low.shape[1] // blocks
    parity = lax.rem(info[0], 2)
    for block in range(blocks):
        columns = slice(block * size, (block + 1) * size)
        rows = slice(block // 2 * size, (block // 2 + 1) * size)
        terms = [
            product_left(low[:, columns], mixed[...]).astype(BF16),
            product_left(normed[:, columns], back_query[...]).astype(BF16),
        ]
        if back_pair is not None:
            terms.append(product_left(normed[:, columns], back_pair[...]).astype(BF16))
        terms = jnp.concatenate(terms, axis=1)

        @pl.when(parity == block % 2)
        def _():
            keep[rows, :] = terms

        @pl.when(parity != block % 2)
        def _():
            send[rows, :] = terms


def attention_weights(low, mixed, normed, back_query, back_pair, layout):
    blocks = layout.blocks
    arrays = [low, mixed, normed, back_query] + ([] if back_pair is None else [back_pair])
    total = mixed.shape[1] + sum(array.shape[1] for array in arrays[3:])
    shape = (low.shape[1] // 2, total)
    return call(
        functools.partial(attention_weights_kernel, blocks),
        "attention_weights",
        layout.info,
        arrays,
        [(shape, BF16)] * 2,
    )


def split_kernel(share, *outs):
    start = 0
    for index, out in enumerate(outs):
        turned = index == 0
        size = out.shape[0] if turned else out.shape[1]
        piece = share[:, start : start + size].astype(F32)
        out[...] = piece.T if turned else piece
        start += size


def split_share(share, sizes):
    rows = share.shape[0]
    shapes = [(sizes[0], rows)] + [(rows, size) for size in sizes[1:]]
    return pl.pallas_call(
        split_kernel,
        out_shape=tuple(jax.ShapeDtypeStruct(shape, F32) for shape in shapes),
        in_specs=[WHOLE],
        out_specs=(WHOLE,) * len(shapes),
        compiler_params=pltpu.CompilerParams(vmem_limit_bytes=32 * 1024 * 1024),
        cost_estimate=cost("split_share"),
        name="split_share",
    )(share)


def window(place, part, width):
    return jnp.minimum(place * part // 128 * 128, width - 256)


def cut(scalars, sums, outs):
    @pl.when(pl.program_id(0) == pl.num_programs(0) - 1)
    def _():
        gate, up, down = outs
        size = gate.shape[0]
        rows = pl.ds(pl.multiple_of(scalars[1], 16), size)
        gate[...] = sums[0][rows, :]
        up[...] = sums[1][rows, :]
        down[...] = pltpu.roll(sums[2][...], 256 - scalars[1], 1)[:, :size]


def begin(started, before, outs, first):
    @pl.when(first)
    def _():
        for index, out in enumerate(outs):
            out[...] = before[index][...] if started else jnp.zeros_like(out)


def feedforward_weights_kernel(
    started, scalars, rows, incoming, gate_weight, up_weight, down_weight, *refs
):
    outs = refs[6:9] if started else refs[:3]
    begin(started, refs[:3], outs, pl.program_id(0) == 0)
    gate = product(rows[...], gate_weight[...])
    up = product(rows[...], up_weight[...])
    back_inner = product_right(incoming[...], down_weight[...])
    inner, back_gate, back_up = swiglu_back(gate, up, back_inner)
    columns = pl.ds(pl.multiple_of(scalars[0], 128), 256)
    rows_part, incoming_part = rows[:, columns], incoming[:, columns]
    outs[0][...] += product_left(rows_part, back_gate)
    outs[1][...] += product_left(rows_part, back_up)
    outs[2][...] += product_left(inner, incoming_part)
    if started:
        cut(scalars, outs, refs[3:6])


def feedforward_prepare_kernel(rows, gate_weight, up_weight, inner_out, gate_out, up_out):
    gate = product(rows[...], gate_weight[...])
    up = product(rows[...], up_weight[...])
    chance = 1.0 / (1.0 + jnp.exp(-gate))
    silu = gate * chance
    inner_out[...] = (silu * up).astype(BF16)
    gate_out[...] = (up * (chance + silu * (1.0 - chance))).astype(BF16)
    up_out[...] = silu.astype(BF16)


def feedforward_finish_kernel(
    started, scalars, rows, incoming, inner, gate_slope, up_slope, down_weight, *refs
):
    outs = refs[6:9] if started else refs[:3]
    begin(started, refs[:3], outs, pl.program_id(0) == 0)
    back_inner = product_right(incoming[...], down_weight[...])
    back_gate = (back_inner * gate_slope[...].astype(F32)).astype(BF16)
    back_up = (back_inner * up_slope[...].astype(F32)).astype(BF16)
    columns = pl.ds(pl.multiple_of(scalars[0], 128), 256)
    rows_part, incoming_part = rows[:, columns], incoming[:, columns]
    outs[0][...] += product_left(rows_part, back_gate)
    outs[1][...] += product_left(rows_part, back_up)
    outs[2][...] += product_left(inner[...], incoming_part)
    if started:
        cut(scalars, outs, refs[3:6])


STEP = 256


def fixed(shape):
    return pl.BlockSpec(shape, lambda i: (0,) * len(shape), pipeline_mode=pl.Buffered(1))


def moving(columns, offset=0):
    return pl.BlockSpec((STEP, columns), lambda i: (i + offset, 0))


def weight_call(kernel, name, layout, moved, still, hidden, steps, before):
    width = moved[0][1][-1]
    shapes = [(256, hidden), (256, hidden), (hidden, 256)]
    started = before is not None
    earlier = list(before) if started else []
    kept = lambda shape: pl.BlockSpec(
        shape, lambda i, s: (0,) * len(shape), pipeline_mode=pl.Buffered(1)
    )
    size = width // layout.blocks
    own = window(layout.own, size, width)
    place = jnp.stack([own, layout.own * size - own])
    outs = [(size, hidden), (size, hidden), (hidden, size)] if started else shapes
    return pl.pallas_call(
        functools.partial(kernel, started),
        out_shape=tuple(jax.ShapeDtypeStruct(shape, F32) for shape in outs),
        grid_spec=pltpu.PrefetchScalarGridSpec(
            num_scalar_prefetch=1,
            grid=(steps,),
            in_specs=[pl.BlockSpec(block, place) for _, block, place in moved]
            + [kept(array.shape) for array in still]
            + ([kept(shape) for shape in shapes] if started else []),
            out_specs=tuple(kept(shape) for shape in outs),
            scratch_shapes=[pltpu.VMEM(shape, F32) for shape in shapes] if started else [],
        ),
        compiler_params=pltpu.CompilerParams(vmem_limit_bytes=48 * MEGA),
        cost_estimate=cost(name),
        name=name,
    )(place, *[array for array, _, _ in moved], *still, *earlier)


def feedforward_weights(rows, incoming, weights, layout, before):
    total, width = rows.shape
    steps = total // STEP
    moved = [
        (rows, (STEP, width), lambda i, s: (i, 0)),
        (incoming, (STEP, width), lambda i, s: (i, 1)),
    ]
    return weight_call(
        feedforward_weights_kernel,
        "feedforward_weights",
        layout,
        moved,
        weights[6:9],
        weights[6].shape[1],
        steps,
        before,
    )


def feedforward_finish(rows, incoming, prepared, weights, layout, before):
    width = weights[6].shape[0]
    moved = [
        (array, (STEP, min(width, array.shape[1])), lambda i, s: (i, 0))
        for array in (rows, incoming, *prepared)
    ]
    return weight_call(
        feedforward_finish_kernel,
        "feedforward_finish",
        layout,
        moved,
        weights[8:9],
        weights[6].shape[1],
        rows.shape[0] // STEP,
        before,
    )


def feedforward_prepare(rows, weights):
    total, width = rows.shape[0], weights[6].shape[0]
    hidden = weights[6].shape[1]
    return pl.pallas_call(
        feedforward_prepare_kernel,
        grid=(total // STEP,),
        out_shape=(jax.ShapeDtypeStruct((total, hidden), BF16),) * 3,
        in_specs=[moving(width), fixed((width, hidden)), fixed((width, hidden))],
        out_specs=(moving(hidden),) * 3,
        compiler_params=pltpu.CompilerParams(vmem_limit_bytes=48 * 1024 * 1024),
        cost_estimate=cost("feedforward_prepare"),
        name="feedforward_prepare",
    )(rows, weights[6], weights[7])


def swiglu_back(gate, up, back_inner):
    chance = 1.0 / (1.0 + jnp.exp(-gate))
    silu = gate * chance
    inner = (silu * up).astype(BF16)
    back_gate = (back_inner * up * (chance + silu * (1.0 - chance))).astype(BF16)
    back_up = (back_inner * silu).astype(BF16)
    return inner, back_gate, back_up


class Layout:
    def __init__(self, lengths, tokens):
        self.tokens = tokens
        self.blocks = lax.axis_size("blk")
        self.own = lax.axis_index("blk")
        self.core = lax.rem(lax.axis_index("tp"), 2)
        index = jnp.arange(tokens * self.blocks, dtype=jnp.int32)
        firsts = first_tokens(lengths, index)
        mine = lax.dynamic_slice_in_dim(index - firsts, self.own * tokens, tokens, 0)
        self.tables = rotary_tables(mine)
        self.firsts = firsts.reshape(self.blocks, tokens)
        self.info = jnp.stack([self.own, self.core]).astype(jnp.int32)


def attention_share(normed, back_rows, blocks):
    return sum_blocks(product_left(normed, back_rows).astype(BF16), blocks)


def body(tokens, lengths, *rest):
    one, two, cotangent = rest[:9], rest[9:18], rest[18]
    layout = Layout(lengths, tokens.shape[0])
    core, blocks = layout.core, layout.blocks
    heads = one[2].shape[1] // HEAD_SIZE
    group = one[1].shape[1] // HEAD_SIZE // heads

    wide, narrow = one[1].shape[1], one[2].shape[1]

    normed_one, query_one, pair_one = front(tokens, None, one, layout)
    pairs_one = gather_pairs(pair_one, blocks)
    mixed_one, logs_one, send, keep = attend(query_one, pairs_one, one[4], layout, heads, group)
    hidden_one, inner_in_one, half_one, send, keep = feed_forward(
        tokens, sum_tp(send, keep), cotangent, one, layout
    )
    pieces = sum_tp(send, keep)
    rows_one = gather_rows(half_one)

    normed_two, query_two, pair_two, inputs_two = front(hidden_one, pieces, two, layout)
    pairs_two = gather_pairs(pair_two, blocks)
    mixed_two, logs_two, send, keep = attend(query_two, pairs_two, two[4], layout, heads, group)

    def prepare(rows, after):
        return feedforward_prepare(tie(after, rows)[1], one)

    pieces = sum_tp(send, keep)

    hidden_two, half_two, last_send, last_keep, send, keep = feed_both(
        inputs_two, pieces, cotangent, two, layout
    )
    rows_two = gather_rows(half_two)

    pieces = sum_tp(send, keep)
    back_hidden, low, back_mixed, delta, gain_feed_two = middle_back(
        hidden_two, cotangent, pieces, two, mixed_two, layout
    )

    def finish_forward(after):
        whole, other = sum_tp(tie(after, last_send)[1], last_keep)
        top, bottom = jnp.where(core == 0, whole, other), jnp.where(core == 0, other, whole)
        last = jnp.concatenate([top, bottom], axis=0).astype(F32)
        prepared_own = prepare(rows_one[0], after)
        prepared_other = prepare(rows_one[1], prepared_own[0])
        return (hidden_two + last).astype(BF16), prepared_own, prepared_other

    back_query, received, (result, prepared_own, prepared_other) = attention_back(
        query_two, back_mixed, logs_two, delta, pairs_two, layout, heads, group, finish_forward
    )
    back_pair, send, keep = pair_back(received, back_query, two, layout)

    state = [None]
    early = [None]

    def weights_two(piece):
        rows, incoming = early[0][piece], rows_one[piece]

        def run(after):
            held, rows_now, incoming_now = tie(after, rows, incoming)
            state[0] = feedforward_weights(
                rows_now, incoming_now, two, layout, state[0]
            )
            return state[0]

        return run

    terms_two = (low, mixed_two, normed_two, back_query, back_pair)

    def share_second(after):
        terms = tie(after, *terms_two)[1:]
        return attention_weights(*terms, layout)

    pieces, bucket_two = sum_tp(send, keep, share_second)

    gradient, half_low, gain_attention_two, send, keep = feed_back(
        inputs_two, two[0], back_hidden, pieces, inner_in_one, one, layout
    )

    pieces = sum_tp(send, keep)
    half_low, pieces = tie(half_low, pieces)
    early[0] = rows_two
    ends = gather_rows(half_low)
    share_two = scatter_blocks(sum_pair(*bucket_two, blocks), blocks)
    back_hidden, low, back_mixed, delta, gain_feed_one = middle_back(
        hidden_one, gradient, pieces, one, mixed_one, layout
    )
    back_query, received, state[0] = attention_back(
        query_one, back_mixed, logs_one, delta, pairs_one, layout, heads, group, weights_two(0)
    )
    back_pair, send, keep = pair_back(received, back_query, one, layout)

    def share_first(after):
        terms = tie(after, low, mixed_one, normed_one, back_query)[1:]
        return attention_weights(*terms, None, layout), weights_two(1)(after)

    pieces, (bucket_one, state[0]) = sum_tp(send, keep, share_first)
    share_one = scatter_blocks(sum_pair(*bucket_one, blocks), blocks)
    tokens_gradient, gain_attention_one = inputs_back(tokens, one[0], back_hidden, pieces, layout)
    feed_two = state[0]
    feed_one = None
    for rows, end, prepared in zip(rows_one, ends, (prepared_own, prepared_other)):
        feed_one = feedforward_finish(rows, end, prepared, one, layout, feed_one)
    share_pair_one = attention_share(normed_one, back_pair, blocks)
    projection_two, *others_two = split_share(share_two, (wide, wide, narrow, narrow))
    projection_one, gradient_query_one = split_share(share_one, (wide, wide))
    shares_two = (*others_two, projection_two)
    shares_one = (
        gradient_query_one,
        share_pair_one[:, :narrow],
        share_pair_one[:, narrow:],
        projection_one,
    )
    gains = jnp.stack([gain_attention_one, gain_feed_one, gain_attention_two, gain_feed_two])
    gains, feed_one = tie(gains, tuple(feed_one))
    gains = gains.reshape(4, blocks, -1).transpose(1, 0, 2)
    gains = jnp.sum(lax.all_to_all(gains, "blk", 0, 0, tiled=True), axis=0)
    return (
        (result, tokens_gradient)
        + (gains[0],)
        + shares_one
        + (gains[1],)
        + tuple(feed_one)
        + (gains[2],)
        + shares_two
        + (gains[3],)
        + tuple(feed_two)
    )


def solution(mesh):
    rows, columns = P("tp", None), P(None, "tp")
    layer = (P(), columns, columns, columns, rows, P(), columns, columns, rows)
    in_specs = (P("blk", None), P()) + layer + layer + (P("blk", None),)
    wide_out, tall_out = P("blk", "tp"), P("tp", "blk")
    layer_out = (
        P("blk"),
        wide_out,
        wide_out,
        wide_out,
        tall_out,
        P("blk"),
        wide_out,
        wide_out,
        tall_out,
    )
    out_specs = (P("blk", None), P("blk", None)) + layer_out + layer_out
    return jax.shard_map(body, mesh=mesh, in_specs=in_specs, out_specs=out_specs, check_vma=False)
```

time: 602 us -> 542 us (0.900)
  Pallas kernels: 108 us -> 157 us
  local copies, waits for them, and re-layouts: 86.2 us -> 49.5 us
  matrix products: 36.8 us -> 1.7 us
  other arithmetic: 43.5 us -> 17.3 us
  waiting for transfers between devices: 207 us -> 191 us
  starting transfers between devices: 93.6 us -> 101 us
    ppermute x18 -> x12, waiting for transfers between devices: 79.5 us -> 14.1 us  [the longest x6 14.1 us: gather_pairs(): slots.append(lax.ppermute(rows, 'blk', pairs) if far else rows)]
    pallas_call x10 -> x26, Pallas kernels: 108 us -> 157 us  [the longest x18 72.7 us: call(): pl.pallas_call(kernel, out_shape=shaped(*outs), scratch_shapes=list(scrat...]
    all_gather x4 -> x3, waiting for transfers between devices: 0.08 us -> 39.8 us  [gather_rows(): own = lax.all_gather(half, 'blk', axis=0, tiled=True)]
    dot_general x28 -> x0, matrix products: 32.8 us -> none  [the longest x14 18.4 us: product(): return jnp.dot(left, right, preferred_element_type=F32)]
    all_to_all x0 -> x1, starting transfers between devices: none -> 25.2 us  [sum_blocks(): lax.all_to_all(partial, 'blk', 0, 0, tiled=True)]
    dynamic_slice x12 -> x0, local copies, waits for them, and re-layouts: 17.6 us -> none  [the longest x4 7.17 us: feedforward_weights(): incoming_part = lax.dynamic_slice_in_dim(incoming, place * part, part, 1)]
    ppermute x52 -> x41, starting transfers between devices: 42.7 us -> 32.1 us  [swap(): return lax.ppermute(rows, axis, [(i, i ^ bit) for i in range(size)])]
    ppermute x52 -> x41, waiting for transfers between devices: 124 us -> 135 us  [swap(): return lax.ppermute(rows, axis, [(i, i ^ bit) for i in range(size)])]
  transfers between devices with their start and end apart: 77 -> 60, of which waited for: 45 -> 34; matrix products, arithmetic and copies ran while one was open for 19% -> 5% of each run, Pallas kernels for 18% -> 27%
where the time goes in v2:
time: 542 us; the launch traced here: 534 us
  waiting for transfers between devices  191 us (35%)
  Pallas kernels  157 us (29%)
  starting transfers between devices  101 us (19%)
  local copies, waits for them, and re-layouts  49.5 us (9%)
  other arithmetic  17.3 us (3%)
  between operations  15.7 us (3%)
    ppermute x41, waiting for transfers between devices, swap(): return lax.ppermute(rows, axis, [(i, i ^ bit) for i in range(size)])  135 us
    pallas_call x18, Pallas kernels, call(): pl.pallas_call(kernel, out_shape=shaped(*outs), scratch_shapes=list(scrat...  72.7 us
    pallas_call x4, Pallas kernels, weight_call(): pl.pallas_call(functools.partial(kernel, started), out_shape=tuple((jax.S...  61 us
    unnamed x282, local copies, waits for them, and re-layouts  47.4 us
    all_gather x3, waiting for transfers between devices, gather_rows(): own = lax.all_gather(half, 'blk', axis=0, tiled=True)  39.8 us
    ppermute x41, starting transfers between devices, swap(): return lax.ppermute(rows, axis, [(i, i ^ bit) for i in range(size)])  32.1 us
    ppermute x6, starting transfers between devices, gather_pairs(): slots.append(lax.ppermute(rows, 'blk', pairs) if far else rows)  29.5 us
    all_to_all x1, starting transfers between devices, sum_blocks(): lax.all_to_all(partial, 'blk', 0, 0, tiled=True)  25.2 us
  transfers between devices with their start and end apart: 60, of which 34 were waited for; matrix products, arithmetic and copies ran while one was open for 5% of the time, Pallas kernels for 27%

profile of v2, /device:TPU:0, one launch (start us, length us, event | category | flops | bytes accessed | tf_op | source)
XLA Modules:
  0.0 533.8 jit_solution(3106046347335024841)
XLA Ops:
  16.4 4.9 collective-permute-start.1
  21.3 4.5 collective-permute-start.3
  35.5 3.8 collective-permute-done.2.refs_3_
  39.2 4.2 collective-permute-done.4.refs_5_.refs_1_
  43.5 2.5 collective-permute-done.6.refs_7_.refs_3_
  47.2 3.5 attend.2
  55.6 9.7 %collective-permute-done.8 = bf16[128,1536]{1,0:T(8,128)(2,1)S(1)} collective-permute-done((bf16[128,1536]{1,0:T(8,128)(2,1)S(1)}, bf16[128,1536]{1,0:T(8,128)(2,1)S(1)}, u32[]{:S(2)}, u32[]{:S(2)}) %collective-permute-start.8) | collective-permute-done | bytes 393248 | tf_op jit(solution)/shard_map/ppermute | solution.py:72
  67.1 7.3 %feed_forward.1 = (f32[256,1536]{1,0:T(8,128)S(1)}, bf16[256,1536]{1,0:T(8,128)(2,1)S(1)}, bf16[128,3072]{1,0:T(8,128)(2,1)}, bf16[128,1536]{1,0:T(8,128)(2,1)S(1)}, f32[128,1536]{1,0:T(8,128)S(1)}) custom-call(s32[2]{0:T(128)S(1)} %pad_add_fusion.info, bf16[256,1536]{1,0:T(8,128)(2,1)S(1)} %copy-done.38, bf16[128,1536]{1,0:T(8,128)(2,1)S(1)} %add_convert_fusion.17.whole, ...), custom_call_target="tpu_custom_call" | custom-call | flops 7699999744 | tf_op jit(solution)/shard_map/feed_forward/pallas_call | solution.py:174
  81.0 9.7 %collective-permute-done.11 = bf16[128,1536]{1,0:T(8,128)(2,1)S(1)} collective-permute-done((bf16[128,1536]{1,0:T(8,128)(2,1)S(1)}, bf16[128,1536]{1,0:T(8,128)(2,1)S(1)}, u32[]{:S(2)}, u32[]{:S(2)}) %collective-permute-start.11) | collective-permute-done | bytes 393248 | tf_op jit(solution)/shard_map/ppermute | solution.py:72
  96.9 2.9 front.3
  100.7 8.8 %collective-permute-start.14 = (bf16[256,384]{1,0:T(8,128)(2,1)S(1)}, bf16[256,384]{1,0:T(8,128)(2,1)S(1)}, u32[]{:S(2)}, u32[]{:S(2)}) collective-permute-start(bf16[256,384]{1,0:T(8,128)(2,1)S(1)} %get-tuple-element.172.refs_0_), channel_id=1, source_target_pairs={{0,8},{4,12},{8,16},{12,20},{16,24},{20,28},{1,9},{5,13},{9,17},{1... | collective-permute-start | bytes 589832 | tf_op jit(solution)/shard_map/ppermute | solution.py:98
  109.5 8.7 %collective-permute-start.16 = (bf16[256,384]{1,0:T(8,128)(2,1)S(1)}, bf16[256,384]{1,0:T(8,128)(2,1)S(1)}, u32[]{:S(2)}, u32[]{:S(2)}) collective-permute-start(bf16[256,384]{1,0:T(8,128)(2,1)S(1)} %get-tuple-element.172.refs_0_), channel_id=1, source_target_pairs={{0,16},{4,20},{8,24},{12,28},{1,17},{5,21},{9,25},{13,29},{2,18},{... | collective-permute-start | bytes 589832 | tf_op jit(solution)/shard_map/ppermute | solution.py:98
  119.5 2.7 collective-permute-start.13
  122.3 5.3 collective-permute-done.16.refs_4_.refs_0_
  127.7 2.6 collective-permute-start.17
  130.3 5.6 %collective-permute-done.18.refs_6_.refs_2_ = bf16[256,384]{1,0:T(8,128)(2,1)S(1)} collective-permute-done((bf16[256,384]{1,0:T(8,128)(2,1)S(1)}, bf16[256,384]{1,0:T(8,128)(2,1)S(1)}, u32[]{:S(2)}, u32[]{:S(2)}) %collective-permute-start.18) | collective-permute-done | bytes 196640 | tf_op jit(solution)/shard_map/ppermute | solution.py:98
  138.3 4.8 collective-permute-done.19.refs_7_.refs_3_
  143.0 3.2 attend.3
  150.4 9.7 %collective-permute-done.21 = bf16[128,1536]{1,0:T(8,128)(2,1)S(1)} collective-permute-done((bf16[128,1536]{1,0:T(8,128)(2,1)S(1)}, bf16[128,1536]{1,0:T(8,128)(2,1)S(1)}, u32[]{:S(2)}, u32[]{:S(2)}) %collective-permute-start.21) | collective-permute-done | bytes 393248 | tf_op jit(solution)/shard_map/ppermute | solution.py:72
  162.0 9.5 %feed_both.1 = (f32[256,1536]{1,0:T(8,128)S(1)}, bf16[128,1536]{1,0:T(8,128)(2,1)}, bf16[128,1536]{1,0:T(8,128)(2,1)S(1)}, f32[128,1536]{1,0:T(8,128)S(1)}, bf16...) custom-call(s32[2]{0:T(128)S(1)} %pad_add_fusion.info, f32[256,1536]{1,0:T(8,128)S(1)} %get-tuple-element.171.base.rows, ...), custom_call_target="tpu_custom_call" | custom-call | flops 9900000256 | tf_op jit(solution)/shard_map/feed_both/pallas_call | solution.py:174
  175.8 9.7 %collective-permute-done.24 = bf16[128,1536]{1,0:T(8,128)(2,1)S(1)} collective-permute-done((bf16[128,1536]{1,0:T(8,128)(2,1)S(1)}, bf16[128,1536]{1,0:T(8,128)(2,1)S(1)}, u32[]{:S(2)}, u32[]{:S(2)}) %collective-permute-start.24) | collective-permute-done | bytes 393248 | tf_op jit(solution)/shard_map/ppermute | solution.py:72
  185.6 18.4 %all-gather.4.cloned.1.call-done.rows.incoming = bf16[1024,3072]{1,0:T(8,128)(2,1)} async-done(((bf16[128,3072]{1,0:T(8,128)(2,1)}), bf16[1024,3072]{1,0:T(8,128)(2,1)}) %all-gather.4.cloned.1.call-update) | async-done | bytes 6291472 | tf_op jit(solution)/shard_map/all_gather | solution.py:133
  206.5 3.1 middle_back.2
  211.8 3.3 attend_back.5
  221.4 8.2 %collective-permute-done.32 = bf16[128,1536]{1,0:T(8,128)(2,1)} collective-permute-done((bf16[128,1536]{1,0:T(8,128)(2,1)}, bf16[128,1536]{1,0:T(8,128)(2,1)}, u32[]{:S(2)}, u32[]{:S(2)}) %collective-permute-start.32) | collective-permute-done | bytes 393248 | tf_op jit(solution)/shard_map/ppermute | solution.py:72
  234.2 5.2 collective-permute-done.26
  241.9 10.7 %feedforward_prepare.2 = (bf16[1024,1024]{1,0:T(8,128)(2,1)S(1)}, bf16[1024,1024]{1,0:T(8,128)(2,1)S(1)}, bf16[1024,1024]{1,0:T(8,128)(2,1)}) custom-call(bf16[1024,3072]{1,0:T(8,128)(2,1)} %all-gather.4.cloned.1.call-done.rows.incoming, bf16[1536,1024]{1,0:T(8,128)(2,1)} %gate_weight.11, bf16[1536,1024]{1,0:T(8,128)(2,1)} %up_weight.11), custom_call_target="tpu_custom_call" | custom-call | flops 12099999744 | tf_op jit(solution)/shard_map/feedforward_prepare/pallas_call | solution.py:885
  255.3 10.9 %feedforward_prepare.3 = (bf16[1024,1024]{1,0:T(8,128)(2,1)S(1)}, bf16[1024,1024]{1,0:T(8,128)(2,1)S(1)}, bf16[1024,1024]{1,0:T(8,128)(2,1)}) custom-call(bf16[1024,3072]{1,0:T(8,128)(2,1)} %collective-permute-done.34.rows.incoming, bf16[1536,1024]{1,0:T(8,128)(2,1)} %gate_weight.11, bf16[1536,1024]{1,0:T(8,128)(2,1)} %up_weight.11), custom_call_target="tpu_custom_call" | custom-call | flops 12099999744 | tf_op jit(solution)/shard_map/feedforward_prepare/pallas_call | solution.py:885
  273.7 4.6 attention_weights.2
  278.3 3.7 collective-permute-done.36
  283.9 12.5 %feed_back.1 = (f32[256,1536]{1,0:T(8,128)S(1)}, bf16[128,1536]{1,0:T(8,128)(2,1)}, f32[1,1536]{1,0:T(1,128)S(1)}, bf16[128,1536]{1,0:T(8,128)(2,1)S(1)}, f32[128,1536]{1,0:T(8,128)S(1)}) custom-call(s32[2]{0:T(128)S(1)} %pad_add_fusion.info, f32[256,1536]{1,0:T(8,128)S(1)} %copy-done.87, f32[1,1536]{1,0:T(1,128)S(1)} %reshape.104.refs_2_.gain, ...), custom_call_target="tpu_custom_call" | custom-call | flops 13200000000 | tf_op jit(solution)/shard_map/feed_back/pallas_call | solution.py:174
  298.8 10.6 %collective-permute-done.39 = bf16[128,1536]{1,0:T(8,128)(2,1)S(1)} collective-permute-done((bf16[128,1536]{1,0:T(8,128)(2,1)S(1)}, bf16[128,1536]{1,0:T(8,128)(2,1)S(1)}, u32[]{:S(2)}, u32[]{:S(2)}) %collective-permute-start.39) | collective-permute-done | bytes 393248 | tf_op jit(solution)/shard_map/ppermute | solution.py:72
  316.7 2.5 middle_back.3
  323.6 3.8 attend_back.7
  329.9 21.4 %all-gather.6.cloned.1.call-done.rows = bf16[1024,1536]{1,0:T(8,128)(2,1)} async-done(((bf16[128,1536]{1,0:T(8,128)(2,1)}), bf16[1024,1536]{1,0:T(8,128)(2,1)}) %all-gather.6.cloned.1.call-update) | async-done | bytes 3145744 | tf_op jit(solution)/shard_map/all_gather | solution.py:133
  358.0 18.5 %feedforward_weights.2 = (f32[256,1024]{1,0:T(8,128)S(1)}, f32[256,1024]{1,0:T(8,128)S(1)}, f32[1024,256]{1,0:T(8,128)S(1)}) custom-call(s32[2]{0:T(128)S(1)} %pad_add_fusion.1.scalars, bf16[1024,1536]{1,0:T(8,128)(2,1)} %all-gather.6.cloned.1.call-done.rows, bf16[1024,3072]{1,0:T(8,128)(2,1)} %all-gather.4.cloned.1.call-done.rows.incoming, ...), custom_call_target="tpu_custom_call" | custom-call | flops 19249999872 | tf_op jit(solution)/shard_map/feedforward_weights/pallas_call | solution.py:827
  379.7 18.9 %collective-permute-done.52 = bf16[768,1152]{1,0:T(8,128)(2,1)S(1)} collective-permute-done((bf16[768,1152]{1,0:T(8,128)(2,1)}, bf16[768,1152]{1,0:T(8,128)(2,1)S(1)}, u32[]{:S(2)}, u32[]{:S(2)}) %collective-permute-start.52) | collective-permute-done | bytes 1769504 | tf_op jit(solution)/shard_map/ppermute | solution.py:72
  402.1 25.2 %all-to-all-start.1 = ((bf16[8,192,384]{2,1,0:T(8,128)(2,1)}), bf16[8,192,384]{2,1,0:T(8,128)(2,1)}, u32[]{:S(2)}, u32[]{:S(2)}) async-start(bf16[8,192,384]{2,1,0:T(8,128)(2,1)} %bitcast.25), calls=%async_computation.2 | async-start | bytes 2359296 | tf_op jit(solution)/shard_map/all_to_all | solution.py:117
  432.4 19.8 %feedforward_weights.3 = (f32[192,1024]{1,0:T(8,128)}, f32[192,1024]{1,0:T(8,128)}, f32[1024,192]{1,0:T(8,128)S(1)}) custom-call(s32[2]{0:T(128)S(1)} %copy-done.82, bf16[1024,1536]{1,0:T(8,128)(2,1)} %collective-permute-done.48.rows, bf16[1024,3072]{1,0:T(8,128)(2,1)} %collective-permute-done.34.rows.incoming, bf16[1536,1024]{1,0:T(8,128)(2,1)} %gate_weight.13, ...), custom_call_target="tpu_custom_call" | custom-call | flops 19249999872 | tf_op jit(solution)/shard_map/feedforward_weights/pallas_call | solution.py:827
  452.3 4.9 attention_weights.3
  463.0 3.4 collective-permute-done.49.other
  467.8 3.1 inputs_back.1
  470.8 12.0 %collective-permute-done.51 = bf16[768,768]{1,0:T(8,128)(2,1)} collective-permute-done((bf16[768,768]{1,0:T(8,128)(2,1)}, bf16[768,768]{1,0:T(8,128)(2,1)}, u32[]{:S(2)}, u32[]{:S(2)}) %collective-permute-start.51) | collective-permute-done | bytes 1179680 | tf_op jit(solution)/shard_map/ppermute | solution.py:72
  482.8 2.6 add_convert_fusion.1
  490.6 10.3 %feedforward_finish.2 = (f32[256,1024]{1,0:T(8,128)S(1)}, f32[256,1024]{1,0:T(8,128)S(1)}, f32[1024,256]{1,0:T(8,128)S(1)}) custom-call(s32[2]{0:T(128)S(1)} %copy-done.82, bf16[1024,3072]{1,0:T(8,128)(2,1)} %all-gather.4.cloned.1.call-done.rows.incoming, bf16[1024,1536]{1,0:T(8,128)(2,1)} %all-gather.8.cloned.1.call-done.incoming, ...), custom_call_target="tpu_custom_call" | custom-call | flops 11550000128 | tf_op jit(solution)/shard_map/feedforward_finish/pallas_call | solution.py:827
  500.9 12.4 %feedforward_finish.3 = (f32[192,1024]{1,0:T(8,128)}, f32[192,1024]{1,0:T(8,128)}, f32[1024,192]{1,0:T(8,128)S(1)}) custom-call(s32[2]{0:T(128)S(1)} %copy-done.82, bf16[1024,3072]{1,0:T(8,128)(2,1)} %collective-permute-done.34.rows.incoming, bf16[1024,1536]{1,0:T(8,128)(2,1)} %collective-permute-done.50.incoming, bf16[1024,1024]{1,0:T(8,128)(2,1)} %copy-done.115, ...), custom_call_target="tpu_custom_call" | custom-call | flops 11550000128 | tf_op jit(solution)/shard_map/feedforward_finish/pallas_call | solution.py:827
  514.0 5.7 %all-to-all-start = ((f32[8,4,192]{2,1,0:T(4,128)}), f32[8,4,192]{2,1,0:T(4,128)S(1)}, u32[]{:S(2)}, u32[]{:S(2)}) async-start(f32[8,4,192]{2,1,0:T(4,128)} %copy.86), calls=%async_computation | async-start | bytes 65536 | tf_op jit(solution)/shard_map/all_to_all | solution.py:1038
  523.6 2.8 all-to-all-done
  (432 shorter events, 135.9 us)
Async XLA Ops:
  7.2 196.8 %all-gather.4.cloned.1.call-start = ((), (), s32[]{:S(2)}) async-start(), calls=%async_computation.4 | async-start | bytes 7077888 | tf_op jit(solution)/shard_map/all_gather | solution.py:133
  16.4 12.4 %collective-permute-start.1 = (bf16[256,384]{1,0:T(8,128)(2,1)S(1)}, bf16[256,384]{1,0:T(8,128)(2,1)S(1)}, u32[]{:S(2)}, u32[]{:S(2)}) collective-permute-start(bf16[256,384]{1,0:T(8,128)(2,1)S(1)} %get-tuple-element.164.refs_0_), channel_id=1, source_target_pairs={{0,8},{4,12},{8,16},{12,20},{16,24},{20,28},{1,9},{5,13},{9,17},{1... | collective-permute-start | bytes 589832 | tf_op jit(solution)/shard_map/ppermute | solution.py:98
  21.3 9.8 %collective-permute-start.3 = (bf16[256,384]{1,0:T(8,128)(2,1)S(1)}, bf16[256,384]{1,0:T(8,128)(2,1)S(1)}, u32[]{:S(2)}, u32[]{:S(2)}) collective-permute-start(bf16[256,384]{1,0:T(8,128)(2,1)S(1)} %get-tuple-element.164.refs_0_), channel_id=1, source_target_pairs={{0,16},{4,20},{8,24},{12,28},{1,17},{5,21},{9,25},{13,29},{2,18},{... | collective-permute-start | bytes 589832 | tf_op jit(solution)/shard_map/ppermute | solution.py:98
  25.8 8.1 %collective-permute-start.5 = (bf16[256,384]{1,0:T(8,128)(2,1)S(1)}, bf16[256,384]{1,0:T(8,128)(2,1)S(1)}, u32[]{:S(2)}, u32[]{:S(2)}) collective-permute-start(bf16[256,384]{1,0:T(8,128)(2,1)S(1)} %get-tuple-element.164.refs_0_), channel_id=1, source_target_pairs={{0,24},{4,28},{1,25},{5,29},{2,26},{6,30},{3,27},{7,31}} | collective-permute-start | bytes 589832 | tf_op jit(solution)/shard_map/ppermute | solution.py:98
  27.1 8.3 %collective-permute-start = (bf16[256,384]{1,0:T(8,128)(2,1)S(1)}, bf16[256,384]{1,0:T(8,128)(2,1)S(1)}, u32[]{:S(2)}, u32[]{:S(2)}) collective-permute-start(bf16[256,384]{1,0:T(8,128)(2,1)S(1)} %get-tuple-element.164.refs_0_), channel_id=1, source_target_pairs={{0,4},{4,0},{8,12},{12,8},{16,20},{20,16},{24,28},{28,24},{1,5},{5... | collective-permute-start | bytes 589832 | tf_op jit(solution)/shard_map/ppermute | solution.py:72
  28.7 10.5 %collective-permute-start.2 = (bf16[256,384]{1,0:T(8,128)(2,1)S(1)}, bf16[256,384]{1,0:T(8,128)(2,1)S(1)}, u32[]{:S(2)}, u32[]{:S(2)}) collective-permute-start(bf16[256,384]{1,0:T(8,128)(2,1)S(1)} %collective-permute-done.1.refs_2_), channel_id=1, source_target_pairs={{0,4},{4,0},{8,12},{12,8},{16,20},{20,16},{24,28},{28,24},{1,5},{5... | collective-permute-start | bytes 589832 | tf_op jit(solution)/shard_map/ppermute | solution.py:72
  31.1 12.3 %collective-permute-start.4 = (bf16[256,384]{1,0:T(8,128)(2,1)S(1)}, bf16[256,384]{1,0:T(8,128)(2,1)S(1)}, u32[]{:S(2)}, u32[]{:S(2)}) collective-permute-start(bf16[256,384]{1,0:T(8,128)(2,1)S(1)} %collective-permute-done.3.refs_4_.refs_0_), channel_id=1, source_target_pairs={{0,4},{4,0},{8,12},{12,8},{16,20},{20,16},{24,28},{28,24},{1,5},{5... | collective-permute-start | bytes 589832 | tf_op jit(solution)/shard_map/ppermute | solution.py:72
  33.9 12.0 %collective-permute-start.6 = (bf16[256,384]{1,0:T(8,128)(2,1)S(1)}, bf16[256,384]{1,0:T(8,128)(2,1)S(1)}, u32[]{:S(2)}, u32[]{:S(2)}) collective-permute-start(bf16[256,384]{1,0:T(8,128)(2,1)S(1)} %collective-permute-done.5.refs_6_.refs_2_), channel_id=1, source_target_pairs={{0,4},{4,0},{8,12},{12,8},{16,20},{20,16},{24,28},{28,24},{1,5},{5... | collective-permute-start | bytes 589832 | tf_op jit(solution)/shard_map/ppermute | solution.py:72
  54.0 11.2 %collective-permute-start.8 = (bf16[128,1536]{1,0:T(8,128)(2,1)S(1)}, bf16[128,1536]{1,0:T(8,128)(2,1)S(1)}, u32[]{:S(2)}, u32[]{:S(2)}) collective-permute-start(bf16[128,1536]{1,0:T(8,128)(2,1)S(1)} %add_convert_fusion.18), channel_id=1, source_target_pairs={{0,2},{1,3},{2,0},{3,1},{4,6},{5,7},{6,4},{7,5},{8,10},{9,11},{10,... | collective-permute-start | bytes 1179656 | tf_op jit(solution)/shard_map/ppermute | solution.py:72
  77.3 274.0 %all-gather.6.cloned.1.call-start = ((), (), s32[]{:S(2)}) async-start(), calls=%async_computation.5 | async-start | bytes 3538944 | tf_op jit(solution)/shard_map/all_gather | solution.py:133
  79.4 11.2 %collective-permute-start.11 = (bf16[128,1536]{1,0:T(8,128)(2,1)S(1)}, bf16[128,1536]{1,0:T(8,128)(2,1)S(1)}, u32[]{:S(2)}, u32[]{:S(2)}) collective-permute-start(bf16[128,1536]{1,0:T(8,128)(2,1)S(1)} %add_convert_fusion.16), channel_id=1, source_target_pairs={{0,2},{1,3},{2,0},{3,1},{4,6},{5,7},{6,4},{7,5},{8,10},{9,11},{10,... | collective-permute-start | bytes 1179656 | tf_op jit(solution)/shard_map/ppermute | solution.py:72
  100.7 21.5 %collective-permute-start.14 = (bf16[256,384]{1,0:T(8,128)(2,1)S(1)}, bf16[256,384]{1,0:T(8,128)(2,1)S(1)}, u32[]{:S(2)}, u32[]{:S(2)}) collective-permute-start(bf16[256,384]{1,0:T(8,128)(2,1)S(1)} %get-tuple-element.172.refs_0_), channel_id=1, source_target_pairs={{0,8},{4,12},{8,16},{12,20},{16,24},{20,28},{1,9},{5,13},{9,17},{1... | collective-permute-start | bytes 589832 | tf_op jit(solution)/shard_map/ppermute | solution.py:98
  109.5 18.1 %collective-permute-start.16 = (bf16[256,384]{1,0:T(8,128)(2,1)S(1)}, bf16[256,384]{1,0:T(8,128)(2,1)S(1)}, u32[]{:S(2)}, u32[]{:S(2)}) collective-permute-start(bf16[256,384]{1,0:T(8,128)(2,1)S(1)} %get-tuple-element.172.refs_0_), channel_id=1, source_target_pairs={{0,16},{4,20},{8,24},{12,28},{1,17},{5,21},{9,25},{13,29},{2,18},{... | collective-permute-start | bytes 589832 | tf_op jit(solution)/shard_map/ppermute | solution.py:98
  118.2 17.6 %collective-permute-start.18 = (bf16[256,384]{1,0:T(8,128)(2,1)S(1)}, bf16[256,384]{1,0:T(8,128)(2,1)S(1)}, u32[]{:S(2)}, u32[]{:S(2)}) collective-permute-start(bf16[256,384]{1,0:T(8,128)(2,1)S(1)} %get-tuple-element.172.refs_0_), channel_id=1, source_target_pairs={{0,24},{4,28},{1,25},{5,29},{2,26},{6,30},{3,27},{7,31}} | collective-permute-start | bytes 589832 | tf_op jit(solution)/shard_map/ppermute | solution.py:98
  119.5 18.7 %collective-permute-start.13 = (bf16[256,384]{1,0:T(8,128)(2,1)S(1)}, bf16[256,384]{1,0:T(8,128)(2,1)S(1)}, u32[]{:S(2)}, u32[]{:S(2)}) collective-permute-start(bf16[256,384]{1,0:T(8,128)(2,1)S(1)} %get-tuple-element.172.refs_0_), channel_id=1, source_target_pairs={{0,4},{4,0},{8,12},{12,8},{16,20},{20,16},{24,28},{28,24},{1,5},{5... | collective-permute-start | bytes 589832 | tf_op jit(solution)/shard_map/ppermute | solution.py:72
  122.2 16.0 %collective-permute-start.15 = (bf16[256,384]{1,0:T(8,128)(2,1)S(1)}, bf16[256,384]{1,0:T(8,128)(2,1)S(1)}, u32[]{:S(2)}, u32[]{:S(2)}) collective-permute-start(bf16[256,384]{1,0:T(8,128)(2,1)S(1)} %collective-permute-done.14.refs_2_), channel_id=1, source_target_pairs={{0,4},{4,0},{8,12},{12,8},{16,20},{20,16},{24,28},{28,24},{1,5},{5... | collective-permute-start | bytes 589832 | tf_op jit(solution)/shard_map/ppermute | solution.py:72
  127.7 10.6 %collective-permute-start.17 = (bf16[256,384]{1,0:T(8,128)(2,1)S(1)}, bf16[256,384]{1,0:T(8,128)(2,1)S(1)}, u32[]{:S(2)}, u32[]{:S(2)}) collective-permute-start(bf16[256,384]{1,0:T(8,128)(2,1)S(1)} %collective-permute-done.16.refs_4_.refs_0_), channel_id=1, source_target_pairs={{0,4},{4,0},{8,12},{12,8},{16,20},{20,16},{24,28},{28,24},{1,5},{5... | collective-permute-start | bytes 589832 | tf_op jit(solution)/shard_map/ppermute | solution.py:72
  135.9 7.2 %collective-permute-start.19 = (bf16[256,384]{1,0:T(8,128)(2,1)S(1)}, bf16[256,384]{1,0:T(8,128)(2,1)S(1)}, u32[]{:S(2)}, u32[]{:S(2)}) collective-permute-start(bf16[256,384]{1,0:T(8,128)(2,1)S(1)} %collective-permute-done.18.refs_6_.refs_2_), channel_id=1, source_target_pairs={{0,4},{4,0},{8,12},{12,8},{16,20},{20,16},{24,28},{28,24},{1,5},{5... | collective-permute-start | bytes 589832 | tf_op jit(solution)/shard_map/ppermute | solution.py:72
  148.9 11.2 %collective-permute-start.21 = (bf16[128,1536]{1,0:T(8,128)(2,1)S(1)}, bf16[128,1536]{1,0:T(8,128)(2,1)S(1)}, u32[]{:S(2)}, u32[]{:S(2)}) collective-permute-start(bf16[128,1536]{1,0:T(8,128)(2,1)S(1)} %add_convert_fusion.14), channel_id=1, source_target_pairs={{0,2},{1,3},{2,0},{3,1},{4,6},{5,7},{6,4},{7,5},{8,10},{9,11},{10,... | collective-permute-start | bytes 1179656 | tf_op jit(solution)/shard_map/ppermute | solution.py:72
  174.2 11.2 %collective-permute-start.24 = (bf16[128,1536]{1,0:T(8,128)(2,1)S(1)}, bf16[128,1536]{1,0:T(8,128)(2,1)S(1)}, u32[]{:S(2)}, u32[]{:S(2)}) collective-permute-start(bf16[128,1536]{1,0:T(8,128)(2,1)S(1)} %add_convert_fusion.12), channel_id=1, source_target_pairs={{0,2},{1,3},{2,0},{3,1},{4,6},{5,7},{6,4},{7,5},{8,10},{9,11},{10,... | collective-permute-start | bytes 1179656 | tf_op jit(solution)/shard_map/ppermute | solution.py:72
  185.6 18.5 %collective-permute-start.25 = (bf16[128,1536]{1,0:T(8,128)(2,1)S(1)}, bf16[128,1536]{1,0:T(8,128)(2,1)}, u32[]{:S(2)}, u32[]{:S(2)}) collective-permute-start(bf16[128,1536]{1,0:T(8,128)(2,1)S(1)} %add_convert_fusion.11.whole), channel_id=1, source_target_pairs={{0,1},{1,0},{2,3},{3,2},{4,5},{5,4},{6,7},{7,6},{8,9},{9,8},{10,11... | collective-permute-start | bytes 1179656 | tf_op jit(solution)/shard_map/ppermute | solution.py:72
  204.0 51.3 %collective-permute-start.34 = (bf16[1024,3072]{1,0:T(8,128)(2,1)}, bf16[1024,3072]{1,0:T(8,128)(2,1)}, u32[]{:S(2)}, u32[]{:S(2)}) collective-permute-start(bf16[1024,3072]{1,0:T(8,128)(2,1)} %all-gather.4.cloned.1.call-done.rows.incoming), channel_id=1, source_target_pairs={{0,1},{1,0},{2,3},{3,2},{4,5},{5,4},{6,7},{7,6},{8,9},{9,8},{10,11... | collective-permute-start | bytes 18874376 | tf_op jit(solution)/shard_map/ppermute | solution.py:72
  217.9 11.7 %collective-permute-start.32 = (bf16[128,1536]{1,0:T(8,128)(2,1)}, bf16[128,1536]{1,0:T(8,128)(2,1)}, u32[]{:S(2)}, u32[]{:S(2)}) collective-permute-start(bf16[128,1536]{1,0:T(8,128)(2,1)} %add_convert_fusion.10), channel_id=1, source_target_pairs={{0,2},{1,3},{2,0},{3,1},{4,6},{5,7},{6,4},{7,5},{8,10},{9,11},{10,... | collective-permute-start | bytes 1179656 | tf_op jit(solution)/shard_map/ppermute | solution.py:72
  219.3 12.1 %collective-permute-start.28 = (bf16[512,384]{1,0:T(8,128)(2,1)}, bf16[512,384]{1,0:T(8,128)(2,1)S(1)}, u32[]{:S(2)}, u32[]{:S(2)}) collective-permute-start(bf16[512,384]{1,0:T(8,128)(2,1)} %copy-done.44), channel_id=1, source_target_pairs={{0,4},{4,0},{8,12},{12,8},{16,20},{20,16},{24,28},{28,24},{1,5},{5... | collective-permute-start | bytes 1179656 | tf_op jit(solution)/shard_map/ppermute | solution.py:72
  221.4 18.0 %collective-permute-start.26 = (bf16[512,384]{1,0:T(8,128)(2,1)}, bf16[512,384]{1,0:T(8,128)(2,1)S(1)}, u32[]{:S(2)}, u32[]{:S(2)}) collective-permute-start(bf16[512,384]{1,0:T(8,128)(2,1)} %copy-done.43), channel_id=1, source_target_pairs={{0,4},{4,0},{8,12},{12,8},{16,20},{20,16},{24,28},{28,24},{1,5},{5... | collective-permute-start | bytes 1179656 | tf_op jit(solution)/shard_map/ppermute | solution.py:72
  230.8 10.0 %collective-permute-start.33 = (bf16[128,1536]{1,0:T(8,128)(2,1)S(1)}, bf16[128,1536]{1,0:T(8,128)(2,1)S(1)}, u32[]{:S(2)}, u32[]{:S(2)}) collective-permute-start(bf16[128,1536]{1,0:T(8,128)(2,1)S(1)} %add_convert_fusion.9), channel_id=1, source_target_pairs={{0,1},{1,0},{2,3},{3,2},{4,5},{5,4},{6,7},{7,6},{8,9},{9,8},{10,11... | collective-permute-start | bytes 1179656 | tf_op jit(solution)/shard_map/ppermute | solution.py:72
  231.6 34.6 %collective-permute-start.29 = (bf16[256,384]{1,0:T(8,128)(2,1)S(1)}, bf16[256,384]{1,0:T(8,128)(2,1)S(1)}, u32[]{:S(2)}, u32[]{:S(2)}) collective-permute-start(bf16[256,384]{1,0:T(8,128)(2,1)S(1)} %get-tuple-element.393), channel_id=1, source_target_pairs={{16,0},{20,4},{24,8},{28,12},{17,1},{21,5},{25,9},{29,13},{18,2},{... | collective-permute-start | bytes 589832 | tf_op jit(solution)/shard_map/ppermute | solution.py:111
  232.9 33.4 %collective-permute-start.30 = (bf16[256,384]{1,0:T(8,128)(2,1)S(1)}, bf16[256,384]{1,0:T(8,128)(2,1)S(1)}, u32[]{:S(2)}, u32[]{:S(2)}) collective-permute-start(bf16[256,384]{1,0:T(8,128)(2,1)S(1)} %get-tuple-element.392), channel_id=1, source_target_pairs={{24,0},{28,4},{25,1},{29,5},{26,2},{30,6},{27,3},{31,7}} | collective-permute-start | bytes 589832 | tf_op jit(solution)/shard_map/ppermute | solution.py:111
  239.4 26.8 %collective-permute-start.27 = (bf16[256,384]{1,0:T(8,128)(2,1)S(1)}, bf16[256,384]{1,0:T(8,128)(2,1)S(1)}, u32[]{:S(2)}, u32[]{:S(2)}) collective-permute-start(bf16[256,384]{1,0:T(8,128)(2,1)S(1)} %get-tuple-element.394), channel_id=1, source_target_pairs={{8,0},{12,4},{16,8},{20,12},{24,16},{28,20},{9,1},{13,5},{17,9},{2... | collective-permute-start | bytes 589832 | tf_op jit(solution)/shard_map/ppermute | solution.py:111
  269.0 191.0 %all-gather.8.cloned.1.call-start = ((), (), s32[]{:S(2)}) async-start(), calls=%async_computation.6 | async-start | bytes 3538944 | tf_op jit(solution)/shard_map/all_gather | solution.py:133
  270.7 11.2 %collective-permute-start.36 = (bf16[128,1536]{1,0:T(8,128)(2,1)S(1)}, bf16[128,1536]{1,0:T(8,128)(2,1)S(1)}, u32[]{:S(2)}, u32[]{:S(2)}) collective-permute-start(bf16[128,1536]{1,0:T(8,128)(2,1)S(1)} %add_convert_fusion.8), channel_id=1, source_target_pairs={{0,2},{1,3},{2,0},{3,1},{4,6},{5,7},{6,4},{7,5},{8,10},{9,11},{10,... | collective-permute-start | bytes 1179656 | tf_op jit(solution)/shard_map/ppermute | solution.py:72
  298.2 11.2 %collective-permute-start.39 = (bf16[128,1536]{1,0:T(8,128)(2,1)S(1)}, bf16[128,1536]{1,0:T(8,128)(2,1)S(1)}, u32[]{:S(2)}, u32[]{:S(2)}) collective-permute-start(bf16[128,1536]{1,0:T(8,128)(2,1)S(1)} %add_convert_fusion.6), channel_id=1, source_target_pairs={{0,2},{1,3},{2,0},{3,1},{4,6},{5,7},{6,4},{7,5},{8,10},{9,11},{10,... | collective-permute-start | bytes 1179656 | tf_op jit(solution)/shard_map/ppermute | solution.py:72
  311.3 176.4 %reduce-scatter.5.cloned.1.call-start = ((), (), s32[]{:S(2)}) async-start(), calls=%async_computation.8 | async-start | bytes 2211840 | tf_op jit(solution)/shard_map/reduce_scatter | solution.py:127
  321.8 29.5 %collective-permute-start.43 = (bf16[512,384]{1,0:T(8,128)(2,1)}, bf16[512,384]{1,0:T(8,128)(2,1)}, u32[]{:S(2)}, u32[]{:S(2)}) collective-permute-start(bf16[512,384]{1,0:T(8,128)(2,1)} %get-tuple-element.239), channel_id=1, source_target_pairs={{0,4},{4,0},{8,12},{12,8},{16,20},{20,16},{24,28},{28,24},{1,5},{5... | collective-permute-start | bytes 1179656 | tf_op jit(solution)/shard_map/ppermute | solution.py:72
  328.1 27.0 %collective-permute-start.41 = (bf16[512,384]{1,0:T(8,128)(2,1)}, bf16[512,384]{1,0:T(8,128)(2,1)}, u32[]{:S(2)}, u32[]{:S(2)}) collective-permute-start(bf16[512,384]{1,0:T(8,128)(2,1)} %get-tuple-element.236), channel_id=1, source_target_pairs={{0,4},{4,0},{8,12},{12,8},{16,20},{20,16},{24,28},{28,24},{1,5},{5... | collective-permute-start | bytes 1179656 | tf_op jit(solution)/shard_map/ppermute | solution.py:72
  351.3 77.2 %collective-permute-start.48 = (bf16[1024,1536]{1,0:T(8,128)(2,1)}, bf16[1024,1536]{1,0:T(8,128)(2,1)}, u32[]{:S(2)}, u32[]{:S(2)}) collective-permute-start(bf16[1024,1536]{1,0:T(8,128)(2,1)} %all-gather.6.cloned.1.call-done.rows), channel_id=1, source_target_pairs={{0,1},{1,0},{2,3},{3,2},{4,5},{5,4},{6,7},{7,6},{8,9},{9,8},{10,11... | collective-permute-start | bytes 9437192 | tf_op jit(solution)/shard_map/ppermute | solution.py:72
  351.3 47.4 %collective-permute-start.52 = (bf16[768,1152]{1,0:T(8,128)(2,1)}, bf16[768,1152]{1,0:T(8,128)(2,1)S(1)}, u32[]{:S(2)}, u32[]{:S(2)}) collective-permute-start(bf16[768,1152]{1,0:T(8,128)(2,1)} %copy-done.25), channel_id=1, source_target_pairs={{0,4},{4,0},{8,12},{12,8},{16,20},{20,16},{24,28},{28,24},{1,5},{5... | collective-permute-start | bytes 5308424 | tf_op jit(solution)/shard_map/ppermute | solution.py:72
  352.4 24.1 %collective-permute-start.44 = (bf16[256,384]{1,0:T(8,128)(2,1)S(1)}, bf16[256,384]{1,0:T(8,128)(2,1)S(1)}, u32[]{:S(2)}, u32[]{:S(2)}) collective-permute-start(bf16[256,384]{1,0:T(8,128)(2,1)S(1)} %get-tuple-element.389), channel_id=1, source_target_pairs={{16,0},{20,4},{24,8},{28,12},{17,1},{21,5},{25,9},{29,13},{18,2},{... | collective-permute-start | bytes 589832 | tf_op jit(solution)/shard_map/ppermute | solution.py:111
  353.7 22.8 %collective-permute-start.45 = (bf16[256,384]{1,0:T(8,128)(2,1)S(1)}, bf16[256,384]{1,0:T(8,128)(2,1)S(1)}, u32[]{:S(2)}, u32[]{:S(2)}) collective-permute-start(bf16[256,384]{1,0:T(8,128)(2,1)S(1)} %get-tuple-element.388), channel_id=1, source_target_pairs={{24,0},{28,4},{25,1},{29,5},{26,2},{30,6},{27,3},{31,7}} | collective-permute-start | bytes 589832 | tf_op jit(solution)/shard_map/ppermute | solution.py:111
  356.2 20.3 %collective-permute-start.42 = (bf16[256,384]{1,0:T(8,128)(2,1)S(1)}, bf16[256,384]{1,0:T(8,128)(2,1)S(1)}, u32[]{:S(2)}, u32[]{:S(2)}) collective-permute-start(bf16[256,384]{1,0:T(8,128)(2,1)S(1)} %get-tuple-element.390), channel_id=1, source_target_pairs={{8,0},{12,4},{16,8},{20,12},{24,16},{28,20},{9,1},{13,5},{17,9},{2... | collective-permute-start | bytes 589832 | tf_op jit(solution)/shard_map/ppermute | solution.py:111
  379.2 48.1 %collective-permute-start.46 = (bf16[128,1536]{1,0:T(8,128)(2,1)S(1)}, bf16[128,1536]{1,0:T(8,128)(2,1)}, u32[]{:S(2)}, u32[]{:S(2)}) collective-permute-start(bf16[128,1536]{1,0:T(8,128)(2,1)S(1)} %get-tuple-element.252), channel_id=1, source_target_pairs={{0,1},{1,0},{2,3},{3,2},{4,5},{5,4},{6,7},{7,6},{8,9},{9,8},{10,11... | collective-permute-start | bytes 1179656 | tf_op jit(solution)/shard_map/ppermute | solution.py:72
  402.1 83.4 %all-to-all-start.1 = ((bf16[8,192,384]{2,1,0:T(8,128)(2,1)}), bf16[8,192,384]{2,1,0:T(8,128)(2,1)}, u32[]{:S(2)}, u32[]{:S(2)}) async-start(bf16[8,192,384]{2,1,0:T(8,128)(2,1)} %bitcast.25), calls=%async_computation.2 | async-start | bytes 2359296 | tf_op jit(solution)/shard_map/all_to_all | solution.py:117
  427.2 92.5 %reduce-scatter.3.cloned.1.call-start = ((), (), s32[]{:S(2)}) async-start(), calls=%async_computation.7 | async-start | bytes 1474560 | tf_op jit(solution)/shard_map/reduce_scatter | solution.py:127
  428.4 28.8 %collective-permute-start.47 = (bf16[128,1536]{1,0:T(8,128)(2,1)S(1)}, bf16[128,1536]{1,0:T(8,128)(2,1)S(1)}, u32[]{:S(2)}, u32[]{:S(2)}) collective-permute-start(bf16[128,1536]{1,0:T(8,128)(2,1)S(1)} %add_convert_fusion.4), channel_id=1, source_target_pairs={{0,2},{1,3},{2,0},{3,1},{4,6},{5,7},{6,4},{7,5},{8,10},{9,11},{10,... | collective-permute-start | bytes 1179656 | tf_op jit(solution)/shard_map/ppermute | solution.py:72
  458.0 24.9 %collective-permute-start.51 = (bf16[768,768]{1,0:T(8,128)(2,1)}, bf16[768,768]{1,0:T(8,128)(2,1)}, u32[]{:S(2)}, u32[]{:S(2)}) collective-permute-start(bf16[768,768]{1,0:T(8,128)(2,1)} %get-tuple-element.290), channel_id=1, source_target_pairs={{0,4},{4,0},{8,12},{12,8},{16,20},{20,16},{24,28},{28,24},{1,5},{5... | collective-permute-start | bytes 3538952 | tf_op jit(solution)/shard_map/ppermute | solution.py:72
  460.0 40.9 %collective-permute-start.50 = (bf16[1024,1536]{1,0:T(8,128)(2,1)}, bf16[1024,1536]{1,0:T(8,128)(2,1)}, u32[]{:S(2)}, u32[]{:S(2)}) collective-permute-start(bf16[1024,1536]{1,0:T(8,128)(2,1)} %all-gather.8.cloned.1.call-done.incoming), channel_id=1, source_target_pairs={{0,1},{1,0},{2,3},{3,2},{4,5},{5,4},{6,7},{7,6},{8,9},{9,8},{10,11... | collective-permute-start | bytes 9437192 | tf_op jit(solution)/shard_map/ppermute | solution.py:72
  461.2 5.1 collective-permute-start.49
  514.0 12.4 %all-to-all-start = ((f32[8,4,192]{2,1,0:T(4,128)}), f32[8,4,192]{2,1,0:T(4,128)S(1)}, u32[]{:S(2)}, u32[]{:S(2)}) async-start(f32[8,4,192]{2,1,0:T(4,128)} %copy.86), calls=%async_computation | async-start | bytes 65536 | tf_op jit(solution)/shard_map/all_to_all | solution.py:1038
  (149 other events, 1902.5 us)
Sparse Core Ops, SparseCore 0:
  77.4 126.5 all-gather.3
  269.1 82.1 all-gather.5
  354.0 75.5 all-gather.7
  431.8 51.8 reduce-scatter.4
  485.9 29.9 reduce-scatter.2

commit v3 on v2

--- a/solution.py
+++ b/solution.py
@@ -161,7 +161,7 @@
     )
 
 
-TIME_FLOPS = 1.1e9
+TIME_FLOPS = 1.3e9
 
 
 def shaped(*shapes):
@@ -962,11 +962,9 @@
         whole, other = sum_tp(tie(after, last_send)[1], last_keep)
         top, bottom = jnp.where(core == 0, whole, other), jnp.where(core == 0, other, whole)
         last = jnp.concatenate([top, bottom], axis=0).astype(F32)
-        prepared_own = prepare(rows_one[0], after)
-        prepared_other = prepare(rows_one[1], prepared_own[0])
-        return (hidden_two + last).astype(BF16), prepared_own, prepared_other
-
-    back_query, received, (result, prepared_own, prepared_other) = attention_back(
+        return (hidden_two + last).astype(BF16), prepare(rows_one[0], after)
+
+    back_query, received, (result, prepared_own) = attention_back(
         query_two, back_mixed, logs_two, delta, pairs_two, layout, heads, group, finish_forward
     )
     back_pair, send, keep = pair_back(received, back_query, two, layout)
@@ -998,7 +996,7 @@
         inputs_two, two[0], back_hidden, pieces, inner_in_one, one, layout
     )
 
-    pieces = sum_tp(send, keep)
+    pieces, prepared_other = sum_tp(send, keep, lambda after: prepare(rows_one[1], after))
     half_low, pieces = tie(half_low, pieces)
     early[0] = rows_two
     ends = gather_rows(half_low)

time: 542 us -> 529 us (0.976)
  starting transfers between devices: 101 us -> 86.7 us
  other arithmetic: 17.3 us -> 22.8 us
    all_gather x3, waiting for transfers between devices: 39.8 us -> 16.2 us  [gather_rows(): own = lax.all_gather(half, 'blk', axis=0, tiled=True)]
    reduce_scatter x2, waiting for transfers between devices: 0.01 us -> 20.4 us  [scatter_blocks(): lax.psum_scatter(both, 'blk', scatter_dimension=0, axis_index_groups=grou...]
    all_to_all x1, starting transfers between devices: 25.2 us -> 5.94 us  [sum_blocks(): lax.all_to_all(partial, 'blk', 0, 0, tiled=True)]
    ppermute x41, waiting for transfers between devices: 135 us -> 146 us  [swap(): return lax.ppermute(rows, axis, [(i, i ^ bit) for i in range(size)])]
    ppermute x6, waiting for transfers between devices: 14.1 us -> 5.24 us  [gather_pairs(): slots.append(lax.ppermute(rows, 'blk', pairs) if far else rows)]
    ppermute x41, starting transfers between devices: 32.1 us -> 38.2 us  [swap(): return lax.ppermute(rows, axis, [(i, i ^ bit) for i in range(size)])]
    unnamed x282 -> x274, local copies, waits for them, and re-layouts: 47.4 us -> 43.8 us
  transfers between devices with their start and end apart: 60 -> 60, of which waited for: 34 -> 36; matrix products, arithmetic and copies ran while one was open for 5% -> 6% of each run, Pallas kernels for 27% -> 27%
where the time goes in v3:
time: 529 us; the launch traced here: 521 us
  waiting for transfers between devices  191 us (36%)
  Pallas kernels  157 us (30%)
  starting transfers between devices  86.7 us (16%)
  local copies, waits for them, and re-layouts  45.9 us (9%)
  other arithmetic  22.8 us (4%)
  between operations  15.8 us (3%)
    ppermute x41, waiting for transfers between devices, swap(): return lax.ppermute(rows, axis, [(i, i ^ bit) for i in range(size)])  146 us
    pallas_call x18, Pallas kernels, call(): pl.pallas_call(kernel, out_shape=shaped(*outs), scratch_shapes=list(scrat...  72.5 us
    pallas_call x4, Pallas kernels, weight_call(): pl.pallas_call(functools.partial(kernel, started), out_shape=tuple((jax.S...  60.9 us
    unnamed x274, local copies, waits for them, and re-layouts  43.8 us
    ppermute x41, starting transfers between devices, swap(): return lax.ppermute(rows, axis, [(i, i ^ bit) for i in range(size)])  38.2 us
    ppermute x6, starting transfers between devices, gather_pairs(): slots.append(lax.ppermute(rows, 'blk', pairs) if far else rows)  29.7 us
    pallas_call x2, Pallas kernels, feedforward_prepare(): pl.pallas_call(feedforward_prepare_kernel, grid=(total // STEP,), out_sha...  21.7 us
    reduce_scatter x2, waiting for transfers between devices, scatter_blocks(): lax.psum_scatter(both, 'blk', scatter_dimension=0, axis_index_groups=grou...  20.4 us
  transfers between devices with their start and end apart: 60, of which 36 were waited for; matrix products, arithmetic and copies ran while one was open for 6% of the time, Pallas kernels for 27%

profile of v3, /device:TPU:0, one launch (start us, length us, event | category | flops | bytes accessed | tf_op | source)
XLA Modules:
  0.0 520.9 jit_solution(10419631733427402294)
XLA Ops:
  16.4 4.9 collective-permute-start.1
  21.3 4.5 collective-permute-start.3
  35.5 3.8 collective-permute-done.2.refs_3_
  39.3 4.2 collective-permute-done.4.refs_5_.refs_1_
  47.3 3.5 attend.2
  54.9 9.7 %collective-permute-done.8 = bf16[128,1536]{1,0:T(8,128)(2,1)S(1)} collective-permute-done((bf16[128,1536]{1,0:T(8,128)(2,1)S(1)}, bf16[128,1536]{1,0:T(8,128)(2,1)S(1)}, u32[]{:S(2)}, u32[]{:S(2)}) %collective-permute-start.8) | collective-permute-done | bytes 393248 | tf_op jit(solution)/shard_map/ppermute | solution.py:72
  66.5 7.3 %feed_forward.1 = (f32[256,1536]{1,0:T(8,128)S(1)}, bf16[256,1536]{1,0:T(8,128)(2,1)S(1)}, bf16[128,3072]{1,0:T(8,128)(2,1)}, bf16[128,1536]{1,0:T(8,128)(2,1)S(1)}, f32[128,1536]{1,0:T(8,128)S(1)}) custom-call(s32[2]{0:T(128)S(1)} %pad_add_fusion.info, bf16[256,1536]{1,0:T(8,128)(2,1)S(1)} %copy-done.35, bf16[128,1536]{1,0:T(8,128)(2,1)S(1)} %add_convert_fusion.17.whole, ...), custom_call_target="tpu_custom_call" | custom-call | flops 9100000256 | tf_op jit(solution)/shard_map/feed_forward/pallas_call | solution.py:174
  77.3 9.7 %collective-permute-done.11 = bf16[128,1536]{1,0:T(8,128)(2,1)S(1)} collective-permute-done((bf16[128,1536]{1,0:T(8,128)(2,1)S(1)}, bf16[128,1536]{1,0:T(8,128)(2,1)S(1)}, u32[]{:S(2)}, u32[]{:S(2)}) %collective-permute-start.11) | collective-permute-done | bytes 393248 | tf_op jit(solution)/shard_map/ppermute | solution.py:72
  92.1 2.8 front.3
  97.6 8.9 %collective-permute-start.14 = (bf16[256,384]{1,0:T(8,128)(2,1)S(1)}, bf16[256,384]{1,0:T(8,128)(2,1)S(1)}, u32[]{:S(2)}, u32[]{:S(2)}) collective-permute-start(bf16[256,384]{1,0:T(8,128)(2,1)S(1)} %get-tuple-element.173.refs_0_), channel_id=1, source_target_pairs={{0,8},{4,12},{8,16},{12,20},{16,24},{20,28},{1,9},{5,13},{9,17},{1... | collective-permute-start | bytes 589832 | tf_op jit(solution)/shard_map/ppermute | solution.py:98
  106.5 8.7 %collective-permute-start.16 = (bf16[256,384]{1,0:T(8,128)(2,1)S(1)}, bf16[256,384]{1,0:T(8,128)(2,1)S(1)}, u32[]{:S(2)}, u32[]{:S(2)}) collective-permute-start(bf16[256,384]{1,0:T(8,128)(2,1)S(1)} %get-tuple-element.173.refs_0_), channel_id=1, source_target_pairs={{0,16},{4,20},{8,24},{12,28},{1,17},{5,21},{9,25},{13,29},{2,18},{... | collective-permute-start | bytes 589832 | tf_op jit(solution)/shard_map/ppermute | solution.py:98
  116.5 2.7 collective-permute-start.13
  120.5 2.6 collective-permute-start.17
  124.0 2.6 collective-permute-start.19
  129.1 4.2 collective-permute-done.17.refs_5_.refs_1_
  133.4 3.5 collective-permute-done.19.refs_7_.refs_3_
  139.1 3.2 attend.3
  145.9 9.7 %collective-permute-done.21 = bf16[128,1536]{1,0:T(8,128)(2,1)S(1)} collective-permute-done((bf16[128,1536]{1,0:T(8,128)(2,1)S(1)}, bf16[128,1536]{1,0:T(8,128)(2,1)S(1)}, u32[]{:S(2)}, u32[]{:S(2)}) %collective-permute-start.21) | collective-permute-done | bytes 393248 | tf_op jit(solution)/shard_map/ppermute | solution.py:72
  157.5 9.6 %feed_both.1 = (f32[256,1536]{1,0:T(8,128)S(1)}, bf16[128,1536]{1,0:T(8,128)(2,1)}, bf16[128,1536]{1,0:T(8,128)(2,1)S(1)}, f32[128,1536]{1,0:T(8,128)S(1)}, bf16...) custom-call(s32[2]{0:T(128)S(1)} %pad_add_fusion.info, f32[256,1536]{1,0:T(8,128)S(1)} %copy-done.81, ...), custom_call_target="tpu_custom_call" | custom-call | flops 11699999744 | tf_op jit(solution)/shard_map/feed_both/pallas_call | solution.py:174
  170.4 9.7 %collective-permute-done.24 = bf16[128,1536]{1,0:T(8,128)(2,1)S(1)} collective-permute-done((bf16[128,1536]{1,0:T(8,128)(2,1)S(1)}, bf16[128,1536]{1,0:T(8,128)(2,1)S(1)}, u32[]{:S(2)}, u32[]{:S(2)}) %collective-permute-start.24) | collective-permute-done | bytes 393248 | tf_op jit(solution)/shard_map/ppermute | solution.py:72
  182.0 2.5 middle_back.2
  186.8 3.4 attend_back.5
  194.2 4.3 collective-permute-start.28
  198.6 5.6 %collective-permute-done.32 = bf16[128,1536]{1,0:T(8,128)(2,1)} collective-permute-done((bf16[128,1536]{1,0:T(8,128)(2,1)}, bf16[128,1536]{1,0:T(8,128)(2,1)}, u32[]{:S(2)}, u32[]{:S(2)}) %collective-permute-start.32) | collective-permute-done | bytes 393248 | tf_op jit(solution)/shard_map/ppermute | solution.py:72
  205.5 11.6 %collective-permute-done.28 = bf16[512,384]{1,0:T(8,128)(2,1)S(1)} collective-permute-done((bf16[512,384]{1,0:T(8,128)(2,1)}, bf16[512,384]{1,0:T(8,128)(2,1)S(1)}, u32[]{:S(2)}, u32[]{:S(2)}) %collective-permute-start.28) | collective-permute-done | bytes 393248 | tf_op jit(solution)/shard_map/ppermute | solution.py:72
  220.6 6.0 %collective-permute-done.26 = bf16[512,384]{1,0:T(8,128)(2,1)S(1)} collective-permute-done((bf16[512,384]{1,0:T(8,128)(2,1)}, bf16[512,384]{1,0:T(8,128)(2,1)S(1)}, u32[]{:S(2)}, u32[]{:S(2)}) %collective-permute-start.26) | collective-permute-done | bytes 393248 | tf_op jit(solution)/shard_map/ppermute | solution.py:72
  229.6 16.2 %all-gather.4.cloned.1.call-done.rows.incoming = bf16[1024,3072]{1,0:T(8,128)(2,1)} async-done(((bf16[128,3072]{1,0:T(8,128)(2,1)}), bf16[1024,3072]{1,0:T(8,128)(2,1)}) %all-gather.4.cloned.1.call-update) | async-done | bytes 6291472 | tf_op jit(solution)/shard_map/all_gather | solution.py:133
  248.1 10.9 %feedforward_prepare.2 = (bf16[1024,1024]{1,0:T(8,128)(2,1)S(1)}, bf16[1024,1024]{1,0:T(8,128)(2,1)S(1)}, bf16[1024,1024]{1,0:T(8,128)(2,1)}) custom-call(bf16[1024,3072]{1,0:T(8,128)(2,1)} %all-gather.4.cloned.1.call-done.rows.incoming, bf16[1536,1024]{1,0:T(8,128)(2,1)} %gate_weight.11, bf16[1536,1024]{1,0:T(8,128)(2,1)} %up_weight.11), custom_call_target="tpu_custom_call" | custom-call | flops 14300000256 | tf_op jit(solution)/shard_map/feedforward_prepare/pallas_call | solution.py:885
  264.1 2.6 collective-permute-start.35
  270.1 4.6 attention_weights.2
  279.8 12.5 %feed_back.1 = (f32[256,1536]{1,0:T(8,128)S(1)}, bf16[128,1536]{1,0:T(8,128)(2,1)}, f32[1,1536]{1,0:T(1,128)S(1)}, bf16[128,1536]{1,0:T(8,128)(2,1)S(1)}, f32[128,1536]{1,0:T(8,128)S(1)}) custom-call(s32[2]{0:T(128)S(1)} %pad_add_fusion.info, f32[256,1536]{1,0:T(8,128)S(1)} %copy-done.82, f32[1,1536]{1,0:T(1,128)S(1)} %reshape.104.refs_2_.gain, ...), custom_call_target="tpu_custom_call" | custom-call | flops 15600000000 | tf_op jit(solution)/shard_map/feed_back/pallas_call | solution.py:174
  295.9 10.8 %feedforward_prepare.3 = (bf16[1024,1024]{1,0:T(8,128)(2,1)S(1)}, bf16[1024,1024]{1,0:T(8,128)(2,1)S(1)}, bf16[1024,1024]{1,0:T(8,128)(2,1)}) custom-call(bf16[1024,3072]{1,0:T(8,128)(2,1)} %collective-permute-done.39.rows.incoming, bf16[1536,1024]{1,0:T(8,128)(2,1)} %gate_weight.11, bf16[1536,1024]{1,0:T(8,128)(2,1)} %up_weight.11), custom_call_target="tpu_custom_call" | custom-call | flops 14300000256 | tf_op jit(solution)/shard_map/feedforward_prepare/pallas_call | solution.py:885
  321.5 3.8 attend_back.7
  326.0 3.4 collective-permute-start.41
  329.6 4.1 collective-permute-done.43
  337.4 8.9 %collective-permute-done.41 = bf16[512,384]{1,0:T(8,128)(2,1)} collective-permute-done((bf16[512,384]{1,0:T(8,128)(2,1)}, bf16[512,384]{1,0:T(8,128)(2,1)}, u32[]{:S(2)}, u32[]{:S(2)}) %collective-permute-start.41) | collective-permute-done | bytes 393248 | tf_op jit(solution)/shard_map/ppermute | solution.py:72
  349.3 18.4 %feedforward_weights.2 = (f32[256,1024]{1,0:T(8,128)S(1)}, f32[256,1024]{1,0:T(8,128)S(1)}, f32[1024,256]{1,0:T(8,128)S(1)}) custom-call(s32[2]{0:T(128)S(1)} %pad_add_fusion.1.scalars, bf16[1024,1536]{1,0:T(8,128)(2,1)} %all-gather.6.cloned.1.call-done.rows, bf16[1024,3072]{1,0:T(8,128)(2,1)} %all-gather.4.cloned.1.call-done.rows.incoming, ...), custom_call_target="tpu_custom_call" | custom-call | flops 22749999104 | tf_op jit(solution)/shard_map/feedforward_weights/pallas_call | solution.py:827
  370.4 29.1 %collective-permute-done.52 = bf16[768,1152]{1,0:T(8,128)(2,1)S(1)} collective-permute-done((bf16[768,1152]{1,0:T(8,128)(2,1)}, bf16[768,1152]{1,0:T(8,128)(2,1)S(1)}, u32[]{:S(2)}, u32[]{:S(2)}) %collective-permute-start.52) | collective-permute-done | bytes 1769504 | tf_op jit(solution)/shard_map/ppermute | solution.py:72
  402.9 5.9 %all-to-all-start.1 = ((bf16[8,192,384]{2,1,0:T(8,128)(2,1)}), bf16[8,192,384]{2,1,0:T(8,128)(2,1)}, u32[]{:S(2)}, u32[]{:S(2)}) async-start(bf16[8,192,384]{2,1,0:T(8,128)(2,1)} %bitcast.25), calls=%async_computation.2 | async-start | bytes 2359296 | tf_op jit(solution)/shard_map/all_to_all | solution.py:117
  414.4 19.8 %feedforward_weights.3 = (f32[192,1024]{1,0:T(8,128)}, f32[192,1024]{1,0:T(8,128)}, f32[1024,192]{1,0:T(8,128)S(1)}) custom-call(s32[2]{0:T(128)S(1)} %copy-done.76, bf16[1024,1536]{1,0:T(8,128)(2,1)} %collective-permute-done.48.rows, bf16[1024,3072]{1,0:T(8,128)(2,1)} %collective-permute-done.39.rows.incoming, bf16[1536,1024]{1,0:T(8,128)(2,1)} %gate_weight.13, ...), custom_call_target="tpu_custom_call" | custom-call | flops 22749999104 | tf_op jit(solution)/shard_map/feedforward_weights/pallas_call | solution.py:827
  434.3 4.9 attention_weights.3
  443.8 20.4 %reduce-scatter.5.cloned.1.call-done.share = bf16[192,1152]{1,0:T(8,128)(2,1)} async-done(((bf16[768,1152]{1,0:T(8,128)(2,1)}), bf16[192,1152]{1,0:T(8,128)(2,1)}) %reduce-scatter.5.cloned.1.call-update) | async-done | bytes 442384 | tf_op jit(solution)/shard_map/reduce_scatter | solution.py:127
  470.7 3.1 inputs_back.1
  473.8 2.6 add_convert_fusion.1
  478.9 10.3 %feedforward_finish.2 = (f32[256,1024]{1,0:T(8,128)S(1)}, f32[256,1024]{1,0:T(8,128)S(1)}, f32[1024,256]{1,0:T(8,128)S(1)}) custom-call(s32[2]{0:T(128)S(1)} %copy-done.76, bf16[1024,3072]{1,0:T(8,128)(2,1)} %all-gather.4.cloned.1.call-done.rows.incoming, bf16[1024,1536]{1,0:T(8,128)(2,1)} %all-gather.8.cloned.1.call-done.incoming, ...), custom_call_target="tpu_custom_call" | custom-call | flops 13649999872 | tf_op jit(solution)/shard_map/feedforward_finish/pallas_call | solution.py:827
  489.2 12.4 %feedforward_finish.3 = (f32[192,1024]{1,0:T(8,128)}, f32[192,1024]{1,0:T(8,128)}, f32[1024,192]{1,0:T(8,128)S(1)}) custom-call(s32[2]{0:T(128)S(1)} %copy-done.76, bf16[1024,3072]{1,0:T(8,128)(2,1)} %collective-permute-done.39.rows.incoming, bf16[1024,1536]{1,0:T(8,128)(2,1)} %collective-permute-done.50.incoming, bf16[1024,1024]{1,0:T(8,128)(2,1)} %copy-done.112, ...), custom_call_target="tpu_custom_call" | custom-call | flops 13649999872 | tf_op jit(solution)/shard_map/feedforward_finish/pallas_call | solution.py:827
  502.3 4.5 all-to-all-start
  510.7 2.8 all-to-all-done
  (424 shorter events, 143.8 us)
Async XLA Ops:
  7.2 238.7 %all-gather.4.cloned.1.call-start = ((), (), s32[]{:S(2)}) async-start(), calls=%async_computation.4 | async-start | bytes 7077888 | tf_op jit(solution)/shard_map/all_gather | solution.py:133
  16.4 12.3 %collective-permute-start.1 = (bf16[256,384]{1,0:T(8,128)(2,1)S(1)}, bf16[256,384]{1,0:T(8,128)(2,1)S(1)}, u32[]{:S(2)}, u32[]{:S(2)}) collective-permute-start(bf16[256,384]{1,0:T(8,128)(2,1)S(1)} %get-tuple-element.165.refs_0_), channel_id=1, source_target_pairs={{0,8},{4,12},{8,16},{12,20},{16,24},{20,28},{1,9},{5,13},{9,17},{1... | collective-permute-start | bytes 589832 | tf_op jit(solution)/shard_map/ppermute | solution.py:98
  21.3 9.8 %collective-permute-start.3 = (bf16[256,384]{1,0:T(8,128)(2,1)S(1)}, bf16[256,384]{1,0:T(8,128)(2,1)S(1)}, u32[]{:S(2)}, u32[]{:S(2)}) collective-permute-start(bf16[256,384]{1,0:T(8,128)(2,1)S(1)} %get-tuple-element.165.refs_0_), channel_id=1, source_target_pairs={{0,16},{4,20},{8,24},{12,28},{1,17},{5,21},{9,25},{13,29},{2,18},{... | collective-permute-start | bytes 589832 | tf_op jit(solution)/shard_map/ppermute | solution.py:98
  25.8 8.1 %collective-permute-start.5 = (bf16[256,384]{1,0:T(8,128)(2,1)S(1)}, bf16[256,384]{1,0:T(8,128)(2,1)S(1)}, u32[]{:S(2)}, u32[]{:S(2)}) collective-permute-start(bf16[256,384]{1,0:T(8,128)(2,1)S(1)} %get-tuple-element.165.refs_0_), channel_id=1, source_target_pairs={{0,24},{4,28},{1,25},{5,29},{2,26},{6,30},{3,27},{7,31}} | collective-permute-start | bytes 589832 | tf_op jit(solution)/shard_map/ppermute | solution.py:98
  27.1 8.3 %collective-permute-start = (bf16[256,384]{1,0:T(8,128)(2,1)S(1)}, bf16[256,384]{1,0:T(8,128)(2,1)S(1)}, u32[]{:S(2)}, u32[]{:S(2)}) collective-permute-start(bf16[256,384]{1,0:T(8,128)(2,1)S(1)} %get-tuple-element.165.refs_0_), channel_id=1, source_target_pairs={{0,4},{4,0},{8,12},{12,8},{16,20},{20,16},{24,28},{28,24},{1,5},{5... | collective-permute-start | bytes 589832 | tf_op jit(solution)/shard_map/ppermute | solution.py:72
  28.7 10.5 %collective-permute-start.2 = (bf16[256,384]{1,0:T(8,128)(2,1)S(1)}, bf16[256,384]{1,0:T(8,128)(2,1)S(1)}, u32[]{:S(2)}, u32[]{:S(2)}) collective-permute-start(bf16[256,384]{1,0:T(8,128)(2,1)S(1)} %collective-permute-done.1.refs_2_), channel_id=1, source_target_pairs={{0,4},{4,0},{8,12},{12,8},{16,20},{20,16},{24,28},{28,24},{1,5},{5... | collective-permute-start | bytes 589832 | tf_op jit(solution)/shard_map/ppermute | solution.py:72
  31.1 12.3 %collective-permute-start.4 = (bf16[256,384]{1,0:T(8,128)(2,1)S(1)}, bf16[256,384]{1,0:T(8,128)(2,1)S(1)}, u32[]{:S(2)}, u32[]{:S(2)}) collective-permute-start(bf16[256,384]{1,0:T(8,128)(2,1)S(1)} %collective-permute-done.3.refs_4_.refs_0_), channel_id=1, source_target_pairs={{0,4},{4,0},{8,12},{12,8},{16,20},{20,16},{24,28},{28,24},{1,5},{5... | collective-permute-start | bytes 589832 | tf_op jit(solution)/shard_map/ppermute | solution.py:72
  33.9 12.0 %collective-permute-start.6 = (bf16[256,384]{1,0:T(8,128)(2,1)S(1)}, bf16[256,384]{1,0:T(8,128)(2,1)S(1)}, u32[]{:S(2)}, u32[]{:S(2)}) collective-permute-start(bf16[256,384]{1,0:T(8,128)(2,1)S(1)} %collective-permute-done.5.refs_6_.refs_2_), channel_id=1, source_target_pairs={{0,4},{4,0},{8,12},{12,8},{16,20},{20,16},{24,28},{28,24},{1,5},{5... | collective-permute-start | bytes 589832 | tf_op jit(solution)/shard_map/ppermute | solution.py:72
  53.4 11.2 %collective-permute-start.8 = (bf16[128,1536]{1,0:T(8,128)(2,1)S(1)}, bf16[128,1536]{1,0:T(8,128)(2,1)S(1)}, u32[]{:S(2)}, u32[]{:S(2)}) collective-permute-start(bf16[128,1536]{1,0:T(8,128)(2,1)S(1)} %add_convert_fusion.18), channel_id=1, source_target_pairs={{0,2},{1,3},{2,0},{3,1},{4,6},{5,7},{6,4},{7,5},{8,10},{9,11},{10,... | collective-permute-start | bytes 1179656 | tf_op jit(solution)/shard_map/ppermute | solution.py:72
  75.7 11.2 %collective-permute-start.11 = (bf16[128,1536]{1,0:T(8,128)(2,1)S(1)}, bf16[128,1536]{1,0:T(8,128)(2,1)S(1)}, u32[]{:S(2)}, u32[]{:S(2)}) collective-permute-start(bf16[128,1536]{1,0:T(8,128)(2,1)S(1)} %add_convert_fusion.16), channel_id=1, source_target_pairs={{0,2},{1,3},{2,0},{3,1},{4,6},{5,7},{6,4},{7,5},{8,10},{9,11},{10,... | collective-permute-start | bytes 1179656 | tf_op jit(solution)/shard_map/ppermute | solution.py:72
  87.1 2.0 collective-permute-start.12
  97.6 21.6 %collective-permute-start.14 = (bf16[256,384]{1,0:T(8,128)(2,1)S(1)}, bf16[256,384]{1,0:T(8,128)(2,1)S(1)}, u32[]{:S(2)}, u32[]{:S(2)}) collective-permute-start(bf16[256,384]{1,0:T(8,128)(2,1)S(1)} %get-tuple-element.173.refs_0_), channel_id=1, source_target_pairs={{0,8},{4,12},{8,16},{12,20},{16,24},{20,28},{1,9},{5,13},{9,17},{1... | collective-permute-start | bytes 589832 | tf_op jit(solution)/shard_map/ppermute | solution.py:98
  106.5 14.0 %collective-permute-start.16 = (bf16[256,384]{1,0:T(8,128)(2,1)S(1)}, bf16[256,384]{1,0:T(8,128)(2,1)S(1)}, u32[]{:S(2)}, u32[]{:S(2)}) collective-permute-start(bf16[256,384]{1,0:T(8,128)(2,1)S(1)} %get-tuple-element.173.refs_0_), channel_id=1, source_target_pairs={{0,16},{4,20},{8,24},{12,28},{1,17},{5,21},{9,25},{13,29},{2,18},{... | collective-permute-start | bytes 589832 | tf_op jit(solution)/shard_map/ppermute | solution.py:98
  115.2 8.8 %collective-permute-start.18 = (bf16[256,384]{1,0:T(8,128)(2,1)S(1)}, bf16[256,384]{1,0:T(8,128)(2,1)S(1)}, u32[]{:S(2)}, u32[]{:S(2)}) collective-permute-start(bf16[256,384]{1,0:T(8,128)(2,1)S(1)} %get-tuple-element.173.refs_0_), channel_id=1, source_target_pairs={{0,24},{4,28},{1,25},{5,29},{2,26},{6,30},{3,27},{7,31}} | collective-permute-start | bytes 589832 | tf_op jit(solution)/shard_map/ppermute | solution.py:98
  116.5 10.1 %collective-permute-start.13 = (bf16[256,384]{1,0:T(8,128)(2,1)S(1)}, bf16[256,384]{1,0:T(8,128)(2,1)S(1)}, u32[]{:S(2)}, u32[]{:S(2)}) collective-permute-start(bf16[256,384]{1,0:T(8,128)(2,1)S(1)} %get-tuple-element.173.refs_0_), channel_id=1, source_target_pairs={{0,4},{4,0},{8,12},{12,8},{16,20},{20,16},{24,28},{28,24},{1,5},{5... | collective-permute-start | bytes 589832 | tf_op jit(solution)/shard_map/ppermute | solution.py:72
  119.2 9.9 %collective-permute-start.15 = (bf16[256,384]{1,0:T(8,128)(2,1)S(1)}, bf16[256,384]{1,0:T(8,128)(2,1)S(1)}, u32[]{:S(2)}, u32[]{:S(2)}) collective-permute-start(bf16[256,384]{1,0:T(8,128)(2,1)S(1)} %collective-permute-done.14.refs_2_), channel_id=1, source_target_pairs={{0,4},{4,0},{8,12},{12,8},{16,20},{20,16},{24,28},{28,24},{1,5},{5... | collective-permute-start | bytes 589832 | tf_op jit(solution)/shard_map/ppermute | solution.py:72
  120.5 12.9 %collective-permute-start.17 = (bf16[256,384]{1,0:T(8,128)(2,1)S(1)}, bf16[256,384]{1,0:T(8,128)(2,1)S(1)}, u32[]{:S(2)}, u32[]{:S(2)}) collective-permute-start(bf16[256,384]{1,0:T(8,128)(2,1)S(1)} %collective-permute-done.16.refs_4_.refs_0_), channel_id=1, source_target_pairs={{0,4},{4,0},{8,12},{12,8},{16,20},{20,16},{24,28},{28,24},{1,5},{5... | collective-permute-start | bytes 589832 | tf_op jit(solution)/shard_map/ppermute | solution.py:72
  124.0 12.9 %collective-permute-start.19 = (bf16[256,384]{1,0:T(8,128)(2,1)S(1)}, bf16[256,384]{1,0:T(8,128)(2,1)S(1)}, u32[]{:S(2)}, u32[]{:S(2)}) collective-permute-start(bf16[256,384]{1,0:T(8,128)(2,1)S(1)} %collective-permute-done.18.refs_6_.refs_2_), channel_id=1, source_target_pairs={{0,4},{4,0},{8,12},{12,8},{16,20},{20,16},{24,28},{28,24},{1,5},{5... | collective-permute-start | bytes 589832 | tf_op jit(solution)/shard_map/ppermute | solution.py:72
  126.6 202.9 %all-gather.6.cloned.1.call-start = ((), (), s32[]{:S(2)}) async-start(), calls=%async_computation.5 | async-start | bytes 3538944 | tf_op jit(solution)/shard_map/all_gather | solution.py:133
  144.4 11.2 %collective-permute-start.21 = (bf16[128,1536]{1,0:T(8,128)(2,1)S(1)}, bf16[128,1536]{1,0:T(8,128)(2,1)S(1)}, u32[]{:S(2)}, u32[]{:S(2)}) collective-permute-start(bf16[128,1536]{1,0:T(8,128)(2,1)S(1)} %add_convert_fusion.14), channel_id=1, source_target_pairs={{0,2},{1,3},{2,0},{3,1},{4,6},{5,7},{6,4},{7,5},{8,10},{9,11},{10,... | collective-permute-start | bytes 1179656 | tf_op jit(solution)/shard_map/ppermute | solution.py:72
  168.9 11.2 %collective-permute-start.24 = (bf16[128,1536]{1,0:T(8,128)(2,1)S(1)}, bf16[128,1536]{1,0:T(8,128)(2,1)S(1)}, u32[]{:S(2)}, u32[]{:S(2)}) collective-permute-start(bf16[128,1536]{1,0:T(8,128)(2,1)S(1)} %add_convert_fusion.12), channel_id=1, source_target_pairs={{0,2},{1,3},{2,0},{3,1},{4,6},{5,7},{6,4},{7,5},{8,10},{9,11},{10,... | collective-permute-start | bytes 1179656 | tf_op jit(solution)/shard_map/ppermute | solution.py:72
  192.8 11.5 %collective-permute-start.32 = (bf16[128,1536]{1,0:T(8,128)(2,1)}, bf16[128,1536]{1,0:T(8,128)(2,1)}, u32[]{:S(2)}, u32[]{:S(2)}) collective-permute-start(bf16[128,1536]{1,0:T(8,128)(2,1)} %add_convert_fusion.10), channel_id=1, source_target_pairs={{0,2},{1,3},{2,0},{3,1},{4,6},{5,7},{6,4},{7,5},{8,10},{9,11},{10,... | collective-permute-start | bytes 1179656 | tf_op jit(solution)/shard_map/ppermute | solution.py:72
  194.2 22.9 %collective-permute-start.28 = (bf16[512,384]{1,0:T(8,128)(2,1)}, bf16[512,384]{1,0:T(8,128)(2,1)S(1)}, u32[]{:S(2)}, u32[]{:S(2)}) collective-permute-start(bf16[512,384]{1,0:T(8,128)(2,1)} %copy-done.39), channel_id=1, source_target_pairs={{0,4},{4,0},{8,12},{12,8},{16,20},{20,16},{24,28},{28,24},{1,5},{5... | collective-permute-start | bytes 1179656 | tf_op jit(solution)/shard_map/ppermute | solution.py:72
  198.6 28.0 %collective-permute-start.26 = (bf16[512,384]{1,0:T(8,128)(2,1)}, bf16[512,384]{1,0:T(8,128)(2,1)S(1)}, u32[]{:S(2)}, u32[]{:S(2)}) collective-permute-start(bf16[512,384]{1,0:T(8,128)(2,1)} %copy-done.38), channel_id=1, source_target_pairs={{0,4},{4,0},{8,12},{12,8},{16,20},{20,16},{24,28},{28,24},{1,5},{5... | collective-permute-start | bytes 1179656 | tf_op jit(solution)/shard_map/ppermute | solution.py:72
  205.5 23.2 %collective-permute-start.33 = (bf16[128,1536]{1,0:T(8,128)(2,1)S(1)}, bf16[128,1536]{1,0:T(8,128)(2,1)S(1)}, u32[]{:S(2)}, u32[]{:S(2)}) collective-permute-start(bf16[128,1536]{1,0:T(8,128)(2,1)S(1)} %add_convert_fusion.9), channel_id=1, source_target_pairs={{0,1},{1,0},{2,3},{3,2},{4,5},{5,4},{6,7},{7,6},{8,9},{9,8},{10,11... | collective-permute-start | bytes 1179656 | tf_op jit(solution)/shard_map/ppermute | solution.py:72
  218.0 41.0 %collective-permute-start.29 = (bf16[256,384]{1,0:T(8,128)(2,1)}, bf16[256,384]{1,0:T(8,128)(2,1)S(1)}, u32[]{:S(2)}, u32[]{:S(2)}) collective-permute-start(bf16[256,384]{1,0:T(8,128)(2,1)} %get-tuple-element.395), channel_id=1, source_target_pairs={{16,0},{20,4},{24,8},{28,12},{17,1},{21,5},{25,9},{29,13},{18,2},{... | collective-permute-start | bytes 589832 | tf_op jit(solution)/shard_map/ppermute | solution.py:111
  219.3 39.7 %collective-permute-start.30 = (bf16[256,384]{1,0:T(8,128)(2,1)}, bf16[256,384]{1,0:T(8,128)(2,1)}, u32[]{:S(2)}, u32[]{:S(2)}) collective-permute-start(bf16[256,384]{1,0:T(8,128)(2,1)} %get-tuple-element.394), channel_id=1, source_target_pairs={{24,0},{28,4},{25,1},{29,5},{26,2},{30,6},{27,3},{31,7}} | collective-permute-start | bytes 589832 | tf_op jit(solution)/shard_map/ppermute | solution.py:111
  227.4 31.6 %collective-permute-start.27 = (bf16[256,384]{1,0:T(8,128)(2,1)}, bf16[256,384]{1,0:T(8,128)(2,1)S(1)}, u32[]{:S(2)}, u32[]{:S(2)}) collective-permute-start(bf16[256,384]{1,0:T(8,128)(2,1)} %get-tuple-element.396), channel_id=1, source_target_pairs={{8,0},{12,4},{16,8},{20,12},{24,16},{28,20},{9,1},{13,5},{17,9},{2... | collective-permute-start | bytes 589832 | tf_op jit(solution)/shard_map/ppermute | solution.py:111
  245.9 50.0 %collective-permute-start.39 = (bf16[1024,3072]{1,0:T(8,128)(2,1)}, bf16[1024,3072]{1,0:T(8,128)(2,1)}, u32[]{:S(2)}, u32[]{:S(2)}) collective-permute-start(bf16[1024,3072]{1,0:T(8,128)(2,1)} %all-gather.4.cloned.1.call-done.rows.incoming), channel_id=1, source_target_pairs={{0,1},{1,0},{2,3},{3,2},{4,5},{5,4},{6,7},{7,6},{8,9},{9,8},{10,11... | collective-permute-start | bytes 18874376 | tf_op jit(solution)/shard_map/ppermute | solution.py:72
  264.1 12.6 %collective-permute-start.35 = (bf16[128,1536]{1,0:T(8,128)(2,1)}, bf16[128,1536]{1,0:T(8,128)(2,1)}, u32[]{:S(2)}, u32[]{:S(2)}) collective-permute-start(bf16[128,1536]{1,0:T(8,128)(2,1)} %add_convert_fusion.8), channel_id=1, source_target_pairs={{0,2},{1,3},{2,0},{3,1},{4,6},{5,7},{6,4},{7,5},{8,10},{9,11},{10,... | collective-permute-start | bytes 1179656 | tf_op jit(solution)/shard_map/ppermute | solution.py:72
  266.8 175.2 %all-gather.8.cloned.1.call-start = ((), (), s32[]{:S(2)}) async-start(), calls=%async_computation.6 | async-start | bytes 3538944 | tf_op jit(solution)/shard_map/all_gather | solution.py:133
  294.1 15.3 %collective-permute-start.38 = (bf16[128,1536]{1,0:T(8,128)(2,1)S(1)}, bf16[128,1536]{1,0:T(8,128)(2,1)S(1)}, u32[]{:S(2)}, u32[]{:S(2)}) collective-permute-start(bf16[128,1536]{1,0:T(8,128)(2,1)S(1)} %add_convert_fusion.6), channel_id=1, source_target_pairs={{0,2},{1,3},{2,0},{3,1},{4,6},{5,7},{6,4},{7,5},{8,10},{9,11},{10,... | collective-permute-start | bytes 1179656 | tf_op jit(solution)/shard_map/ppermute | solution.py:72
  311.3 152.9 %reduce-scatter.5.cloned.1.call-start = ((), (), s32[]{:S(2)}) async-start(), calls=%async_computation.8 | async-start | bytes 2211840 | tf_op jit(solution)/shard_map/reduce_scatter | solution.py:127
  321.4 12.3 %collective-permute-start.43 = (bf16[512,384]{1,0:T(8,128)(2,1)}, bf16[512,384]{1,0:T(8,128)(2,1)}, u32[]{:S(2)}, u32[]{:S(2)}) collective-permute-start(bf16[512,384]{1,0:T(8,128)(2,1)} %get-tuple-element.241), channel_id=1, source_target_pairs={{0,4},{4,0},{8,12},{12,8},{16,20},{20,16},{24,28},{28,24},{1,5},{5... | collective-permute-start | bytes 1179656 | tf_op jit(solution)/shard_map/ppermute | solution.py:72
  326.0 20.3 %collective-permute-start.41 = (bf16[512,384]{1,0:T(8,128)(2,1)}, bf16[512,384]{1,0:T(8,128)(2,1)}, u32[]{:S(2)}, u32[]{:S(2)}) collective-permute-start(bf16[512,384]{1,0:T(8,128)(2,1)} %get-tuple-element.238), channel_id=1, source_target_pairs={{0,4},{4,0},{8,12},{12,8},{16,20},{20,16},{24,28},{28,24},{1,5},{5... | collective-permute-start | bytes 1179656 | tf_op jit(solution)/shard_map/ppermute | solution.py:72
  329.5 81.3 %collective-permute-start.48 = (bf16[1024,1536]{1,0:T(8,128)(2,1)}, bf16[1024,1536]{1,0:T(8,128)(2,1)}, u32[]{:S(2)}, u32[]{:S(2)}) collective-permute-start(bf16[1024,1536]{1,0:T(8,128)(2,1)} %all-gather.6.cloned.1.call-done.rows), channel_id=1, source_target_pairs={{0,1},{1,0},{2,3},{3,2},{4,5},{5,4},{6,7},{7,6},{8,9},{9,8},{10,11... | collective-permute-start | bytes 9437192 | tf_op jit(solution)/shard_map/ppermute | solution.py:72
  329.5 70.0 %collective-permute-start.52 = (bf16[768,1152]{1,0:T(8,128)(2,1)}, bf16[768,1152]{1,0:T(8,128)(2,1)S(1)}, u32[]{:S(2)}, u32[]{:S(2)}) collective-permute-start(bf16[768,1152]{1,0:T(8,128)(2,1)} %copy-done.23), channel_id=1, source_target_pairs={{0,4},{4,0},{8,12},{12,8},{16,20},{20,16},{24,28},{28,24},{1,5},{5... | collective-permute-start | bytes 5308424 | tf_op jit(solution)/shard_map/ppermute | solution.py:72
  334.8 32.9 %collective-permute-start.44 = (bf16[256,384]{1,0:T(8,128)(2,1)S(1)}, bf16[256,384]{1,0:T(8,128)(2,1)S(1)}, u32[]{:S(2)}, u32[]{:S(2)}) collective-permute-start(bf16[256,384]{1,0:T(8,128)(2,1)S(1)} %get-tuple-element.391), channel_id=1, source_target_pairs={{16,0},{20,4},{24,8},{28,12},{17,1},{21,5},{25,9},{29,13},{18,2},{... | collective-permute-start | bytes 589832 | tf_op jit(solution)/shard_map/ppermute | solution.py:111
  336.1 31.6 %collective-permute-start.45 = (bf16[256,384]{1,0:T(8,128)(2,1)S(1)}, bf16[256,384]{1,0:T(8,128)(2,1)S(1)}, u32[]{:S(2)}, u32[]{:S(2)}) collective-permute-start(bf16[256,384]{1,0:T(8,128)(2,1)S(1)} %get-tuple-element.390), channel_id=1, source_target_pairs={{24,0},{28,4},{25,1},{29,5},{26,2},{30,6},{27,3},{31,7}} | collective-permute-start | bytes 589832 | tf_op jit(solution)/shard_map/ppermute | solution.py:111
  347.5 20.3 %collective-permute-start.42 = (bf16[256,384]{1,0:T(8,128)(2,1)S(1)}, bf16[256,384]{1,0:T(8,128)(2,1)S(1)}, u32[]{:S(2)}, u32[]{:S(2)}) collective-permute-start(bf16[256,384]{1,0:T(8,128)(2,1)S(1)} %get-tuple-element.392), channel_id=1, source_target_pairs={{8,0},{12,4},{16,8},{20,12},{24,16},{28,20},{9,1},{13,5},{17,9},{2... | collective-permute-start | bytes 589832 | tf_op jit(solution)/shard_map/ppermute | solution.py:111
  370.4 38.5 %collective-permute-start.46 = (bf16[128,1536]{1,0:T(8,128)(2,1)S(1)}, bf16[128,1536]{1,0:T(8,128)(2,1)}, u32[]{:S(2)}, u32[]{:S(2)}) collective-permute-start(bf16[128,1536]{1,0:T(8,128)(2,1)S(1)} %get-tuple-element.254), channel_id=1, source_target_pairs={{0,1},{1,0},{2,3},{3,2},{4,5},{5,4},{6,7},{7,6},{8,9},{9,8},{10,11... | collective-permute-start | bytes 1179656 | tf_op jit(solution)/shard_map/ppermute | solution.py:72
  402.9 73.5 %all-to-all-start.1 = ((bf16[8,192,384]{2,1,0:T(8,128)(2,1)}), bf16[8,192,384]{2,1,0:T(8,128)(2,1)}, u32[]{:S(2)}, u32[]{:S(2)}) async-start(bf16[8,192,384]{2,1,0:T(8,128)(2,1)} %bitcast.25), calls=%async_computation.2 | async-start | bytes 2359296 | tf_op jit(solution)/shard_map/all_to_all | solution.py:117
  408.9 98.0 %reduce-scatter.3.cloned.1.call-start = ((), (), s32[]{:S(2)}) async-start(), calls=%async_computation.7 | async-start | bytes 1474560 | tf_op jit(solution)/shard_map/reduce_scatter | solution.py:127
  410.1 29.2 %collective-permute-start.47 = (bf16[128,1536]{1,0:T(8,128)(2,1)S(1)}, bf16[128,1536]{1,0:T(8,128)(2,1)S(1)}, u32[]{:S(2)}, u32[]{:S(2)}) collective-permute-start(bf16[128,1536]{1,0:T(8,128)(2,1)S(1)} %add_convert_fusion.4), channel_id=1, source_target_pairs={{0,2},{1,3},{2,0},{3,1},{4,6},{5,7},{6,4},{7,5},{8,10},{9,11},{10,... | collective-permute-start | bytes 1179656 | tf_op jit(solution)/shard_map/ppermute | solution.py:72
  440.0 33.9 %collective-permute-start.51 = (bf16[768,768]{1,0:T(8,128)(2,1)}, bf16[768,768]{1,0:T(8,128)(2,1)}, u32[]{:S(2)}, u32[]{:S(2)}) collective-permute-start(bf16[768,768]{1,0:T(8,128)(2,1)} %get-tuple-element.292), channel_id=1, source_target_pairs={{0,4},{4,0},{8,12},{12,8},{16,20},{20,16},{24,28},{28,24},{1,5},{5... | collective-permute-start | bytes 3538952 | tf_op jit(solution)/shard_map/ppermute | solution.py:72
  442.0 47.2 %collective-permute-start.50 = (bf16[1024,1536]{1,0:T(8,128)(2,1)}, bf16[1024,1536]{1,0:T(8,128)(2,1)}, u32[]{:S(2)}, u32[]{:S(2)}) collective-permute-start(bf16[1024,1536]{1,0:T(8,128)(2,1)} %all-gather.8.cloned.1.call-done.incoming), channel_id=1, source_target_pairs={{0,1},{1,0},{2,3},{3,2},{4,5},{5,4},{6,7},{7,6},{8,9},{9,8},{10,11... | collective-permute-start | bytes 9437192 | tf_op jit(solution)/shard_map/ppermute | solution.py:72
  443.2 25.0 %collective-permute-start.49 = (bf16[128,1536]{1,0:T(8,128)(2,1)S(1)}, bf16[128,1536]{1,0:T(8,128)(2,1)}, u32[]{:S(2)}, u32[]{:S(2)}) collective-permute-start(bf16[128,1536]{1,0:T(8,128)(2,1)S(1)} %add_convert_fusion.3.whole), channel_id=1, source_target_pairs={{0,1},{1,0},{2,3},{3,2},{4,5},{5,4},{6,7},{7,6},{8,9},{9,8},{10,11... | collective-permute-start | bytes 1179656 | tf_op jit(solution)/shard_map/ppermute | solution.py:72
  502.3 11.2 %all-to-all-start = ((f32[8,4,192]{2,1,0:T(4,128)}), f32[8,4,192]{2,1,0:T(4,128)S(1)}, u32[]{:S(2)}, u32[]{:S(2)}) async-start(f32[8,4,192]{2,1,0:T(4,128)} %copy.86), calls=%async_computation | async-start | bytes 65536 | tf_op jit(solution)/shard_map/all_to_all | solution.py:1036
  (145 other events, 1748.0 us)
Sparse Core Ops, SparseCore 0:
  126.7 119.0 all-gather.3
  266.9 56.3 all-gather.5
  325.5 85.4 all-gather.7
  413.1 51.0 reduce-scatter.4
  476.6 28.2 reduce-scatter.2
